TPU v7x, 128 devices: a whole 4x4x4 slice. The times are simulated.
128 devices in a mesh: row: 8 (over y, x_hi), col: 16 (over x_lo, z, core).
Axes of the slice: x: 4 (x_hi: 2, x_lo: 2; x = x_hi * 2 + x_lo), y: 4, z: 4, core: 2. Of those that a mesh axis runs over, the one named last changes fastest.
Arguments:
- tokens: bfloat16 [512, 12288], P('col', 'row'), may hold values from -6 to 6
- weight: bfloat16 [12288, 49152], P('row', 'col'), may hold values from -0.0546875 to 0.0546875
- cotangent: bfloat16 [512, 49152], P('row', 'col'), may hold values from -6 to 6
Outputs:
- activated: bfloat16 [512, 49152], P('row', 'col')
- input_grad: bfloat16 [512, 12288], P('col', 'row')
- weight_grad: bfloat16 [12288, 49152], P('row', 'col')
All inputs are finite; a program needn't handle non-finite values.
Results may differ from a plain program's by a relative error of at most 0.025.
Values may be sent and summed in bfloat16 or wider, within the bound.
No kernel may reach another device: no remote copies, remote signals or barrier semaphores. Data moves between devices by JAX's collectives and lax.ppermute only.
A program may use at most 128 MiB of HBM per device.

v0:
```python
import jax
import jax.numpy as jnp
from jax import lax
from jax.sharding import PartitionSpec as P


def gelu_parts(pre):
    coeff = 0.7978845608
    inner = coeff * (pre + 0.044715 * pre * pre * pre)
    tval = jnp.tanh(inner)
    value = 0.5 * pre * (1.0 + tval)
    slope = 0.5 * (1.0 + tval) + 0.5 * pre * (1.0 - tval * tval) * coeff * (
        1.0 + 3.0 * 0.044715 * pre * pre
    )
    return (value, slope)


def local(tokens, weight, cotangent):
    full_tokens = lax.all_gather(tokens, "col", axis=0, tiled=True)
    part = full_tokens
    preact = lax.psum_scatter(
        jnp.dot(part, weight, preferred_element_type=jnp.float32).astype(jnp.bfloat16),
        "row",
        scatter_dimension=0,
        tiled=True,
    ).astype(jnp.float32)
    value, slope = gelu_parts(preact)
    local_grad = (cotangent.astype(jnp.float32) * slope).astype(jnp.bfloat16)
    grad_full = lax.all_gather(local_grad, "row", axis=0, tiled=True)
    activated = value.astype(jnp.bfloat16)
    part = grad_full
    input_grad = lax.psum_scatter(
        lax.dot_general(
            part, weight, (((1,), (1,)), ((), ())), preferred_element_type=jnp.float32
        ).astype(jnp.bfloat16),
        "col",
        scatter_dimension=0,
        tiled=True,
    )
    weight_grad = lax.dot_general(
        full_tokens, grad_full, (((0,), (0,)), ((), ())), preferred_element_type=jnp.float32
    ).astype(jnp.bfloat16)
    return (activated, input_grad, weight_grad)


def solution(mesh):
    return jax.shard_map(
        local,
        mesh=mesh,
        in_specs=(P("col", "row"), P("row", "col"), P("row", "col")),
        out_specs=(P("row", "col"), P("col", "row"), P("row", "col")),
        check_vma=False,
    )
```

profile of v0, /device:TPU:1, one launch (start us, length us, event | category | flops | bytes accessed | tf_op | source)
XLA Modules:
  0.0 272.8 jit_solution(3861103282754504877)
XLA Ops:
  7.2 0.0 all-gather.3.cloned.1.call-start
  7.2 0.7 all-gather.3.cloned.1.call-update
  7.9 0.0 reduce-scatter.3.cloned.1.call-start
  7.9 38.7 %all-gather.3.cloned.1.call-done = bf16[512,1536]{1,0:T(8,128)(2,1)} async-done(((bf16[32,1536]{1,0:T(8,128)(2,1)}), bf16[512,1536]{1,0:T(8,128)(2,1)}) %all-gather.3.cloned.1.call-update) | async-done | bytes 1572880 | tf_op jit(solution)/shard_map/all_gather | solution.py:19
  46.6 9.2 %convolution_convert_fusion.1 = bf16[512,3072]{1,0:T(8,128)(2,1)} fusion(bf16[512,1536]{1,0:T(8,128)(2,1)} %all-gather.3.cloned.1.call-done, bf16[1536,3072]{1,0:T(8,128)(2,1)} %param.4), kind=kOutput, calls=%fused_computation.2 | convolution fusion | flops 4833411072 | bytes 14155776 | tf_op jit(solution)/shard_map/dot_general | solution.py:22
  55.8 0.0 copy-start
  55.8 0.0 reduce-scatter.3.cloned.1.call-update
  55.9 0.0 all-gather.5.cloned.1.call-start
  55.9 77.6 %reduce-scatter.3.cloned.1.call-done = bf16[64,3072]{1,0:T(8,128)(2,1)} async-done(((bf16[512,3072]{1,0:T(8,128)(2,1)}), bf16[64,3072]{1,0:T(8,128)(2,1)}) %reduce-scatter.3.cloned.1.call-update) | async-done | bytes 393232 | tf_op jit(solution)/shard_map/reduce_scatter | solution.py:21
  133.5 0.0 copy-done
  133.5 2.5 fusion.8
  136.0 0.0 all-gather.5.cloned.1.call-update
  136.0 0.0 reduce-scatter.5.cloned.1.call-start
  136.1 62.6 %all-gather.5.cloned.1.call-done = bf16[512,3072]{1,0:T(8,128)(2,1)} async-done(((bf16[64,3072]{1,0:T(8,128)(2,1)}), bf16[512,3072]{1,0:T(8,128)(2,1)}) %all-gather.5.cloned.1.call-update) | async-done | bytes 3145744 | tf_op jit(solution)/shard_map/all_gather | solution.py:29
  198.7 0.0 copy-start.1
  198.7 10.5 %convolution_convert_fusion.2 = bf16[512,1536]{1,0:T(8,128)(2,1)} fusion(bf16[512,3072]{1,0:T(8,128)(2,1)} %all-gather.5.cloned.1.call-done, bf16[1536,3072]{1,0:T(8,128)(2,1)} %param.4), kind=kOutput, calls=%fused_computation.3 | convolution fusion | flops 4832624640 | bytes 14155776 | tf_op jit(solution)/shard_map/dot_general | solution.py:33
  209.2 0.0 reduce-scatter.5.cloned.1.call-update
  209.2 0.0 copy-done.1
  209.2 8.9 %fusion = bf16[1536,3072]{0,1:T(8,128)(2,1)} fusion(bf16[512,3072]{1,0:T(8,128)(2,1)S(1)} %copy-done.1, bf16[512,1536]{1,0:T(8,128)(2,1)} %all-gather.3.cloned.1.call-done), kind=kOutput, calls=%fused_computation.1 | convolution fusion | flops 4836556800 | bytes 14155776 | tf_op jit(solution)/shard_map/dot_general | solution.py:40
  218.2 12.6 %copy.6 = bf16[1536,3072]{1,0:T(8,128)(2,1)} copy(bf16[1536,3072]{0,1:T(8,128)(2,1)} %fusion) | data formatting | bytes 18874368
  230.8 35.5 %reduce-scatter.5.cloned.1.call-done = bf16[32,1536]{1,0:T(8,128)(2,1)} async-done(((bf16[512,1536]{1,0:T(8,128)(2,1)}), bf16[32,1536]{1,0:T(8,128)(2,1)}) %reduce-scatter.5.cloned.1.call-update) | async-done | bytes 98320 | tf_op jit(solution)/shard_map/reduce_scatter | solution.py:32
Async XLA Ops:
  7.2 39.5 %all-gather.3.cloned.1.call-start = ((), (), s32[]{:S(2)}) async-start(), calls=%async_computation.2 | async-start | bytes 1671168 | tf_op jit(solution)/shard_map/all_gather | solution.py:19
  7.9 125.6 %reduce-scatter.3.cloned.1.call-start = ((), (), s32[]{:S(2)}) async-start(), calls=%async_computation.3 | async-start | bytes 3538944 | tf_op jit(solution)/shard_map/reduce_scatter | solution.py:21
  55.8 77.7 %copy-start = (bf16[64,3072]{1,0:T(8,128)(2,1)S(1)}, bf16[64,3072]{1,0:T(8,128)(2,1)}, u32[]{:S(2)}) copy-start(bf16[64,3072]{1,0:T(8,128)(2,1)} %param.5) | copy-start | bytes 1179652
  55.9 142.8 %all-gather.5.cloned.1.call-start = ((), (), s32[]{:S(2)}) async-start(), calls=%async_computation.4 | async-start | bytes 3538944 | tf_op jit(solution)/shard_map/all_gather | solution.py:29
  136.0 130.3 %reduce-scatter.5.cloned.1.call-start = ((), (), s32[]{:S(2)}) async-start(), calls=%async_computation.5 | async-start | bytes 1671168 | tf_op jit(solution)/shard_map/reduce_scatter | solution.py:32
  198.7 10.5 %copy-start.1 = (bf16[512,3072]{1,0:T(8,128)(2,1)S(1)}, bf16[512,3072]{1,0:T(8,128)(2,1)}, u32[]{:S(2)}) copy-start(bf16[512,3072]{1,0:T(8,128)(2,1)} %all-gather.5.cloned.1.call-done) | copy-start | bytes 9437188
Sparse Core Ops, SparseCore 0:
  9.7 36.8 all-gather.2
  56.0 77.5 reduce-scatter.2
  136.4 62.2 all-gather.4
  209.3 56.9 reduce-scatter.4
where the time goes:
time: 276 us; the launch traced here: 273 us
  waiting for transfers between devices  215 us (78%)
  matrix products  28.6 us (10%)
  between operations  13.8 us (5%)
  local copies, waits for them, and re-layouts  12.6 us (5%)
    reduce_scatter x1, waiting for transfers between devices, local(): lax.psum_scatter(jnp.dot(part, weight, preferred_element_type=jnp.float32...  77.6 us
    all_gather x1, waiting for transfers between devices, local(): grad_full = lax.all_gather(local_grad, 'row', axis=0, tiled=True)  62.6 us
    all_gather x1, waiting for transfers between devices, local(): full_tokens = lax.all_gather(tokens, 'col', axis=0, tiled=True)  38.7 us
    reduce_scatter x1, waiting for transfers between devices, local(): lax.psum_scatter(lax.dot_general(part, weight, (((1,), (1,)), ((), ())),...  35.5 us
    unnamed x5, local copies, waits for them, and re-layouts  12.6 us
    dot_general x1, matrix products, local(): lax.dot_general(part, weight, (((1,), (1,)), ((), ())), preferred_element...  10.5 us
    dot_general x1, matrix products, local(): jnp.dot(part, weight, preferred_element_type=jnp.float32)  9.2 us
    dot_general x1, matrix products, local(): lax.dot_general(full_tokens, grad_full, (((0,), (0,)), ((), ())), preferr...  8.93 us
  transfers between devices with their start and end apart: 4, of which 4 were waited for; matrix products, arithmetic and copies ran while one was open for 8% of the time, Pallas kernels for 0%

commit v1 on v0

v1 whole, which is shorter than its diff:
```python
import jax
import jax.numpy as jnp
from jax import lax
from jax.sharding import Mesh
from jax.sharding import PartitionSpec as P

ROW = ("y", "xh")
PLANE = ("xl", "z")


def gelu_parts(pre):
    coeff = 0.7978845608
    inner = coeff * (pre + 0.044715 * pre * pre * pre)
    tval = jnp.tanh(inner)
    value = 0.5 * pre * (1.0 + tval)
    slope = 0.5 * (1.0 + tval) + 0.5 * pre * (1.0 - tval * tval) * coeff * (
        1.0 + 3.0 * 0.044715 * pre * pre
    )
    return (value, slope)


def local(tokens, weight, cotangent):
    rows, width = tokens.shape
    half = width // 2
    mine = lax.all_to_all(tokens, "c", 1, 0, tiled=True)
    spread = jnp.broadcast_to(mine[None], (8, 2 * rows, half)).reshape(16 * rows, half)
    part = lax.all_to_all(spread, PLANE, 0, 0, tiled=True)
    full_tokens = lax.all_gather(part, "c", axis=1, tiled=True)

    partial = jnp.dot(full_tokens, weight, preferred_element_type=jnp.float32).astype(jnp.bfloat16)
    got = lax.all_to_all(partial, ROW, 0, 0, tiled=True)
    block, hidden = cotangent.shape
    preact = jnp.sum(got.reshape(8, block, hidden).astype(jnp.float32), axis=0)
    value, slope = gelu_parts(preact)
    local_grad = (cotangent.astype(jnp.float32) * slope).astype(jnp.bfloat16)
    activated = value.astype(jnp.bfloat16)
    spread = jnp.broadcast_to(local_grad[None], (8, block, hidden)).reshape(8 * block, hidden)
    grad_full = lax.all_to_all(spread, ROW, 0, 0, tiled=True)

    part = lax.dot_general(
        grad_full, weight, (((1,), (1,)), ((), ())), preferred_element_type=jnp.float32
    ).astype(jnp.bfloat16)
    pair = lax.all_to_all(part.reshape(16 * rows, 2, half), "c", 1, 1, tiled=True)
    pair = jnp.sum(pair.astype(jnp.float32), axis=1).astype(jnp.bfloat16)
    got = lax.all_to_all(pair, PLANE, 0, 0, tiled=True)
    total = jnp.sum(got.reshape(8, 2 * rows, half).astype(jnp.float32), axis=0).astype(jnp.bfloat16)
    input_grad = lax.all_to_all(total, "c", 0, 1, tiled=True)

    weight_grad = jnp.dot(full_tokens.T, grad_full, preferred_element_type=jnp.float32).astype(
        jnp.bfloat16
    )
    return (activated, input_grad, weight_grad)


def solution(mesh):
    fine = Mesh(mesh.devices.reshape(4, 2, 2, 4, 2), ("y", "xh", "xl", "z", "c"))
    row, col = P(ROW), ("xl", "z", "c")
    return jax.shard_map(
        local,
        mesh=fine,
        in_specs=(P(col, ROW), P(ROW, col), P(ROW, col)),
        out_specs=(P(ROW, col), P(col, ROW), P(ROW, col)),
        check_vma=False,
    )
```

time: 276 us -> 194 us (0.70)
  waiting for transfers between devices: 215 us -> 13.6 us
  blocking collectives: 0 us -> 120 us
  matrix products: 28.6 us -> 22.7 us
  starting transfers between devices: 0.16 us -> 4.19 us
    all_to_all x0 -> x6, blocking collectives: none -> 120 us  [the longest x1 45.6 us: local(): got = lax.all_to_all(partial, ROW, 0, 0, tiled=True)]
    reduce_scatter x2 -> x0, waiting for transfers between devices: 113 us -> none  [the longest x1 77.6 us: local(): lax.psum_scatter(jnp.dot(part, weight, preferred_element_type=jnp.float32...]
    all_gather x2 -> x1, waiting for transfers between devices: 101 us -> 13.5 us  [local(): full_tokens = lax.all_gather(part, 'c', axis=1, tiled=True)]
    dot_general x3, matrix products: 28.6 us -> 22.7 us  [the longest x1 9.49 us: local(): jnp.dot(full_tokens.T, grad_full, preferred_element_type=jnp.float32)]
    all_to_all x0 -> x1, starting transfers between devices: none -> 4.15 us  [local(): got = lax.all_to_all(pair, PLANE, 0, 0, tiled=True)]
    unnamed x5 -> x13, local copies, waits for them, and re-layouts: 12.6 us -> 13.1 us
  transfers between devices with their start and end apart: 4 -> 2, of which waited for: 4 -> 1; matrix products, arithmetic and copies ran while one was open for 8% -> 11% of each run, Pallas kernels for 0% -> 0%
where the time goes in v1:
time: 194 us; the launch traced here: 193 us
  blocking collectives  120 us (62%)
  matrix products  22.7 us (12%)
  local copies, waits for them, and re-layouts  15.2 us (8%)
  between operations  14.1 us (7%)
  waiting for transfers between devices  13.6 us (7%)
  starting transfers between devices  4.19 us (2%)
  other arithmetic  3.3 us (2%)
    all_to_all x1, blocking collectives, local(): got = lax.all_to_all(partial, ROW, 0, 0, tiled=True)  45.6 us
    all_to_all x1, blocking collectives, local(): grad_full = lax.all_to_all(spread, ROW, 0, 0, tiled=True)  41 us
    all_to_all x1, blocking collectives, local(): part = lax.all_to_all(spread, PLANE, 0, 0, tiled=True)  17.6 us
    all_gather x1, waiting for transfers between devices, local(): full_tokens = lax.all_gather(part, 'c', axis=1, tiled=True)  13.5 us
    unnamed x13, local copies, waits for them, and re-layouts  13.1 us
    dot_general x1, matrix products, local(): jnp.dot(full_tokens.T, grad_full, preferred_element_type=jnp.float32)  9.49 us
    dot_general x1, matrix products, local(): jnp.dot(full_tokens, weight, preferred_element_type=jnp.float32)  8.07 us
    all_to_all x1, blocking collectives, local(): lax.all_to_all(part.reshape(16 * rows, 2, half), 'c', 1, 1, tiled=True)  7.19 us
  transfers between devices with their start and end apart: 2, of which 1 were waited for; matrix products, arithmetic and copies ran while one was open for 11% of the time, Pallas kernels for 0%

profile of v1, /device:TPU:1, one launch (start us, length us, event | category | flops | bytes accessed | tf_op | source)
XLA Modules:
  0.0 193.3 jit_solution(2894751780303506655)
XLA Ops:
  7.2 0.0 all-gather.2.cloned.1.call-start
  7.2 0.9 copy.25
  8.1 4.9 %all_to_all.76 = bf16[32,2,768]{2,0,1:T(8,128)(2,1)S(1)} all-to-all(bf16[32,2,768]{2,0,1:T(8,128)(2,1)S(1)} %bitcast.36), channel_id=1, replica_groups=mesh['y'=4,'xh'=2,'xl'=2,'z'=4,'c'=2] {'c'}, dimensions={1} | all-to-all | bytes 196608 | tf_op jit(solution)/shard_map/all_to_all | solution.py:25
  13.0 0.1 broadcast_in_dim.7
  13.0 17.6 %all_to_all.77 = bf16[8,64,768]{2,1,0:T(8,128)(2,1)} all-to-all(bf16[8,64,768]{2,1,0:T(8,128)(2,1)S(1)} %broadcast_in_dim.7), channel_id=1, replica_groups=mesh['y'=4,'xh'=2,'xl'=2,'z'=4,'c'=2] {'xl','z'}, dimensions={0} | all-to-all | bytes 1572864 | tf_op jit(solution)/shard_map/all_to_all | solution.py:27
  30.6 0.0 all-gather.2.cloned.1.call-update
  30.6 13.5 %all-gather.2.cloned.1.call-done = bf16[512,1536]{1,0:T(8,128)(2,1)} async-done(((bf16[512,768]{1,0:T(8,128)(2,1)}), bf16[512,1536]{1,0:T(8,128)(2,1)}) %all-gather.2.cloned.1.call-update) | async-done | bytes 1572880 | tf_op jit(solution)/shard_map/all_gather | solution.py:28
  44.2 8.1 %convolution_convert_fusion.1 = bf16[512,3072]{1,0:T(8,128)(2,1)S(1)} fusion(bf16[512,1536]{1,0:T(8,128)(2,1)} %all-gather.2.cloned.1.call-done, bf16[1536,3072]{1,0:T(8,128)(2,1)} %param.4), kind=kOutput, calls=%fused_computation.3 | convolution fusion | flops 4833411072 | bytes 14155776 | tf_op jit(solution)/shard_map/dot_general | solution.py:30
  52.3 45.6 %all_to_all.78 = bf16[8,64,3072]{2,1,0:T(8,128)(2,1)S(1)} all-to-all(bf16[8,64,3072]{2,1,0:T(8,128)(2,1)S(1)} %bitcast.30), channel_id=1, replica_groups=mesh['y'=4,'xh'=2,'xl'=2,'z'=4,'c'=2] {'y','xh'}, dimensions={0} | all-to-all | bytes 6291456 | tf_op jit(solution)/shard_map/all_to_all | solution.py:31
  97.8 0.5 convert_reduce_fusion
  98.4 0.5 copy-done.1
  98.8 1.3 fusion.7
  100.1 0.4 broadcast_in_dim.16
  100.5 41.0 %all_to_all.79 = bf16[8,64,3072]{2,1,0:T(8,128)(2,1)S(1)} all-to-all(bf16[8,64,3072]{2,1,0:T(8,128)(2,1)S(1)} %broadcast_in_dim.16), channel_id=1, replica_groups=mesh['y'=4,'xh'=2,'xl'=2,'z'=4,'c'=2] {'y','xh'}, dimensions={0} | all-to-all | bytes 6291456 | tf_op jit(solution)/shard_map/all_to_all | solution.py:38
  141.5 5.1 %convolution_convert_fusion.2 = bf16[512,1536]{1,0:T(8,128)(2,1)S(1)} fusion(bf16[512,3072]{1,0:T(8,128)(2,1)S(1)} %bitcast.28, bf16[1536,3072]{1,0:T(8,128)(2,1)S(1)} %bitcast.40), kind=kOutput, calls=%fused_computation.4 | convolution fusion | flops 4832624640 | bytes 14155776 | tf_op jit(solution)/shard_map/dot_general | solution.py:40
  146.7 0.1 copy.24
  146.8 7.2 %all_to_all.80 = bf16[512,2,768]{2,0,1:T(8,128)(2,1)S(1)} all-to-all(bf16[512,2,768]{2,0,1:T(8,128)(2,1)S(1)} %bitcast.27), channel_id=1, replica_groups=mesh['y'=4,'xh'=2,'xl'=2,'z'=4,'c'=2] {'c'}, dimensions={1} | all-to-all | bytes 3145728 | tf_op jit(solution)/shard_map/all_to_all | solution.py:43
  154.0 1.4 reduce_sum.34
  155.3 4.2 %all-to-all-start.5 = ((bf16[8,64,768]{2,1,0:T(8,128)(2,1)}), bf16[8,64,768]{2,1,0:T(8,128)(2,1)S(1)}, u32[]{:S(2)}, u32[]{:S(2)}) async-start(bf16[8,64,768]{2,1,0:T(8,128)(2,1)} %bitcast.5), calls=%async_computation.5 | async-start | bytes 1572864 | tf_op jit(solution)/shard_map/all_to_all | solution.py:45
  159.5 9.5 %fusion = bf16[1536,3072]{0,1:T(8,128)(2,1)} fusion(bf16[512,3072]{1,0:T(8,128)(2,1)} %bitcast.29, bf16[512,1536]{1,0:T(8,128)(2,1)S(1)} %copy-done.2), kind=kOutput, calls=%fused_computation.1 | convolution fusion | flops 4836556800 | bytes 14155776 | tf_op jit(solution)/shard_map/dot_general | solution.py:49
  169.0 12.6 %copy.18 = bf16[1536,3072]{1,0:T(8,128)(2,1)} copy(bf16[1536,3072]{0,1:T(8,128)(2,1)} %fusion) | data formatting | bytes 18874368
  181.6 0.1 reduce_sum.35
  181.7 4.1 %all_to_all.81 = bf16[2,32,768]{2,1,0:T(8,128)(2,1)S(1)} all-to-all(bf16[2,32,768]{2,1,0:T(8,128)(2,1)S(1)} %bitcast.33), channel_id=1, replica_groups=mesh['y'=4,'xh'=2,'xl'=2,'z'=4,'c'=2] {'c'}, dimensions={0} | all-to-all | bytes 196608 | tf_op jit(solution)/shard_map/all_to_all | solution.py:47
  185.8 0.6 copy.21
  (13 shorter events, 0.0 us)
Async XLA Ops:
  7.2 37.0 %all-gather.2.cloned.1.call-start = ((), (), s32[]{:S(2)}) async-start(), calls=%async_computation.7 | async-start | bytes 2359296 | tf_op jit(solution)/shard_map/all_gather | solution.py:28
  52.2 89.3 %slice-start = ((s8[9437184]{0:T(1024)(128)(4,1)}), s8[4194304]{0:T(1024)(128)(4,1)S(1)}, s32[]{:S(2)}) async-start(s8[9437184]{0:T(1024)(128)(4,1)} %bitcast.39), calls=%async_computation.8 | async-start | bytes 8388608
  97.8 1.0 copy-start.1
  97.8 43.7 %slice-start.1 = ((s8[9437184]{0:T(1024)(128)(4,1)}), s8[4194304]{0:T(1024)(128)(4,1)S(1)}, s32[]{:S(2)}) async-start(s8[9437184]{0:T(1024)(128)(4,1)} %bitcast.39), calls=%async_computation.9 | async-start | bytes 8388608
  100.1 41.4 %slice-start.2 = ((s8[9437184]{0:T(1024)(128)(4,1)}), s8[1048576]{0:T(1024)(128)(4,1)S(1)}, s32[]{:S(2)}) async-start(s8[9437184]{0:T(1024)(128)(4,1)} %bitcast.39), calls=%async_computation.10 | async-start | bytes 2097152
  141.5 5.1 %copy-start = (bf16[8,64,3072]{2,1,0:T(8,128)(2,1)}, bf16[8,64,3072]{2,1,0:T(8,128)(2,1)S(1)}, u32[]{:S(2)}) copy-start(bf16[8,64,3072]{2,1,0:T(8,128)(2,1)S(1)} %all_to_all.79) | copy-start | bytes 9437188
  146.8 12.7 %copy-start.2 = (bf16[512,1536]{1,0:T(8,128)(2,1)S(1)}, bf16[512,1536]{1,0:T(8,128)(2,1)}, u32[]{:S(2)}) copy-start(bf16[512,1536]{1,0:T(8,128)(2,1)} %all-gather.2.cloned.1.call-done) | copy-start | bytes 4718596
  155.3 26.2 %all-to-all-start.5 = ((bf16[8,64,768]{2,1,0:T(8,128)(2,1)}), bf16[8,64,768]{2,1,0:T(8,128)(2,1)S(1)}, u32[]{:S(2)}, u32[]{:S(2)}) async-start(bf16[8,64,768]{2,1,0:T(8,128)(2,1)} %bitcast.5), calls=%async_computation.5 | async-start | bytes 1572864 | tf_op jit(solution)/shard_map/all_to_all | solution.py:45
Sparse Core Ops, SparseCore 0:
  30.7 13.3 all-gather.1

commit v2 on v1

v2 whole, which is shorter than its diff:
```python
import functools

import jax
import jax.numpy as jnp
from jax import lax
from jax.experimental import pallas as pl
from jax.experimental.pallas import tpu as pltpu
from jax.sharding import Mesh
from jax.sharding import PartitionSpec as P

N_Y = 4
ROW = ("y", "xh")
PLANE = ("xl", "z")
SWAP = ((0, 1), (1, 0))
LIMIT = 40 * 2**20
F32, BF16 = jnp.float32, jnp.bfloat16
VMEM = pltpu.VMEM


def gelu_parts(pre):
    coeff = 0.7978845608
    inner = coeff * (pre + 0.044715 * pre * pre * pre)
    tval = jnp.tanh(inner)
    value = 0.5 * pre * (1.0 + tval)
    slope = 0.5 * (1.0 + tval) + 0.5 * pre * (1.0 - tval * tval) * coeff * (
        1.0 + 3.0 * 0.044715 * pre * pre
    )
    return (value, slope)


def ahead(array, distance):
    return lax.ppermute(array, "y", [(i, (i + distance) % N_Y) for i in range(N_Y)])


def across(array):
    return lax.ppermute(array, "xh", SWAP)


def block_of(place, distance, side):
    return lax.rem(place[0] + distance, N_Y) * 2 + lax.rem(place[1] + side, 2)


def forward_kernel(pieces, place, tokens, weight, *outs):
    held = outs[-1]
    outs = outs[:-1]
    rows = tokens.shape[1]

    @pl.when(pl.program_id(0) == 0)
    def _():
        for distance in range(N_Y):
            for side in range(2):
                start = (2 * distance + side) * rows
                held[start : start + rows, :] = tokens[block_of(place, distance, side)]

    part = jnp.dot(held[...], weight[...], preferred_element_type=F32).astype(BF16)
    for out, piece in zip(outs, pieces):
        for slot, (distance, side) in enumerate(piece):
            start = (2 * distance + side) * rows
            out[slot * rows : (slot + 1) * rows, :] = part[start : start + rows, :]


def forward(place, tokens, weight, pieces, name):
    blocks, rows, width = tokens.shape
    hidden = weight.shape[1]
    step = 512
    outs = [jax.ShapeDtypeStruct((len(piece) * rows, hidden), BF16) for piece in pieces]
    specs = [pl.BlockSpec((len(piece) * rows, step), lambda i, _: (0, i)) for piece in pieces]
    return pl.pallas_call(
        functools.partial(forward_kernel, pieces),
        out_shape=outs + [jax.ShapeDtypeStruct((blocks * rows, width), BF16)],
        grid_spec=pltpu.PrefetchScalarGridSpec(
            num_scalar_prefetch=1,
            grid=(hidden // step,),
            in_specs=[
                pl.BlockSpec((blocks, rows, width), lambda i, _: (0, 0, 0)),
                pl.BlockSpec((width, step), lambda i, _: (0, i)),
            ],
            out_specs=specs + [pl.BlockSpec((blocks * rows, width), lambda i, _: (0, 0))],
        ),
        compiler_params=pltpu.CompilerParams(vmem_limit_bytes=LIMIT),
        cost_estimate=pl.CostEstimate(
            flops=2 * blocks * rows * width * hidden,
            bytes_accessed=2 * (width * hidden + blocks * rows * (2 * width + hidden)),
            transcendentals=0,
        ),
        name=name,
    )(place, tokens, weight)


def backward_kernel(pieces, place, *refs):
    grads = refs[: len(pieces)]
    weight, out, held = refs[len(pieces) :]
    rows = out.shape[1]

    @pl.when(pl.program_id(0) == 0)
    def _():
        for grad, piece in zip(grads, pieces):
            for slot, (distance, side) in enumerate(piece):
                start = (2 * distance + side) * rows
                held[start : start + rows, :] = grad[slot * rows : (slot + 1) * rows, :]

    part = lax.dot_general(
        held[...], weight[...], (((1,), (1,)), ((), ())), preferred_element_type=F32
    ).astype(BF16)
    for distance in range(N_Y):
        for side in range(2):
            start = (2 * distance + side) * rows
            out[block_of(place, distance, side)] = part[start : start + rows, :]


def backward(place, grads, weight, pieces, name):
    width, hidden = weight.shape
    rows = grads[0].shape[0] // len(pieces[0])
    blocks = 2 * N_Y
    step = 256
    whole = lambda a: pl.BlockSpec(a.shape, lambda i, _: (0, 0))
    return pl.pallas_call(
        functools.partial(backward_kernel, pieces),
        out_shape=[
            jax.ShapeDtypeStruct((blocks, rows, width), BF16),
            jax.ShapeDtypeStruct((blocks * rows, hidden), BF16),
        ],
        grid_spec=pltpu.PrefetchScalarGridSpec(
            num_scalar_prefetch=1,
            grid=(width // step,),
            in_specs=[whole(a) for a in grads]
            + [pl.BlockSpec((step, hidden), lambda i, _: (i, 0))],
            out_specs=[
                pl.BlockSpec((blocks, rows, step), lambda i, _: (0, 0, i)),
                pl.BlockSpec((blocks * rows, hidden), lambda i, _: (0, 0)),
            ],
        ),
        compiler_params=pltpu.CompilerParams(vmem_limit_bytes=LIMIT),
        cost_estimate=pl.CostEstimate(
            flops=2 * blocks * rows * width * hidden,
            bytes_accessed=2 * (width * hidden + blocks * rows * (width + 2 * hidden)),
            transcendentals=0,
        ),
        name=name,
    )(place, *grads, weight)


def weight_grad_kernel(tok_a, tok_b, grad_a, grad_b, out):
    dims = (((0,), (0,)), ((), ()))
    total = lax.dot_general(tok_a[...], grad_a[...], dims, preferred_element_type=F32)
    total += lax.dot_general(tok_b[...], grad_b[...], dims, preferred_element_type=F32)
    out[...] = total.astype(out.dtype)


def weight_grad_of(tok_a, tok_b, grad_a, grad_b):
    rows, width = tok_a.shape
    hidden = grad_a.shape[1]
    step = 512
    whole = pl.BlockSpec((rows, width), lambda i: (0, 0))
    part = pl.BlockSpec((rows, step), lambda i: (0, i))
    return pl.pallas_call(
        weight_grad_kernel,
        grid=(hidden // step,),
        in_specs=[whole, whole, part, part],
        out_specs=pl.BlockSpec((width, step), lambda i: (0, i)),
        out_shape=jax.ShapeDtypeStruct((width, hidden), BF16),
        compiler_params=pltpu.CompilerParams(vmem_limit_bytes=LIMIT),
        cost_estimate=pl.CostEstimate(
            flops=4 * rows * width * hidden,
            bytes_accessed=2 * (width * hidden + 2 * rows * (width + hidden)),
            transcendentals=0,
        ),
        name="weight_grad",
    )(tok_a, tok_b, grad_a, grad_b)


def middle(preact, cot):
    value, slope = gelu_parts(preact)
    return value.astype(BF16), (cot.astype(F32) * slope).astype(BF16)


def local(tokens, weight, cotangent):
    rows, width = tokens.shape
    block, hidden = cotangent.shape
    core = lax.axis_index("c")
    place = jnp.stack([lax.axis_index("y"), lax.axis_index("xh")]).astype(jnp.int32)
    cots = cotangent.reshape(2, rows, hidden)
    cot_own = lax.dynamic_index_in_dim(cots, core, 0, False)
    cot_other = lax.dynamic_index_in_dim(cots, 1 - core, 0, False)
    by_distance = [[(d, 0), (d, 1)] for d in range(N_Y)]
    by_side = [[(d, s) for d in range(N_Y)] for s in range(2)]

    spread = jnp.broadcast_to(tokens[None], (8, rows, width))
    own = lax.all_to_all(spread, PLANE, 0, 0, tiled=True)
    other = lax.ppermute(own, "c", SWAP)

    *parts, tok_own = forward(place, own, weight, by_distance, "forward_own")
    got = [ahead(parts[d], d) for d in (1, 2, 3)]
    *sides, tok_other = forward(place, other, weight, by_side, "forward_other")
    got_side = across(sides[1])

    total = sum((a.astype(F32) for a in got), parts[0].astype(F32))
    got_own = across(total[rows:].astype(BF16))

    pair = (sides[0].astype(F32) + got_side.astype(F32)).reshape(N_Y, rows, hidden)
    got = [ahead(pair[d].astype(BF16), d) for d in (1, 2, 3)]

    act_own, grad_own = middle(total[:rows] + got_own.astype(F32), cot_own)
    near = jnp.concatenate([grad_own] + [ahead(grad_own, -d) for d in (1, 2, 3)], axis=0)
    far = across(near)

    act_other, grad_other = middle(sum((a.astype(F32) for a in got), pair[0]), cot_other)
    both = jnp.concatenate([grad_other, across(grad_other)], axis=0)
    wide = [both] + [ahead(both, -d) for d in (1, 2, 3)]

    back_other, full_other = backward(place, wide, weight, by_distance, "backward_other")
    arrived = lax.ppermute(back_other, "c", SWAP)
    back_own, full_own = backward(place, [near, far], weight, by_side, "backward_own")
    chip = (back_own.astype(F32) + arrived.astype(F32)).astype(BF16)
    got = lax.all_to_all(chip, PLANE, 0, 0, tiled=True)
    input_grad = jnp.sum(got.astype(F32), axis=0).astype(BF16)
    weight_grad = weight_grad_of(tok_own, tok_other, full_own, full_other)
    first = core == 0
    activated = jnp.concatenate(
        [jnp.where(first, act_own, act_other), jnp.where(first, act_other, act_own)], axis=0
    )
    return (activated, input_grad, weight_grad)


def solution(mesh):
    fine = Mesh(mesh.devices.reshape(N_Y, 2, 2, 4, 2), ("y", "xh", "xl", "z", "c"))
    col = ("xl", "z", "c")
    return jax.shard_map(
        local,
        mesh=fine,
        in_specs=(P(col, ROW), P(ROW, col), P(ROW, col)),
        out_specs=(P(ROW, col), P(col, ROW), P(ROW, col)),
        check_vma=False,
    )
```

time: 194 us -> 141 us (0.73)
  blocking collectives: 120 us -> 18.1 us
  starting transfers between devices: 4.19 us -> 33.7 us
  Pallas kernels: 0 us -> 26.4 us
  waiting for transfers between devices: 13.6 us -> 39.6 us
  matrix products: 22.7 us -> 0 us
  between operations: 14.1 us -> 0.78 us
  other arithmetic: 3.3 us -> 8.69 us
    all_to_all x6 -> x1, blocking collectives: 120 us -> 18.1 us  [local(): own = lax.all_to_all(spread, PLANE, 0, 0, tiled=True)]
    ppermute x0 -> x18, waiting for transfers between devices: none -> 38.1 us  [the longest x12 32.4 us: ahead(): lax.ppermute(array, 'y', [(i, (i + distance) % N_Y) for i in range(N_Y)])]
    ppermute x0 -> x18, starting transfers between devices: none -> 29.4 us  [the longest x12 14 us: ahead(): lax.ppermute(array, 'y', [(i, (i + distance) % N_Y) for i in range(N_Y)])]
    pallas_call x0 -> x5, Pallas kernels: none -> 26.4 us  [the longest x2 9.85 us: forward(): pl.pallas_call(functools.partial(forward_kernel, pieces), out_shape=outs...]
    dot_general x3 -> x0, matrix products: 22.7 us -> none  [the longest x1 9.49 us: local(): jnp.dot(full_tokens.T, grad_full, preferred_element_type=jnp.float32)]
    all_gather x1 -> x0, waiting for transfers between devices: 13.5 us -> none  [local(): full_tokens = lax.all_gather(part, 'c', axis=1, tiled=True)]
    unnamed x13 -> x20, local copies, waits for them, and re-layouts: 13.1 us -> 11.7 us
  transfers between devices with their start and end apart: 2 -> 19, of which waited for: 1 -> 10; matrix products, arithmetic and copies ran while one was open for 11% -> 3% of each run, Pallas kernels for 0% -> 19%
where the time goes in v2:
time: 141 us
  waiting for transfers between devices  39.6 us (28%)
  starting transfers between devices  33.7 us (24%)
  Pallas kernels  26.4 us (19%)
  blocking collectives  18.1 us (13%)
  local copies, waits for them, and re-layouts  13.4 us (10%)
  other arithmetic  8.69 us (6%)
    ppermute x12, waiting for transfers between devices, ahead(): lax.ppermute(array, 'y', [(i, (i + distance) % N_Y) for i in range(N_Y)])  32.4 us
    all_to_all x1, blocking collectives, local(): own = lax.all_to_all(spread, PLANE, 0, 0, tiled=True)  18.1 us
    ppermute x12, starting transfers between devices, ahead(): lax.ppermute(array, 'y', [(i, (i + distance) % N_Y) for i in range(N_Y)])  14 us
    unnamed x20, local copies, waits for them, and re-layouts  11.7 us
    pallas_call x2, Pallas kernels, forward(): pl.pallas_call(functools.partial(forward_kernel, pieces), out_shape=outs...  9.85 us
    ppermute x4, starting transfers between devices, across(): return lax.ppermute(array, 'xh', SWAP)  9.18 us
    pallas_call x2, Pallas kernels, backward(): pl.pallas_call(functools.partial(backward_kernel, pieces), out_shape=[jax...  8.87 us
    pallas_call x1, Pallas kernels, weight_grad_of(): pl.pallas_call(weight_grad_kernel, grid=(hidden // step,), in_specs=[whol...  7.65 us
  transfers between devices with their start and end apart: 19, of which 10 were waited for; matrix products, arithmetic and copies ran while one was open for 3% of the time, Pallas kernels for 19%

profile of v2, /device:TPU:1, one launch (start us, length us, event | category | flops | bytes accessed | tf_op | source)
XLA Modules:
  0.0 140.6 jit_solution(9811190078951561704)
XLA Ops:
  1.6 18.1 %all_to_all.10.tokens = bf16[8,32,1536]{2,1,0:T(8,128)(2,1)S(1)} all-to-all(bf16[8,32,1536]{2,1,0:T(8,128)(2,1)S(1)} %broadcast_in_dim.2), channel_id=1, replica_groups=mesh['y'=4,'xh'=2,'xl'=2,'z'=4,'c'=2] {'xl','z'}, dimensions={0} | all-to-all | bytes 1572864 | tf_op jit(solution)/shard_map/all_to_all | solution.py:189
  19.7 2.4 %collective-permute-start.4 = (bf16[8,32,1536]{2,1,0:T(8,128)(2,1)S(1)}, bf16[8,32,1536]{2,1,0:T(8,128)(2,1)S(1)}, u32[]{:S(2)}, u32[]{:S(2)}) collective-permute-start(bf16[8,32,1536]{2,1,0:T(8,128)(2,1)S(1)} %all_to_all.10.tokens), channel_id=1, source_target_pairs={{0,1},{1,0},{2,3},{3,2},{4,5},{5,4},{6,7},{7,6},{8,9},{9,8},{10,11... | collective-permute-start | bytes 2359304 | tf_op jit(solution)/shard_map/ppermute | solution.py:190
  22.1 3.7 %copy-done = bf16[1536,3072]{1,0:T(8,128)(2,1)S(1)} copy-done((bf16[1536,3072]{1,0:T(8,128)(2,1)S(1)}, bf16[1536,3072]{1,0:T(8,128)(2,1)}, u32[]{:S(2)}) %copy-start) | copy-done | bytes 9437208
  25.8 5.0 %forward_own.1 = (bf16[64,3072]{1,0:T(8,128)(2,1)S(1)}, bf16[64,3072]{1,0:T(8,128)(2,1)S(1)}, bf16[64,3072]{1,0:T(8,128)(2,1)S(1)}, bf16[64,3072]{1,0:T(8,128)(2,1)S(1)}, bf16[256,1536]{1,0:T(8,128)(2,1)S(1)}) custom-call(s32[2]{0:T(128)S(1)} %pad_add_fusion.place, bf16[8,32,1536]{2,1,0:T(8,128)(2,1)S(1)} %all_to_all.10.tokens, bf16[1536,3072]{1,0:T(8,128)(2,1)S(1)} %copy-done), custom_call_target="tpu_custom_call" | custom-call | flops 2415919104 | bytes 12582912 | tf_op jit(solution)/shard_map/forward_own/pallas_call | solution.py:68
  33.0 2.6 %collective-permute-start.1 = (bf16[64,3072]{1,0:T(8,128)(2,1)S(1)}, bf16[64,3072]{1,0:T(8,128)(2,1)S(1)}, u32[]{:S(2)}, u32[]{:S(2)}) collective-permute-start(bf16[64,3072]{1,0:T(8,128)(2,1)S(1)} %get-tuple-element.17), channel_id=1, source_target_pairs={{0,64},{32,96},{64,0},{96,32},{1,65},{33,97},{65,1},{97,33},{2,66}... | collective-permute-start | bytes 1179656 | tf_op jit(solution)/shard_map/ppermute | solution.py:32
  36.7 4.9 %forward_other.1 = (bf16[128,3072]{1,0:T(8,128)(2,1)S(1)}, bf16[128,3072]{1,0:T(8,128)(2,1)S(1)}, bf16[256,1536]{1,0:T(8,128)(2,1)S(1)}) custom-call(s32[2]{0:T(128)S(1)} %pad_add_fusion.place, bf16[8,32,1536]{2,1,0:T(8,128)(2,1)S(1)} %collective-permute-done.4.tokens, bf16[1536,3072]{1,0:T(8,128)(2,1)S(1)} %copy-done.1), custom_call_target="tpu_custom_call" | custom-call | flops 2415919104 | bytes 12582912 | tf_op jit(solution)/shard_map/forward_other/pallas_call | solution.py:68
  41.6 2.5 %collective-permute-start.5 = (bf16[128,3072]{1,0:T(8,128)(2,1)S(1)}, bf16[128,3072]{1,0:T(8,128)(2,1)S(1)}, u32[]{:S(2)}, u32[]{:S(2)}) collective-permute-start(bf16[128,3072]{1,0:T(8,128)(2,1)S(1)} %get-tuple-element.20), channel_id=1, source_target_pairs={{0,16},{16,0},{1,17},{17,1},{2,18},{18,2},{3,19},{19,3},{4,20},{20... | collective-permute-start | bytes 2359304 | tf_op jit(solution)/shard_map/ppermute | solution.py:36
  44.1 9.2 %collective-permute-done.1 = bf16[64,3072]{1,0:T(8,128)(2,1)S(1)} collective-permute-done((bf16[64,3072]{1,0:T(8,128)(2,1)S(1)}, bf16[64,3072]{1,0:T(8,128)(2,1)S(1)}, u32[]{:S(2)}, u32[]{:S(2)}) %collective-permute-start.1) | collective-permute-done | bytes 393248 | tf_op jit(solution)/shard_map/ppermute | solution.py:32
  54.2 2.5 %collective-permute-start.3 = (bf16[32,3072]{1,0:T(8,128)(2,1)}, bf16[32,3072]{1,0:T(8,128)(2,1)S(1)}, u32[]{:S(2)}, u32[]{:S(2)}) collective-permute-start(bf16[32,3072]{1,0:T(8,128)(2,1)} %slice.57), channel_id=1, source_target_pairs={{0,16},{16,0},{1,17},{17,1},{2,18},{18,2},{3,19},{19,3},{4,20},{20... | collective-permute-start | bytes 589832 | tf_op jit(solution)/shard_map/ppermute | solution.py:36
  56.6 4.7 %collective-permute-done.5 = bf16[128,3072]{1,0:T(8,128)(2,1)S(1)} collective-permute-done((bf16[128,3072]{1,0:T(8,128)(2,1)S(1)}, bf16[128,3072]{1,0:T(8,128)(2,1)S(1)}, u32[]{:S(2)}, u32[]{:S(2)}) %collective-permute-start.5) | collective-permute-done | bytes 786464 | tf_op jit(solution)/shard_map/ppermute | solution.py:36
  63.2 2.3 %collective-permute-start.8 = (bf16[32,3072]{1,0:T(8,128)(2,1)S(1)}, bf16[32,3072]{1,0:T(8,128)(2,1)S(1)}, u32[]{:S(2)}, u32[]{:S(2)}) collective-permute-start(bf16[32,3072]{1,0:T(8,128)(2,1)S(1)} %get-tuple-element.32), channel_id=1, source_target_pairs={{0,96},{32,0},{64,32},{96,64},{1,97},{33,1},{65,33},{97,65},{2,98}... | collective-permute-start | bytes 589832 | tf_op jit(solution)/shard_map/ppermute | solution.py:32
  65.6 3.0 %collective-permute-done.6 = bf16[32,3072]{1,0:T(8,128)(2,1)S(1)} collective-permute-done((bf16[32,3072]{1,0:T(8,128)(2,1)S(1)}, bf16[32,3072]{1,0:T(8,128)(2,1)S(1)}, u32[]{:S(2)}, u32[]{:S(2)}) %collective-permute-start.6) | collective-permute-done | bytes 196640 | tf_op jit(solution)/shard_map/ppermute | solution.py:32
  70.4 2.1 %collective-permute-done.7 = bf16[32,3072]{1,0:T(8,128)(2,1)S(1)} collective-permute-done((bf16[32,3072]{1,0:T(8,128)(2,1)S(1)}, bf16[32,3072]{1,0:T(8,128)(2,1)S(1)}, u32[]{:S(2)}, u32[]{:S(2)}) %collective-permute-start.7) | collective-permute-done | bytes 196640 | tf_op jit(solution)/shard_map/ppermute | solution.py:32
  74.2 2.5 %collective-permute-start.13 = (bf16[32,3072]{1,0:T(8,128)(2,1)S(1)}, bf16[32,3072]{1,0:T(8,128)(2,1)S(1)}, u32[]{:S(2)}, u32[]{:S(2)}) collective-permute-start(bf16[32,3072]{1,0:T(8,128)(2,1)S(1)} %get-tuple-element.35), channel_id=1, source_target_pairs={{0,16},{16,0},{1,17},{17,1},{2,18},{18,2},{3,19},{19,3},{4,20},{20... | collective-permute-start | bytes 589832 | tf_op jit(solution)/shard_map/ppermute | solution.py:36
  76.7 2.7 %collective-permute-start.10 = (bf16[32,3072]{1,0:T(8,128)(2,1)S(1)}, bf16[32,3072]{1,0:T(8,128)(2,1)S(1)}, u32[]{:S(2)}, u32[]{:S(2)}) collective-permute-start(bf16[32,3072]{1,0:T(8,128)(2,1)S(1)} %get-tuple-element.34), channel_id=1, source_target_pairs={{0,64},{32,96},{64,0},{96,32},{1,65},{33,97},{65,1},{97,33},{2,66}... | collective-permute-start | bytes 589832 | tf_op jit(solution)/shard_map/ppermute | solution.py:32
  87.0 9.2 %collective-permute-done.16.refs_3_ = bf16[64,3072]{1,0:T(8,128)(2,1)S(1)} collective-permute-done((bf16[64,3072]{1,0:T(8,128)(2,1)S(1)}, bf16[64,3072]{1,0:T(8,128)(2,1)S(1)}, u32[]{:S(2)}, u32[]{:S(2)}) %collective-permute-start.16) | collective-permute-done | bytes 393248 | tf_op jit(solution)/shard_map/ppermute | solution.py:32
  96.2 4.4 %collective-permute-done.15.refs_2_ = bf16[64,3072]{1,0:T(8,128)(2,1)S(1)} collective-permute-done((bf16[64,3072]{1,0:T(8,128)(2,1)S(1)}, bf16[64,3072]{1,0:T(8,128)(2,1)S(1)}, u32[]{:S(2)}, u32[]{:S(2)}) %collective-permute-start.15) | collective-permute-done | bytes 393248 | tf_op jit(solution)/shard_map/ppermute | solution.py:32
  100.6 2.7 %collective-permute-done.14.refs_1_ = bf16[64,3072]{1,0:T(8,128)(2,1)S(1)} collective-permute-done((bf16[64,3072]{1,0:T(8,128)(2,1)S(1)}, bf16[64,3072]{1,0:T(8,128)(2,1)S(1)}, u32[]{:S(2)}, u32[]{:S(2)}) %collective-permute-start.14) | collective-permute-done | bytes 393248 | tf_op jit(solution)/shard_map/ppermute | solution.py:32
  103.3 3.7 %copy-done.2 = bf16[1536,3072]{1,0:T(8,128)(2,1)S(1)} copy-done((bf16[1536,3072]{1,0:T(8,128)(2,1)S(1)}, bf16[1536,3072]{1,0:T(8,128)(2,1)}, u32[]{:S(2)}) %copy-start.2) | copy-done | bytes 9437208
  107.0 4.4 %backward_other.1 = (bf16[8,32,1536]{2,1,0:T(8,128)(2,1)S(1)}, bf16[256,3072]{1,0:T(8,128)(2,1)S(1)}) custom-call(s32[2]{0:T(128)S(1)} %pad_add_fusion.place, bf16[64,3072]{1,0:T(8,128)(2,1)S(1)} %pad_maximum_fusion.2.refs_0_, bf16[64,3072]{1,0:T(8,128)(2,1)S(1)} %collective-permute-done.14.refs_1_, bf16[64,3072]{1,0:T(8,128)(2,1)S(1)} %collective-permute-done.15.refs_2_, ...), custom_call_target="tpu_custom_call" | custom-call | flops 2415919104 | bytes 13369344 | tf_op jit(solution)/shard_map/backward_other/pallas_call | solution.py:117
  111.4 3.8 %collective-permute-start.17 = (bf16[8,32,1536]{2,1,0:T(8,128)(2,1)S(1)}, bf16[8,32,1536]{2,1,0:T(8,128)(2,1)S(1)}, u32[]{:S(2)}, u32[]{:S(2)}) collective-permute-start(bf16[8,32,1536]{2,1,0:T(8,128)(2,1)S(1)} %get-tuple-element.22), channel_id=1, source_target_pairs={{0,1},{1,0},{2,3},{3,2},{4,5},{5,4},{6,7},{7,6},{8,9},{9,8},{10,11... | collective-permute-start | bytes 2359304 | tf_op jit(solution)/shard_map/ppermute | solution.py:212
  115.4 4.4 %backward_own.1 = (bf16[8,32,1536]{2,1,0:T(8,128)(2,1)S(1)}, bf16[256,3072]{1,0:T(8,128)(2,1)S(1)}) custom-call(s32[2]{0:T(128)S(1)} %pad_add_fusion.place, bf16[128,3072]{1,0:T(8,128)(2,1)S(1)} %pad_maximum_fusion.refs_0_, bf16[128,3072]{1,0:T(8,128)(2,1)S(1)} %collective-permute-done.12.refs_1_, bf16[1536,3072]{1,0:T(8,128)(2,1)S(1)} %copy-done.2), custom_call_target="tpu_custom_call" | custom-call | flops 2415919104 | bytes 13369344 | tf_op jit(solution)/shard_map/backward_own/pallas_call | solution.py:117
  122.1 4.3 %all-to-all-start.1 = ((bf16[8,32,1536]{2,1,0:T(8,128)(2,1)}), bf16[8,32,1536]{2,1,0:T(8,128)(2,1)}, u32[]{:S(2)}, u32[]{:S(2)}) async-start(bf16[8,32,1536]{2,1,0:T(8,128)(2,1)} %add_convert_fusion), calls=%async_computation.1 | async-start | bytes 1572864 | tf_op jit(solution)/shard_map/all_to_all | solution.py:215
  129.5 7.7 %weight_grad.1 = bf16[1536,3072]{1,0:T(8,128)(2,1)} custom-call(bf16[256,1536]{1,0:T(8,128)(2,1)S(1)} %copy-done.6, bf16[256,1536]{1,0:T(8,128)(2,1)S(1)} %copy-done.8, bf16[256,3072]{1,0:T(8,128)(2,1)S(1)} %copy-done.4, bf16[256,3072]{1,0:T(8,128)(2,1)S(1)} %get-tuple-element.26.grad_b), custom_call_target="tpu_custom_call" | custom-call | flops 4831838208 | bytes 14155776 | tf_op jit(solution)/shard_map/weight_grad/pallas_call | solution.py:156
  (54 shorter events, 27.1 us)
Async XLA Ops:
  19.7 17.0 %collective-permute-start.4 = (bf16[8,32,1536]{2,1,0:T(8,128)(2,1)S(1)}, bf16[8,32,1536]{2,1,0:T(8,128)(2,1)S(1)}, u32[]{:S(2)}, u32[]{:S(2)}) collective-permute-start(bf16[8,32,1536]{2,1,0:T(8,128)(2,1)S(1)} %all_to_all.10.tokens), channel_id=1, source_target_pairs={{0,1},{1,0},{2,3},{3,2},{4,5},{5,4},{6,7},{7,6},{8,9},{9,8},{10,11... | collective-permute-start | bytes 2359304 | tf_op jit(solution)/shard_map/ppermute | solution.py:190
  22.1 3.7 %copy-start = (bf16[1536,3072]{1,0:T(8,128)(2,1)S(1)}, bf16[1536,3072]{1,0:T(8,128)(2,1)}, u32[]{:S(2)}) copy-start(bf16[1536,3072]{1,0:T(8,128)(2,1)} %refs_4_.1) | copy-start | bytes 28311556
  25.8 10.9 %copy-start.1 = (bf16[1536,3072]{1,0:T(8,128)(2,1)S(1)}, bf16[1536,3072]{1,0:T(8,128)(2,1)}, u32[]{:S(2)}) copy-start(bf16[1536,3072]{1,0:T(8,128)(2,1)} %refs_4_.1) | copy-start | bytes 28311556
  31.7 12.4 %collective-permute-start = (bf16[64,3072]{1,0:T(8,128)(2,1)S(1)}, bf16[64,3072]{1,0:T(8,128)(2,1)S(1)}, u32[]{:S(2)}, u32[]{:S(2)}) collective-permute-start(bf16[64,3072]{1,0:T(8,128)(2,1)S(1)} %get-tuple-element.16), channel_id=1, source_target_pairs={{0,32},{32,64},{64,96},{96,0},{1,33},{33,65},{65,97},{97,1},{2,34}... | collective-permute-start | bytes 1179656 | tf_op jit(solution)/shard_map/ppermute | solution.py:32
  33.0 20.3 %collective-permute-start.1 = (bf16[64,3072]{1,0:T(8,128)(2,1)S(1)}, bf16[64,3072]{1,0:T(8,128)(2,1)S(1)}, u32[]{:S(2)}, u32[]{:S(2)}) collective-permute-start(bf16[64,3072]{1,0:T(8,128)(2,1)S(1)} %get-tuple-element.17), channel_id=1, source_target_pairs={{0,64},{32,96},{64,0},{96,32},{1,65},{33,97},{65,1},{97,33},{2,66}... | collective-permute-start | bytes 1179656 | tf_op jit(solution)/shard_map/ppermute | solution.py:32
  35.6 17.7 %collective-permute-start.2 = (bf16[64,3072]{1,0:T(8,128)(2,1)S(1)}, bf16[64,3072]{1,0:T(8,128)(2,1)S(1)}, u32[]{:S(2)}, u32[]{:S(2)}) collective-permute-start(bf16[64,3072]{1,0:T(8,128)(2,1)S(1)} %get-tuple-element.18), channel_id=1, source_target_pairs={{0,96},{32,0},{64,32},{96,64},{1,97},{33,1},{65,33},{97,65},{2,98}... | collective-permute-start | bytes 1179656 | tf_op jit(solution)/shard_map/ppermute | solution.py:32
  41.6 21.2 %copy-start.7 = (bf16[256,1536]{1,0:T(8,128)(2,1)}, bf16[256,1536]{1,0:T(8,128)(2,1)S(1)}, u32[]{:S(2)}) copy-start(bf16[256,1536]{1,0:T(8,128)(2,1)S(1)} %get-tuple-element.24.tok_b) | copy-start | bytes 2359300
  41.6 19.8 %collective-permute-start.5 = (bf16[128,3072]{1,0:T(8,128)(2,1)S(1)}, bf16[128,3072]{1,0:T(8,128)(2,1)S(1)}, u32[]{:S(2)}, u32[]{:S(2)}) collective-permute-start(bf16[128,3072]{1,0:T(8,128)(2,1)S(1)} %get-tuple-element.20), channel_id=1, source_target_pairs={{0,16},{16,0},{1,17},{17,1},{2,18},{18,2},{3,19},{19,3},{4,20},{20... | collective-permute-start | bytes 2359304 | tf_op jit(solution)/shard_map/ppermute | solution.py:36
  54.2 11.4 %collective-permute-start.3 = (bf16[32,3072]{1,0:T(8,128)(2,1)}, bf16[32,3072]{1,0:T(8,128)(2,1)S(1)}, u32[]{:S(2)}, u32[]{:S(2)}) collective-permute-start(bf16[32,3072]{1,0:T(8,128)(2,1)} %slice.57), channel_id=1, source_target_pairs={{0,16},{16,0},{1,17},{17,1},{2,18},{18,2},{3,19},{19,3},{4,20},{20... | collective-permute-start | bytes 589832 | tf_op jit(solution)/shard_map/ppermute | solution.py:36
  61.4 11.2 %copy-start.9 = (bf16[64,3072]{1,0:T(8,128)(2,1)S(1)}, bf16[64,3072]{1,0:T(8,128)(2,1)}, u32[]{:S(2)}) copy-start(bf16[64,3072]{1,0:T(8,128)(2,1)} %param.5) | copy-start | bytes 1179652
  62.8 5.8 %collective-permute-start.6 = (bf16[32,3072]{1,0:T(8,128)(2,1)S(1)}, bf16[32,3072]{1,0:T(8,128)(2,1)S(1)}, u32[]{:S(2)}, u32[]{:S(2)}) collective-permute-start(bf16[32,3072]{1,0:T(8,128)(2,1)S(1)} %get-tuple-element.31), channel_id=1, source_target_pairs={{0,32},{32,64},{64,96},{96,0},{1,33},{33,65},{65,97},{97,1},{2,34}... | collective-permute-start | bytes 589832 | tf_op jit(solution)/shard_map/ppermute | solution.py:32
  63.2 7.2 %collective-permute-start.8 = (bf16[32,3072]{1,0:T(8,128)(2,1)S(1)}, bf16[32,3072]{1,0:T(8,128)(2,1)S(1)}, u32[]{:S(2)}, u32[]{:S(2)}) collective-permute-start(bf16[32,3072]{1,0:T(8,128)(2,1)S(1)} %get-tuple-element.32), channel_id=1, source_target_pairs={{0,96},{32,0},{64,32},{96,64},{1,97},{33,1},{65,33},{97,65},{2,98}... | collective-permute-start | bytes 589832 | tf_op jit(solution)/shard_map/ppermute | solution.py:32
  65.5 7.0 %collective-permute-start.7 = (bf16[32,3072]{1,0:T(8,128)(2,1)S(1)}, bf16[32,3072]{1,0:T(8,128)(2,1)S(1)}, u32[]{:S(2)}, u32[]{:S(2)}) collective-permute-start(bf16[32,3072]{1,0:T(8,128)(2,1)S(1)} %get-tuple-element.33), channel_id=1, source_target_pairs={{0,64},{32,96},{64,0},{96,32},{1,65},{33,97},{65,1},{97,33},{2,66}... | collective-permute-start | bytes 589832 | tf_op jit(solution)/shard_map/ppermute | solution.py:32
  74.2 6.1 %collective-permute-start.13 = (bf16[32,3072]{1,0:T(8,128)(2,1)S(1)}, bf16[32,3072]{1,0:T(8,128)(2,1)S(1)}, u32[]{:S(2)}, u32[]{:S(2)}) collective-permute-start(bf16[32,3072]{1,0:T(8,128)(2,1)S(1)} %get-tuple-element.35), channel_id=1, source_target_pairs={{0,16},{16,0},{1,17},{17,1},{2,18},{18,2},{3,19},{19,3},{4,20},{20... | collective-permute-start | bytes 589832 | tf_op jit(solution)/shard_map/ppermute | solution.py:36
  76.7 6.3 %collective-permute-start.11 = (bf16[32,3072]{1,0:T(8,128)(2,1)S(1)}, bf16[32,3072]{1,0:T(8,128)(2,1)S(1)}, u32[]{:S(2)}, u32[]{:S(2)}) collective-permute-start(bf16[32,3072]{1,0:T(8,128)(2,1)S(1)} %get-tuple-element.34), channel_id=1, source_target_pairs={{0,32},{32,64},{64,96},{96,0},{1,33},{33,65},{65,97},{97,1},{2,34}... | collective-permute-start | bytes 589832 | tf_op jit(solution)/shard_map/ppermute | solution.py:32
  76.7 8.6 %collective-permute-start.10 = (bf16[32,3072]{1,0:T(8,128)(2,1)S(1)}, bf16[32,3072]{1,0:T(8,128)(2,1)S(1)}, u32[]{:S(2)}, u32[]{:S(2)}) collective-permute-start(bf16[32,3072]{1,0:T(8,128)(2,1)S(1)} %get-tuple-element.34), channel_id=1, source_target_pairs={{0,64},{32,96},{64,0},{96,32},{1,65},{33,97},{65,1},{97,33},{2,66}... | collective-permute-start | bytes 589832 | tf_op jit(solution)/shard_map/ppermute | solution.py:32
  79.4 5.9 %collective-permute-start.9 = (bf16[32,3072]{1,0:T(8,128)(2,1)S(1)}, bf16[32,3072]{1,0:T(8,128)(2,1)S(1)}, u32[]{:S(2)}, u32[]{:S(2)}) collective-permute-start(bf16[32,3072]{1,0:T(8,128)(2,1)S(1)} %get-tuple-element.34), channel_id=1, source_target_pairs={{0,96},{32,0},{64,32},{96,64},{1,97},{33,1},{65,33},{97,65},{2,98}... | collective-permute-start | bytes 589832 | tf_op jit(solution)/shard_map/ppermute | solution.py:32
  80.3 15.9 %collective-permute-start.16 = (bf16[64,3072]{1,0:T(8,128)(2,1)S(1)}, bf16[64,3072]{1,0:T(8,128)(2,1)S(1)}, u32[]{:S(2)}, u32[]{:S(2)}) collective-permute-start(bf16[64,3072]{1,0:T(8,128)(2,1)S(1)} %pad_maximum_fusion.2.refs_0_), channel_id=1, source_target_pairs={{0,32},{32,64},{64,96},{96,0},{1,33},{33,65},{65,97},{97,1},{2,34}... | collective-permute-start | bytes 1179656 | tf_op jit(solution)/shard_map/ppermute | solution.py:32
  80.9 19.6 %collective-permute-start.15 = (bf16[64,3072]{1,0:T(8,128)(2,1)S(1)}, bf16[64,3072]{1,0:T(8,128)(2,1)S(1)}, u32[]{:S(2)}, u32[]{:S(2)}) collective-permute-start(bf16[64,3072]{1,0:T(8,128)(2,1)S(1)} %pad_maximum_fusion.2.refs_0_), channel_id=1, source_target_pairs={{0,64},{32,96},{64,0},{96,32},{1,65},{33,97},{65,1},{97,33},{2,66}... | collective-permute-start | bytes 1179656 | tf_op jit(solution)/shard_map/ppermute | solution.py:32
  83.0 20.3 %collective-permute-start.14 = (bf16[64,3072]{1,0:T(8,128)(2,1)S(1)}, bf16[64,3072]{1,0:T(8,128)(2,1)S(1)}, u32[]{:S(2)}, u32[]{:S(2)}) collective-permute-start(bf16[64,3072]{1,0:T(8,128)(2,1)S(1)} %pad_maximum_fusion.2.refs_0_), channel_id=1, source_target_pairs={{0,96},{32,0},{64,32},{96,64},{1,97},{33,1},{65,33},{97,65},{2,98}... | collective-permute-start | bytes 1179656 | tf_op jit(solution)/shard_map/ppermute | solution.py:32
  85.4 30.0 %collective-permute-start.12 = (bf16[128,3072]{1,0:T(8,128)(2,1)S(1)}, bf16[128,3072]{1,0:T(8,128)(2,1)S(1)}, u32[]{:S(2)}, u32[]{:S(2)}) collective-permute-start(bf16[128,3072]{1,0:T(8,128)(2,1)S(1)} %pad_maximum_fusion.refs_0_), channel_id=1, source_target_pairs={{0,16},{16,0},{1,17},{17,1},{2,18},{18,2},{3,19},{19,3},{4,20},{20... | collective-permute-start | bytes 2359304 | tf_op jit(solution)/shard_map/ppermute | solution.py:36
  111.4 9.6 %collective-permute-start.17 = (bf16[8,32,1536]{2,1,0:T(8,128)(2,1)S(1)}, bf16[8,32,1536]{2,1,0:T(8,128)(2,1)S(1)}, u32[]{:S(2)}, u32[]{:S(2)}) collective-permute-start(bf16[8,32,1536]{2,1,0:T(8,128)(2,1)S(1)} %get-tuple-element.22), channel_id=1, source_target_pairs={{0,1},{1,0},{2,3},{3,2},{4,5},{5,4},{6,7},{7,6},{8,9},{9,8},{10,11... | collective-permute-start | bytes 2359304 | tf_op jit(solution)/shard_map/ppermute | solution.py:212
  122.1 5.1 %copy-start.4 = (bf16[256,3072]{1,0:T(8,128)(2,1)S(1)}, bf16[256,3072]{1,0:T(8,128)(2,1)}, u32[]{:S(2)}) copy-start(bf16[256,3072]{1,0:T(8,128)(2,1)} %copy-done.3) | copy-start | bytes 4718596
  122.1 16.6 %all-to-all-start.1 = ((bf16[8,32,1536]{2,1,0:T(8,128)(2,1)}), bf16[8,32,1536]{2,1,0:T(8,128)(2,1)}, u32[]{:S(2)}, u32[]{:S(2)}) async-start(bf16[8,32,1536]{2,1,0:T(8,128)(2,1)} %add_convert_fusion), calls=%async_computation.1 | async-start | bytes 1572864 | tf_op jit(solution)/shard_map/all_to_all | solution.py:215
  (5 other events, 8.0 us)

commit v3 on v1

v3 whole, which is shorter than its diff:
```python
import functools

import jax
import jax.numpy as jnp
from jax import lax
from jax.experimental import pallas as pl
from jax.experimental.pallas import tpu as pltpu
from jax.sharding import Mesh
from jax.sharding import PartitionSpec as P

N_Y = 4
ROW = ("y", "xh")
PLANE = ("xl", "z")
SWAP = ((0, 1), (1, 0))
MIB = 2**20
STEP = 512
F32, BF16 = jnp.float32, jnp.bfloat16
ON_CHIP = pl.BlockSpec(memory_space=pltpu.VMEM)
SCALARS = pl.BlockSpec(memory_space=pltpu.SMEM)
ANYWHERE = pl.BlockSpec(memory_space=pl.ANY)
IN_HBM = pl.BlockSpec(memory_space=pltpu.HBM)
BY_DISTANCE = tuple(((d, 0), (d, 1)) for d in range(N_Y))
BY_SIDE = tuple(tuple((d, s) for d in range(N_Y)) for s in range(2))


def gelu_parts(pre):
    coeff = 0.7978845608
    inner = coeff * (pre + 0.044715 * pre * pre * pre)
    tval = jnp.tanh(inner)
    value = 0.5 * pre * (1.0 + tval)
    slope = 0.5 * (1.0 + tval) + 0.5 * pre * (1.0 - tval * tval) * coeff * (
        1.0 + 3.0 * 0.044715 * pre * pre
    )
    return (value, slope)


def ahead(array, distance):
    return lax.ppermute(array, "y", [(i, (i + distance) % N_Y) for i in range(N_Y)])


def across(array):
    return lax.ppermute(array, "xh", SWAP)


def other_core(array):
    return lax.ppermute(array, "c", SWAP)


def after(value, *others):
    return lax.optimization_barrier((value, others))[0]


def block_of(place, distance, side):
    return lax.rem(place[0] + distance, N_Y) * 2 + lax.rem(place[1] + side, 2)


def tiles_of(width):
    return [slice(i, i + STEP) for i in range(0, width, STEP)]


def call(kernel, name, outs, ins, args, flops, size, transcendentals=0, scratch=(), limit=16, aliases=None):
    return pl.pallas_call(
        kernel,
        out_shape=[jax.ShapeDtypeStruct(shape, dtype) for shape, dtype, _ in outs],
        in_specs=ins,
        out_specs=[spec for _, _, spec in outs],
        scratch_shapes=list(scratch),
        input_output_aliases=aliases or {},
        compiler_params=pltpu.CompilerParams(vmem_limit_bytes=limit * MIB),
        cost_estimate=pl.CostEstimate(
            flops=flops, bytes_accessed=size, transcendentals=transcendentals
        ),
        name=name,
    )(*args)


def load_kernel(offset, source, out, sem):
    columns = slice(offset, offset + out.shape[1])
    copy = pltpu.make_async_copy(source.at[:, columns], out, sem)
    copy.start()
    copy.wait()


def load(weight, part, name):
    width = weight.shape[0]
    count = part.stop - part.start
    return call(
        functools.partial(load_kernel, part.start),
        name,
        [((width, count), BF16, ON_CHIP)],
        [ANYWHERE],
        [weight],
        flops=0,
        size=4 * width * count,
        scratch=[pltpu.SemaphoreType.DMA(())],
        limit=48,
    )[0]


def row_of(rows, core, distance, side):
    return (core * 2 * N_Y + 2 * distance + side) * rows


def place_tokens(place, tokens, held, core):
    rows = tokens.shape[1]
    for distance in range(N_Y):
        for side in range(2):
            start = row_of(rows, core, distance, side)
            held[start : start + rows, :] = tokens[block_of(place, distance, side)]


def put_sides(part, outs, columns, rows, core):
    for side, out in enumerate(outs):
        for distance in range(N_Y):
            start, to = (2 * distance + side) * rows, (core * N_Y + distance) * rows
            out[to : to + rows, columns] = part[start : start + rows, :]


def tile_copy(weight, offset, tiles, sems, i):
    columns = pl.ds(pl.multiple_of(offset + i * STEP, STEP), STEP)
    return pltpu.make_async_copy(weight.at[:, columns], tiles.at[i], sems.at[i])


def forward_side_kernel(place, own, other, weight, toks, first, second):
    rows = own.shape[1]
    place_tokens(place, own, toks, 0)
    place_tokens(place, other, toks, 1)

    def body(i, carry):
        columns = pl.ds(pl.multiple_of(i * STEP, STEP), STEP)
        part = jnp.dot(toks[...], weight[:, columns], preferred_element_type=F32).astype(BF16)
        for core in range(2):
            start = row_of(rows, core, 0, 0)
            put_sides(part[start : start + 2 * N_Y * rows], (first, second), columns, rows, core)
        return carry

    lax.fori_loop(0, weight.shape[1] // STEP, body, 0)


def forward_side(place, own, other, weight):
    blocks, rows, width = own.shape
    count = weight.shape[1]
    side = ((blocks * rows, count), BF16, ON_CHIP)
    return call(
        forward_side_kernel,
        "forward_side",
        [((2 * blocks * rows, width), BF16, ON_CHIP), side, side],
        [SCALARS] + [ON_CHIP] * 3,
        [place, own, other, weight],
        flops=4 * blocks * rows * width * count,
        size=2 * width * count,
    )


def forward_distance_kernel(offset, toks, weight, *refs):
    *outs, tiles, sems = refs
    steps = tiles.shape[0]
    rows = outs[0].shape[0] // 4
    for i in range(steps):
        tile_copy(weight, offset, tiles, sems, i).start()

    def body(i, carry):
        tile_copy(weight, offset, tiles, sems, i).wait()
        columns = pl.ds(pl.multiple_of(i * STEP, STEP), STEP)
        part = jnp.dot(toks[...], tiles[i], preferred_element_type=F32).astype(BF16)
        for distance, out in enumerate(outs):
            for side in range(2):
                for core in range(2):
                    start, to = row_of(rows, core, distance, side), (2 * side + core) * rows
                    out[to : to + rows, columns] = part[start : start + rows, :]
        return carry

    lax.fori_loop(0, steps, body, 0)


def forward_distance(toks, weight, part):
    tokens, width = toks.shape
    count = part.stop - part.start
    return call(
        functools.partial(forward_distance_kernel, part.start),
        "forward_distance",
        [((tokens // N_Y, count), BF16, ON_CHIP)] * N_Y,
        [ON_CHIP, ANYWHERE],
        [toks, weight],
        flops=2 * tokens * width * count,
        size=2 * width * count,
        scratch=[
            pltpu.VMEM((count // STEP, width, STEP), BF16),
            pltpu.SemaphoreType.DMA((count // STEP,)),
        ],
        limit=48,
    )


def assemble(grads, pieces, held, core):
    rows = held.shape[0] // (2 * N_Y)
    for grad, piece in zip(grads, pieces):
        for slot, (distance, side) in enumerate(piece):
            start, at = (2 * distance + side) * rows, (2 * slot + core) * rows
            held[start : start + rows, :] = grad[at : at + rows, :]


def times_weight(grad, weight, columns):
    return lax.dot_general(
        grad, weight[columns, :], (((1,), (1,)), ((), ())), preferred_element_type=F32
    )


def backward_first_kernel(pieces, *refs):
    grads = refs[: len(pieces)]
    weight, out, full, held, sem = refs[len(pieces) :]
    half = held.shape[0] // 2
    for core in range(2):
        assemble(grads, pieces, held.at[core * half : (core + 1) * half], core)
    copy = pltpu.make_async_copy(held, full, sem)
    copy.start()

    def body(i, carry):
        columns = pl.ds(pl.multiple_of(i * STEP, STEP), STEP)
        out[:, columns] = times_weight(held[...], weight, columns)
        return carry

    lax.fori_loop(0, weight.shape[0] // STEP, body, 0)
    copy.wait()


def backward_first(grads, weight, pieces):
    width, hidden = weight.shape
    count = sum(grad.shape[0] for grad in grads)
    return call(
        functools.partial(backward_first_kernel, pieces),
        "backward_first",
        [((count, width), F32, ON_CHIP), ((count, hidden), BF16, IN_HBM)],
        [ON_CHIP] * (len(grads) + 1),
        [*grads, weight],
        flops=2 * count * width * hidden,
        size=2 * width * hidden,
        scratch=[pltpu.VMEM((count, hidden), BF16), pltpu.SemaphoreType.DMA(())],
    )


def backward_last_kernel(pieces, core, place, *refs):
    grads = refs[: len(pieces)]
    weight, begun, out, full, held, sem = refs[len(pieces) :]
    assemble(grads, pieces, held, core)
    copy = pltpu.make_async_copy(held, full, sem)
    copy.start()
    rows = out.shape[1]
    half = slice(core * 2 * N_Y * rows, (core + 1) * 2 * N_Y * rows)

    def body(i, carry):
        columns = pl.ds(pl.multiple_of(i * STEP, STEP), STEP)
        part = (begun[half, columns] + times_weight(held[...], weight, columns)).astype(BF16)
        for distance in range(N_Y):
            for side in range(2):
                start = (2 * distance + side) * rows
                out[block_of(place, distance, side), :, columns] = part[start : start + rows, :]
        return carry

    lax.fori_loop(0, weight.shape[0] // STEP, body, 0)
    copy.wait()


def backward_last(place, grads, weight, begun, pieces, core, name):
    width, hidden = weight.shape
    count = begun.shape[0] // 2
    return call(
        functools.partial(backward_last_kernel, pieces, core),
        name,
        [((2 * N_Y, count // (2 * N_Y), width), BF16, ON_CHIP), ((count, hidden), BF16, IN_HBM)],
        [SCALARS] + [ON_CHIP] * (len(grads) + 2),
        [place, *grads, weight, begun],
        flops=2 * count * width * hidden,
        size=2 * width * hidden,
        scratch=[pltpu.VMEM((count, hidden), BF16), pltpu.SemaphoreType.DMA(())],
    )


def add_kernel(mine, got, out):
    for block in range(out.shape[0]):
        out[block] = (mine[block].astype(F32) + got[block].astype(F32)).astype(BF16)


def turn_kernel(tok, out, held, sem):
    held[...] = tok[...].T
    copy = pltpu.make_async_copy(held, out, sem)
    copy.start()
    copy.wait()


def turn(tok):
    rows, width = tok.shape
    return call(
        turn_kernel,
        "turn_tokens",
        [((width, rows), BF16, IN_HBM)],
        [ON_CHIP],
        [tok],
        flops=0,
        size=4 * rows * width,
        scratch=[pltpu.VMEM((width, rows), BF16), pltpu.SemaphoreType.DMA(())],
    )[0]


def weight_grad_kernel(corners, *refs):
    turned, *grads = refs[: len(corners) + 1]
    out, held_turned, held, tiles, sems = refs[len(corners) + 1 :]
    step = tiles.shape[2]
    steps = held.shape[1] // step
    loads = [pltpu.make_async_copy(turned, held_turned, sems.at[2])]
    for i, (grad, (row, column)) in enumerate(zip(grads, corners)):
        rows, columns = slice(row, row + grad.shape[0]), slice(column, column + grad.shape[1])
        loads.append(pltpu.make_async_copy(grad, held.at[rows, columns], sems.at[3 + i]))
    for load in loads:
        load.start()
    for load in loads:
        load.wait()

    def copy(i):
        columns = pl.ds(pl.multiple_of(i * step, step), step)
        slot = lax.rem(i, 2)
        return pltpu.make_async_copy(tiles.at[slot], out.at[:, columns], sems.at[slot])

    def body(i, carry):
        columns = pl.ds(pl.multiple_of(i * step, step), step)

        @pl.when(i >= 2)
        def _():
            copy(i - 2).wait()

        total = jnp.dot(held_turned[...], held[:, columns], preferred_element_type=F32)
        tiles[lax.rem(i, 2)] = total.astype(BF16)
        copy(i).start()
        return carry

    lax.fori_loop(0, steps, body, 0)
    copy(steps - 2).wait()
    copy(steps - 1).wait()


def weight_grad_of(turned, grads, corners, hidden):
    width, rows = turned.shape
    return call(
        functools.partial(weight_grad_kernel, corners),
        "weight_grad",
        [((width, hidden), BF16, IN_HBM)],
        [ANYWHERE] * (1 + len(grads)),
        [turned, *grads],
        flops=2 * rows * width * hidden,
        size=2 * width * hidden,
        scratch=[
            pltpu.VMEM(turned.shape, BF16),
            pltpu.VMEM((rows, hidden), BF16),
            pltpu.VMEM((2, width, STEP), BF16),
            pltpu.SemaphoreType.DMA((3 + len(grads),)),
        ],
        limit=56,
    )[0]


def sum_distance_kernel(mine, got_1, got_2, got_3, near, far):
    rows = near.shape[0]
    for columns in tiles_of(near.shape[1]):
        total = mine[:, columns].astype(F32)
        for got in (got_1, got_2, got_3):
            total += got[:, columns].astype(F32)
        near[:, columns] = total[:rows]
        far[:, columns] = total[rows:].astype(BF16)


def sum_side_kernel(mine, got, *outs):
    rows = outs[0].shape[0] // 2
    for columns in tiles_of(mine.shape[1]):
        for distance, out in enumerate(outs):
            for core in range(2):
                start = (core * N_Y + distance) * rows
                block = slice(start, start + rows)
                total = mine[block, columns].astype(F32) + got[block, columns].astype(F32)
                out[core * rows : (core + 1) * rows, columns] = total.astype(out.dtype)


def gelu_kernel(offset, place, *refs):
    terms = refs[:-3]
    cot, act, grad = refs[-3:]
    rows = act.shape[0] // 2
    for side in range(2):
        core = lax.rem(place[2] + side, 2)
        block = slice(side * rows, (side + 1) * rows)
        absolute = pl.ds(pl.multiple_of(core * rows, rows), rows)
        for columns in tiles_of(act.shape[1]):
            pre = terms[0][block, columns].astype(F32)
            for term in terms[1:]:
                pre += term[block, columns].astype(F32)
            value, slope = gelu_parts(pre)
            act[absolute, columns] = value.astype(BF16)
            from_cot = slice(offset + columns.start, offset + columns.stop)
            grad[block, columns] = (cot[absolute, from_cot].astype(F32) * slope).astype(BF16)


def gelu_step(place, terms, cot, offset, name):
    shape = terms[0].shape
    size = shape[0] * shape[1]
    return call(
        functools.partial(gelu_kernel, offset),
        name,
        [(shape, BF16, ON_CHIP), (shape, BF16, ON_CHIP)],
        [SCALARS] + [ON_CHIP] * (len(terms) + 1),
        [place, *terms, cot],
        flops=40 * size,
        size=8 * size,
        transcendentals=size,
    )


def last_sum_kernel(got, out):
    for columns in tiles_of(out.shape[1]):
        total = got[0, :, columns].astype(F32)
        for i in range(1, got.shape[0]):
            total += got[i, :, columns].astype(F32)
        out[:, columns] = total.astype(BF16)


def local(tokens, weight, cotangent):
    rows, width = tokens.shape
    block, hidden = cotangent.shape
    cut = hidden // 2
    part_a, part_b = slice(0, cut), slice(cut, hidden)
    small_a, small_b = (block, cut), (block, hidden - cut)
    place = jnp.stack([lax.axis_index(a) for a in ("y", "xh", "c")]).astype(jnp.int32)

    spread = jnp.broadcast_to(tokens[None], (8, rows, width))
    own = lax.all_to_all(spread, PLANE, 0, 0, tiled=True)
    other = other_core(own)

    held = load(after(weight, own), part_b, "load_forward")
    toks, *sides = forward_side(place, own, other, held)
    got_side = across(sides[1])
    parts = forward_distance(toks, weight, part_a)
    got_a = [ahead(parts[d], d) for d in (1, 2, 3)]
    got_side = after(got_side, parts[0])
    kept, *sent = call(
        sum_side_kernel,
        "sum_b",
        [(small_b, F32 if d == 0 else BF16, ON_CHIP) for d in range(N_Y)],
        [ON_CHIP] * 2,
        [sides[0], got_side],
        flops=8 * block * hidden,
        size=16 * block * hidden,
    )
    got_b = [ahead(sent[d - 1], d) for d in (1, 2, 3)]
    got_a = after(got_a, sent[0])
    near, far = call(
        sum_distance_kernel,
        "sum_a",
        [(small_a, F32, ON_CHIP), (small_a, BF16, ON_CHIP)],
        [ON_CHIP] * 4,
        [parts[0], *got_a],
        flops=8 * block * hidden,
        size=16 * block * hidden,
    )
    got_far = across(far)

    act_b, grad_b = gelu_step(place, [kept, *got_b], cotangent, cut, "gelu_b")
    grad_b_far = across(grad_b)
    got_far = after(got_far, grad_b)
    act_a, grad_a = gelu_step(place, [near, got_far], cotangent, 0, "gelu_a")
    by_y = [ahead(grad_a, -d) for d in (1, 2, 3)]
    both = jnp.concatenate([grad_b, grad_b_far], axis=0)
    wide = [ahead(both, -d) for d in (1, 2, 3)]
    by_y = jnp.concatenate([grad_a] + after(by_y, both), axis=0)
    by_y_far = across(by_y)
    late, toks = after((weight, toks), by_y)
    held_a, held_b = load(late, part_a, "load_a"), load(late, part_b, "load_b")
    turned = turn(toks)
    activated = jnp.concatenate([act_a, act_b], axis=1)

    by_y_far = after(by_y_far, held_a, held_b, turned, activated)
    begun, full_a = backward_first([by_y, by_y_far], held_a, BY_SIDE)
    wide = [both, *after(wide, begun)]
    theirs, full_theirs = backward_last(place, wide, held_b, begun, BY_DISTANCE, 1, "backward_other")
    arrived = other_core(theirs)
    wide = after(wide, theirs)
    mine, full_mine = backward_last(place, wide, held_b, begun, BY_DISTANCE, 0, "backward_own")
    (chip,) = call(
        add_kernel,
        "chip_sum",
        [(mine.shape, BF16, ON_CHIP)],
        [ON_CHIP] * 2,
        [mine, arrived],
        flops=mine.size,
        size=6 * mine.size,
    )
    last = lax.all_to_all(chip, PLANE, 0, 0, tiled=True)
    full_mine = after(full_mine, chip)
    corners = [(0, 0), (0, cut), (8 * rows, cut)]
    weight_grad = weight_grad_of(turned, [full_a, full_mine, full_theirs], corners, hidden)
    (input_grad,) = call(
        last_sum_kernel,
        "last_sum",
        [((rows, width), BF16, ON_CHIP)],
        [ON_CHIP],
        [last],
        flops=8 * rows * width,
        size=16 * rows * width,
    )
    return (activated, input_grad, weight_grad)


def solution(mesh):
    fine = Mesh(mesh.devices.reshape(N_Y, 2, 2, 4, 2), ("y", "xh", "xl", "z", "c"))
    col = ("xl", "z", "c")
    return jax.shard_map(
        local,
        mesh=fine,
        in_specs=(P(col, ROW), P(ROW, col), P(ROW, col)),
        out_specs=(P(ROW, col), P(col, ROW), P(ROW, col)),
        check_vma=False,
    )
```

time: 194 us -> 133 us (0.69)
  blocking collectives: 120 us -> 18.1 us
  Pallas kernels: 0 us -> 37.7 us
  waiting for transfers between devices: 13.6 us -> 43 us
  starting transfers between devices: 4.19 us -> 28.6 us
  matrix products: 22.7 us -> 0 us
  between operations: 14.1 us -> 0.89 us
  local copies, waits for them, and re-layouts: 15.2 us -> 4.02 us
  other arithmetic: 3.3 us -> 0.08 us
    all_to_all x6 -> x1, blocking collectives: 120 us -> 18.1 us  [local(): own = lax.all_to_all(spread, PLANE, 0, 0, tiled=True)]
    ppermute x0 -> x18, waiting for transfers between devices: none -> 40.6 us  [the longest x4 21.2 us: across(): return lax.ppermute(array, 'xh', SWAP)]
    pallas_call x0 -> x16, Pallas kernels: none -> 37.7 us  [call(): pl.pallas_call(kernel, out_shape=[jax.ShapeDtypeStruct(shape, dtype) for...]
    ppermute x0 -> x18, starting transfers between devices: none -> 25.1 us  [the longest x12 14.9 us: ahead(): lax.ppermute(array, 'y', [(i, (i + distance) % N_Y) for i in range(N_Y)])]
    dot_general x3 -> x0, matrix products: 22.7 us -> none  [the longest x1 9.49 us: local(): jnp.dot(full_tokens.T, grad_full, preferred_element_type=jnp.float32)]
    all_gather x1 -> x0, waiting for transfers between devices: 13.5 us -> none  [local(): full_tokens = lax.all_gather(part, 'c', axis=1, tiled=True)]
    unnamed x13 -> x17, local copies, waits for them, and re-layouts: 13.1 us -> 3.03 us
    all_to_all x1, waiting for transfers between devices: 0.01 us -> 2.4 us  [local(): last = lax.all_to_all(chip, PLANE, 0, 0, tiled=True)]
  transfers between devices with their start and end apart: 2 -> 19, of which waited for: 1 -> 10; matrix products, arithmetic and copies ran while one was open for 11% -> 0% of each run, Pallas kernels for 0% -> 23%
where the time goes in v3:
time: 133 us; the launch traced here: 132 us
  waiting for transfers between devices  43 us (32%)
  Pallas kernels  37.7 us (28%)
  starting transfers between devices  28.6 us (22%)
  blocking collectives  18.1 us (14%)
  local copies, waits for them, and re-layouts  4.02 us (3%)
    pallas_call x16, Pallas kernels, call(): pl.pallas_call(kernel, out_shape=[jax.ShapeDtypeStruct(shape, dtype) for...  37.7 us
    ppermute x4, waiting for transfers between devices, across(): return lax.ppermute(array, 'xh', SWAP)  21.2 us
    ppermute x12, waiting for transfers between devices, ahead(): lax.ppermute(array, 'y', [(i, (i + distance) % N_Y) for i in range(N_Y)])  19.4 us
    all_to_all x1, blocking collectives, local(): own = lax.all_to_all(spread, PLANE, 0, 0, tiled=True)  18.1 us
    ppermute x12, starting transfers between devices, ahead(): lax.ppermute(array, 'y', [(i, (i + distance) % N_Y) for i in range(N_Y)])  14.9 us
    ppermute x4, starting transfers between devices, across(): return lax.ppermute(array, 'xh', SWAP)  6.23 us
    ppermute x2, starting transfers between devices, other_core(): return lax.ppermute(array, 'c', SWAP)  3.96 us
    all_to_all x1, starting transfers between devices, local(): last = lax.all_to_all(chip, PLANE, 0, 0, tiled=True)  3.55 us
  transfers between devices with their start and end apart: 19, of which 10 were waited for; matrix products, arithmetic and copies ran while one was open for 0% of the time, Pallas kernels for 23%

profile of v3, /device:TPU:1, one launch (start us, length us, event | category | flops | bytes accessed | tf_op | source)
XLA Modules:
  0.0 132.4 jit_solution(3564096231571469838)
XLA Ops:
  1.6 18.1 %all_to_all.10.own = bf16[8,32,1536]{2,1,0:T(8,128)(2,1)S(1)} all-to-all(bf16[8,32,1536]{2,1,0:T(8,128)(2,1)S(1)} %broadcast_in_dim.2), channel_id=1, replica_groups=mesh['y'=4,'xh'=2,'xl'=2,'z'=4,'c'=2] {'xl','z'}, dimensions={0} | all-to-all | bytes 1572864 | tf_op jit(solution)/shard_map/all_to_all | solution.py:432
  19.7 2.4 %collective-permute-start = (bf16[8,32,1536]{2,1,0:T(8,128)(2,1)S(1)}, bf16[8,32,1536]{2,1,0:T(8,128)(2,1)S(1)}, u32[]{:S(2)}, u32[]{:S(2)}) collective-permute-start(bf16[8,32,1536]{2,1,0:T(8,128)(2,1)S(1)} %all_to_all.10.own), channel_id=1, source_target_pairs={{0,1},{1,0},{2,3},{3,2},{4,5},{5,4},{6,7},{7,6},{8,9},{9,8},{10,11... | collective-permute-start | bytes 2359304 | tf_op jit(solution)/shard_map/ppermute | solution.py:46
  24.5 3.6 %forward_side.1 = (bf16[512,1536]{1,0:T(8,128)(2,1)S(1)}, bf16[256,1536]{1,0:T(8,128)(2,1)S(1)}, bf16[256,1536]{1,0:T(8,128)(2,1)S(1)}) custom-call(s32[3]{0:T(128)S(1)} %pad_add_fusion.place, bf16[8,32,1536]{2,1,0:T(8,128)(2,1)S(1)} %all_to_all.10.own, bf16[8,32,1536]{2,1,0:T(8,128)(2,1)S(1)} %collective-permute-done.other, ...), custom_call_target="tpu_custom_call" | custom-call | flops 2415919104 | bytes 4718592 | tf_op jit(solution)/shard_map/forward_side/pallas_call | solution.py:62
  28.1 2.5 %collective-permute-start.4 = (bf16[256,1536]{1,0:T(8,128)(2,1)S(1)}, bf16[256,1536]{1,0:T(8,128)(2,1)S(1)}, u32[]{:S(2)}, u32[]{:S(2)}) collective-permute-start(bf16[256,1536]{1,0:T(8,128)(2,1)S(1)} %get-tuple-element.53), channel_id=1, source_target_pairs={{0,16},{16,0},{1,17},{17,1},{2,18},{18,2},{3,19},{19,3},{4,20},{20... | collective-permute-start | bytes 2359304 | tf_op jit(solution)/shard_map/ppermute | solution.py:42
  30.6 4.4 %forward_distance.1 = (bf16[128,1536]{1,0:T(8,128)(2,1)S(1)}, bf16[128,1536]{1,0:T(8,128)(2,1)S(1)}, bf16[128,1536]{1,0:T(8,128)(2,1)S(1)}, bf16[128,1536]{1,0:T(8,128)(2,1)S(1)}) custom-call(bf16[512,1536]{1,0:T(8,128)(2,1)S(1)} %get-tuple-element.73.toks.tok, bf16[1536,3072]{1,0:T(8,128)(2,1)} %source.2), custom_call_target="tpu_custom_call" | custom-call | flops 2415919104 | bytes 4718592 | tf_op jit(solution)/shard_map/forward_distance/pallas_call | solution.py:62
  36.4 2.6 %collective-permute-start.2 = (bf16[128,1536]{1,0:T(8,128)(2,1)S(1)}, bf16[128,1536]{1,0:T(8,128)(2,1)S(1)}, u32[]{:S(2)}, u32[]{:S(2)}) collective-permute-start(bf16[128,1536]{1,0:T(8,128)(2,1)S(1)} %get-tuple-element.50), channel_id=1, source_target_pairs={{0,64},{32,96},{64,0},{96,32},{1,65},{33,97},{65,1},{97,33},{2,66}... | collective-permute-start | bytes 1179656 | tf_op jit(solution)/shard_map/ppermute | solution.py:38
  40.1 8.7 %collective-permute-done.4.got = bf16[256,1536]{1,0:T(8,128)(2,1)S(1)} collective-permute-done((bf16[256,1536]{1,0:T(8,128)(2,1)S(1)}, bf16[256,1536]{1,0:T(8,128)(2,1)S(1)}, u32[]{:S(2)}, u32[]{:S(2)}) %collective-permute-start.4) | collective-permute-done | bytes 786464 | tf_op jit(solution)/shard_map/ppermute | solution.py:42
  50.4 2.6 %collective-permute-start.7 = (bf16[64,1536]{1,0:T(8,128)(2,1)S(1)}, bf16[64,1536]{1,0:T(8,128)(2,1)S(1)}, u32[]{:S(2)}, u32[]{:S(2)}) collective-permute-start(bf16[64,1536]{1,0:T(8,128)(2,1)S(1)} %get-tuple-element.62), channel_id=1, source_target_pairs={{0,64},{32,96},{64,0},{96,32},{1,65},{33,97},{65,1},{97,33},{2,66}... | collective-permute-start | bytes 589832 | tf_op jit(solution)/shard_map/ppermute | solution.py:38
  54.1 2.4 %collective-permute-done.2.got_2 = bf16[128,1536]{1,0:T(8,128)(2,1)S(1)} collective-permute-done((bf16[128,1536]{1,0:T(8,128)(2,1)S(1)}, bf16[128,1536]{1,0:T(8,128)(2,1)S(1)}, u32[]{:S(2)}, u32[]{:S(2)}) %collective-permute-start.2) | collective-permute-done | bytes 393248 | tf_op jit(solution)/shard_map/ppermute | solution.py:38
  57.2 4.6 %collective-permute-done.6.refs_1_ = bf16[64,1536]{1,0:T(8,128)(2,1)S(1)} collective-permute-done((bf16[64,1536]{1,0:T(8,128)(2,1)S(1)}, bf16[64,1536]{1,0:T(8,128)(2,1)S(1)}, u32[]{:S(2)}, u32[]{:S(2)}) %collective-permute-start.6) | collective-permute-done | bytes 196640 | tf_op jit(solution)/shard_map/ppermute | solution.py:38
  61.8 3.1 %collective-permute-done.7.refs_2_ = bf16[64,1536]{1,0:T(8,128)(2,1)S(1)} collective-permute-done((bf16[64,1536]{1,0:T(8,128)(2,1)S(1)}, bf16[64,1536]{1,0:T(8,128)(2,1)S(1)}, u32[]{:S(2)}, u32[]{:S(2)}) %collective-permute-start.7) | collective-permute-done | bytes 196640 | tf_op jit(solution)/shard_map/ppermute | solution.py:38
  67.3 2.6 %collective-permute-start.13 = (bf16[64,1536]{1,0:T(8,128)(2,1)S(1)}, bf16[64,1536]{1,0:T(8,128)(2,1)S(1)}, u32[]{:S(2)}, u32[]{:S(2)}) collective-permute-start(bf16[64,1536]{1,0:T(8,128)(2,1)S(1)} %get-tuple-element.68), channel_id=1, source_target_pairs={{0,96},{32,0},{64,32},{96,64},{1,97},{33,1},{65,33},{97,65},{2,98}... | collective-permute-start | bytes 589832 | tf_op jit(solution)/shard_map/ppermute | solution.py:38
  72.7 2.4 %collective-permute-done.13 = bf16[64,1536]{1,0:T(8,128)(2,1)S(1)} collective-permute-done((bf16[64,1536]{1,0:T(8,128)(2,1)S(1)}, bf16[64,1536]{1,0:T(8,128)(2,1)S(1)}, u32[]{:S(2)}, u32[]{:S(2)}) %collective-permute-start.13) | collective-permute-done | bytes 196640 | tf_op jit(solution)/shard_map/ppermute | solution.py:38
  76.8 5.2 %collective-permute-done.15 = bf16[64,1536]{1,0:T(8,128)(2,1)S(1)} collective-permute-done((bf16[64,1536]{1,0:T(8,128)(2,1)S(1)}, bf16[64,1536]{1,0:T(8,128)(2,1)S(1)}, u32[]{:S(2)}, u32[]{:S(2)}) %collective-permute-start.15) | collective-permute-done | bytes 196640 | tf_op jit(solution)/shard_map/ppermute | solution.py:38
  82.1 2.6 %collective-permute-start.16 = (bf16[256,1536]{1,0:T(8,128)(2,1)S(1)}, bf16[256,1536]{1,0:T(8,128)(2,1)S(1)}, u32[]{:S(2)}, u32[]{:S(2)}) collective-permute-start(bf16[256,1536]{1,0:T(8,128)(2,1)S(1)} %constant_dynamic-update-slice_fusion.4.refs_0_), channel_id=1, source_target_pairs={{0,16},{16,0},{1,17},{17,1},{2,18},{18,2},{3,19},{19,3},{4,20},{20... | collective-permute-start | bytes 2359304 | tf_op jit(solution)/shard_map/ppermute | solution.py:42
  86.3 2.5 %load_a.1.refs_2_ = bf16[1536,1536]{1,0:T(8,128)(2,1)S(1)} custom-call(bf16[1536,3072]{1,0:T(8,128)(2,1)} %source.2), custom_call_target="tpu_custom_call" | custom-call | bytes 9437184 | tf_op jit(solution)/shard_map/load_a/pallas_call | solution.py:62
  88.8 2.3 %load_b.1.refs_4_ = bf16[1536,1536]{1,0:T(8,128)(2,1)S(1)} custom-call(bf16[1536,3072]{1,0:T(8,128)(2,1)} %source.2), custom_call_target="tpu_custom_call" | custom-call | bytes 9437184 | tf_op jit(solution)/shard_map/load_b/pallas_call | solution.py:62
  91.7 10.3 %collective-permute-done.16.refs_1_ = bf16[256,1536]{1,0:T(8,128)(2,1)S(1)} collective-permute-done((bf16[256,1536]{1,0:T(8,128)(2,1)S(1)}, bf16[256,1536]{1,0:T(8,128)(2,1)S(1)}, u32[]{:S(2)}, u32[]{:S(2)}) %collective-permute-start.16) | collective-permute-done | bytes 786464 | tf_op jit(solution)/shard_map/ppermute | solution.py:42
  102.1 3.3 %backward_first.1 = (f32[512,1536]{1,0:T(8,128)S(1)}, bf16[512,1536]{1,0:T(8,128)(2,1)S(1)}) custom-call(bf16[256,1536]{1,0:T(8,128)(2,1)S(1)} %constant_dynamic-update-slice_fusion.4.refs_0_, bf16[256,1536]{1,0:T(8,128)(2,1)S(1)} %collective-permute-done.16.refs_1_, bf16[1536,1536]{1,0:T(8,128)(2,1)S(1)} %load_a.1.refs_2_), custom_call_target="tpu_custom_call" | custom-call | flops 2415919104 | bytes 4718592 | tf_op jit(solution)/shard_map/backward_first/pallas_call | solution.py:62
  106.5 2.5 %backward_other.1 = (bf16[8,32,1536]{2,1,0:T(8,128)(2,1)S(1)}, bf16[256,1536]{1,0:T(8,128)(2,1)S(1)}) custom-call(s32[3]{0:T(128)S(1)} %pad_add_fusion.place, bf16[128,1536]{1,0:T(8,128)(2,1)S(1)} %constant_dynamic-update-slice_fusion.2.refs_0_, bf16[128,1536]{1,0:T(8,128)(2,1)S(1)} %collective-permute-done.10.refs_1_, ...), custom_call_target="tpu_custom_call" | custom-call | flops 1207959552 | bytes 4718592 | tf_op jit(solution)/shard_map/backward_other/pallas_call | solution.py:62
  111.5 2.5 %backward_own.1 = (bf16[8,32,1536]{2,1,0:T(8,128)(2,1)S(1)}, bf16[256,1536]{1,0:T(8,128)(2,1)S(1)}) custom-call(s32[3]{0:T(128)S(1)} %pad_add_fusion.place, bf16[128,1536]{1,0:T(8,128)(2,1)S(1)} %constant_dynamic-update-slice_fusion.2.refs_0_, bf16[128,1536]{1,0:T(8,128)(2,1)S(1)} %collective-permute-done.10.refs_1_, ...), custom_call_target="tpu_custom_call" | custom-call | flops 1207959552 | bytes 4718592 | tf_op jit(solution)/shard_map/backward_own/pallas_call | solution.py:62
  115.9 3.5 %all-to-all-start.1 = ((bf16[8,32,1536]{2,1,0:T(8,128)(2,1)}), bf16[8,32,1536]{2,1,0:T(8,128)(2,1)S(1)}, u32[]{:S(2)}, u32[]{:S(2)}) async-start(bf16[8,32,1536]{2,1,0:T(8,128)(2,1)} %chip_sum.1), calls=%async_computation.1 | async-start | bytes 1572864 | tf_op jit(solution)/shard_map/all_to_all | solution.py:493
  119.5 9.7 %weight_grad.1 = bf16[1536,3072]{1,0:T(8,128)(2,1)} custom-call(bf16[1536,512]{1,0:T(8,128)(2,1)} %copy-done, bf16[512,1536]{1,0:T(8,128)(2,1)} %copy-done.4, bf16[256,1536]{1,0:T(8,128)(2,1)} %copy-done.3, bf16[256,1536]{1,0:T(8,128)(2,1)} %copy-done.2), custom_call_target="tpu_custom_call" | custom-call | flops 4831838208 | bytes 9437184 | tf_op jit(solution)/shard_map/weight_grad/pallas_call | solution.py:62
  129.2 2.4 %all-to-all-done.1.got = bf16[8,32,1536]{2,1,0:T(8,128)(2,1)S(1)} async-done(((bf16[8,32,1536]{2,1,0:T(8,128)(2,1)}), bf16[8,32,1536]{2,1,0:T(8,128)(2,1)S(1)}, u32[]{:S(2)}, u32[]{:S(2)}) %all-to-all-start.1) | async-done | bytes 786464 | tf_op jit(solution)/shard_map/all_to_all | solution.py:493
  (53 shorter events, 24.6 us)
Async XLA Ops:
  19.7 4.8 %collective-permute-start = (bf16[8,32,1536]{2,1,0:T(8,128)(2,1)S(1)}, bf16[8,32,1536]{2,1,0:T(8,128)(2,1)S(1)}, u32[]{:S(2)}, u32[]{:S(2)}) collective-permute-start(bf16[8,32,1536]{2,1,0:T(8,128)(2,1)S(1)} %all_to_all.10.own), channel_id=1, source_target_pairs={{0,1},{1,0},{2,3},{3,2},{4,5},{5,4},{6,7},{7,6},{8,9},{9,8},{10,11... | collective-permute-start | bytes 2359304 | tf_op jit(solution)/shard_map/ppermute | solution.py:46
  28.1 20.8 %collective-permute-start.4 = (bf16[256,1536]{1,0:T(8,128)(2,1)S(1)}, bf16[256,1536]{1,0:T(8,128)(2,1)S(1)}, u32[]{:S(2)}, u32[]{:S(2)}) collective-permute-start(bf16[256,1536]{1,0:T(8,128)(2,1)S(1)} %get-tuple-element.53), channel_id=1, source_target_pairs={{0,16},{16,0},{1,17},{17,1},{2,18},{18,2},{3,19},{19,3},{4,20},{20... | collective-permute-start | bytes 2359304 | tf_op jit(solution)/shard_map/ppermute | solution.py:42
  30.6 34.3 %copy-start.1 = (bf16[64,3072]{1,0:T(8,128)(2,1)S(1)}, bf16[64,3072]{1,0:T(8,128)(2,1)}, u32[]{:S(2)}) copy-start(bf16[64,3072]{1,0:T(8,128)(2,1)} %refs_2_.1) | copy-start | bytes 1179652
  35.0 18.0 %collective-permute-start.1 = (bf16[128,1536]{1,0:T(8,128)(2,1)S(1)}, bf16[128,1536]{1,0:T(8,128)(2,1)S(1)}, u32[]{:S(2)}, u32[]{:S(2)}) collective-permute-start(bf16[128,1536]{1,0:T(8,128)(2,1)S(1)} %get-tuple-element.49), channel_id=1, source_target_pairs={{0,32},{32,64},{64,96},{96,0},{1,33},{33,65},{65,97},{97,1},{2,34}... | collective-permute-start | bytes 1179656 | tf_op jit(solution)/shard_map/ppermute | solution.py:38
  36.4 20.1 %collective-permute-start.2 = (bf16[128,1536]{1,0:T(8,128)(2,1)S(1)}, bf16[128,1536]{1,0:T(8,128)(2,1)S(1)}, u32[]{:S(2)}, u32[]{:S(2)}) collective-permute-start(bf16[128,1536]{1,0:T(8,128)(2,1)S(1)} %get-tuple-element.50), channel_id=1, source_target_pairs={{0,64},{32,96},{64,0},{96,32},{1,65},{33,97},{65,1},{97,33},{2,66}... | collective-permute-start | bytes 1179656 | tf_op jit(solution)/shard_map/ppermute | solution.py:38
  39.0 17.4 %collective-permute-start.3 = (bf16[128,1536]{1,0:T(8,128)(2,1)S(1)}, bf16[128,1536]{1,0:T(8,128)(2,1)S(1)}, u32[]{:S(2)}, u32[]{:S(2)}) collective-permute-start(bf16[128,1536]{1,0:T(8,128)(2,1)S(1)} %get-tuple-element.51), channel_id=1, source_target_pairs={{0,96},{32,0},{64,32},{96,64},{1,97},{33,1},{65,33},{97,65},{2,98}... | collective-permute-start | bytes 1179656 | tf_op jit(solution)/shard_map/ppermute | solution.py:38
  49.0 12.8 %collective-permute-start.6 = (bf16[64,1536]{1,0:T(8,128)(2,1)S(1)}, bf16[64,1536]{1,0:T(8,128)(2,1)S(1)}, u32[]{:S(2)}, u32[]{:S(2)}) collective-permute-start(bf16[64,1536]{1,0:T(8,128)(2,1)S(1)} %get-tuple-element.55), channel_id=1, source_target_pairs={{0,32},{32,64},{64,96},{96,0},{1,33},{33,65},{65,97},{97,1},{2,34}... | collective-permute-start | bytes 589832 | tf_op jit(solution)/shard_map/ppermute | solution.py:38
  50.4 14.5 %collective-permute-start.7 = (bf16[64,1536]{1,0:T(8,128)(2,1)S(1)}, bf16[64,1536]{1,0:T(8,128)(2,1)S(1)}, u32[]{:S(2)}, u32[]{:S(2)}) collective-permute-start(bf16[64,1536]{1,0:T(8,128)(2,1)S(1)} %get-tuple-element.62), channel_id=1, source_target_pairs={{0,64},{32,96},{64,0},{96,32},{1,65},{33,97},{65,1},{97,33},{2,66}... | collective-permute-start | bytes 589832 | tf_op jit(solution)/shard_map/ppermute | solution.py:38
  53.0 11.9 %collective-permute-start.8 = (bf16[64,1536]{1,0:T(8,128)(2,1)S(1)}, bf16[64,1536]{1,0:T(8,128)(2,1)S(1)}, u32[]{:S(2)}, u32[]{:S(2)}) collective-permute-start(bf16[64,1536]{1,0:T(8,128)(2,1)S(1)} %get-tuple-element.63), channel_id=1, source_target_pairs={{0,96},{32,0},{64,32},{96,64},{1,97},{33,1},{65,33},{97,65},{2,98}... | collective-permute-start | bytes 589832 | tf_op jit(solution)/shard_map/ppermute | solution.py:38
  56.7 9.7 %collective-permute-start.5 = (bf16[64,1536]{1,0:T(8,128)(2,1)S(1)}, bf16[64,1536]{1,0:T(8,128)(2,1)S(1)}, u32[]{:S(2)}, u32[]{:S(2)}) collective-permute-start(bf16[64,1536]{1,0:T(8,128)(2,1)S(1)} %get-tuple-element.60), channel_id=1, source_target_pairs={{0,16},{16,0},{1,17},{17,1},{2,18},{18,2},{3,19},{19,3},{4,20},{20... | collective-permute-start | bytes 589832 | tf_op jit(solution)/shard_map/ppermute | solution.py:42
  65.8 6.9 %collective-permute-start.9 = (bf16[64,1536]{1,0:T(8,128)(2,1)S(1)}, bf16[64,1536]{1,0:T(8,128)(2,1)S(1)}, u32[]{:S(2)}, u32[]{:S(2)}) collective-permute-start(bf16[64,1536]{1,0:T(8,128)(2,1)S(1)} %get-tuple-element.64), channel_id=1, source_target_pairs={{0,16},{16,0},{1,17},{17,1},{2,18},{18,2},{3,19},{19,3},{4,20},{20... | collective-permute-start | bytes 589832 | tf_op jit(solution)/shard_map/ppermute | solution.py:42
  67.3 7.8 %collective-permute-start.13 = (bf16[64,1536]{1,0:T(8,128)(2,1)S(1)}, bf16[64,1536]{1,0:T(8,128)(2,1)S(1)}, u32[]{:S(2)}, u32[]{:S(2)}) collective-permute-start(bf16[64,1536]{1,0:T(8,128)(2,1)S(1)} %get-tuple-element.68), channel_id=1, source_target_pairs={{0,96},{32,0},{64,32},{96,64},{1,97},{33,1},{65,33},{97,65},{2,98}... | collective-permute-start | bytes 589832 | tf_op jit(solution)/shard_map/ppermute | solution.py:38
  69.9 6.9 %collective-permute-start.14 = (bf16[64,1536]{1,0:T(8,128)(2,1)S(1)}, bf16[64,1536]{1,0:T(8,128)(2,1)S(1)}, u32[]{:S(2)}, u32[]{:S(2)}) collective-permute-start(bf16[64,1536]{1,0:T(8,128)(2,1)S(1)} %get-tuple-element.68), channel_id=1, source_target_pairs={{0,64},{32,96},{64,0},{96,32},{1,65},{33,97},{65,1},{97,33},{2,66}... | collective-permute-start | bytes 589832 | tf_op jit(solution)/shard_map/ppermute | solution.py:38
  70.0 12.0 %collective-permute-start.15 = (bf16[64,1536]{1,0:T(8,128)(2,1)S(1)}, bf16[64,1536]{1,0:T(8,128)(2,1)S(1)}, u32[]{:S(2)}, u32[]{:S(2)}) collective-permute-start(bf16[64,1536]{1,0:T(8,128)(2,1)S(1)} %get-tuple-element.68), channel_id=1, source_target_pairs={{0,32},{32,64},{64,96},{96,0},{1,33},{33,65},{65,97},{97,1},{2,34}... | collective-permute-start | bytes 589832 | tf_op jit(solution)/shard_map/ppermute | solution.py:38
  82.1 20.0 %collective-permute-start.16 = (bf16[256,1536]{1,0:T(8,128)(2,1)S(1)}, bf16[256,1536]{1,0:T(8,128)(2,1)S(1)}, u32[]{:S(2)}, u32[]{:S(2)}) collective-permute-start(bf16[256,1536]{1,0:T(8,128)(2,1)S(1)} %constant_dynamic-update-slice_fusion.4.refs_0_), channel_id=1, source_target_pairs={{0,16},{16,0},{1,17},{17,1},{2,18},{18,2},{3,19},{19,3},{4,20},{20... | collective-permute-start | bytes 2359304 | tf_op jit(solution)/shard_map/ppermute | solution.py:42
  84.7 21.8 %collective-permute-start.10 = (bf16[128,1536]{1,0:T(8,128)(2,1)S(1)}, bf16[128,1536]{1,0:T(8,128)(2,1)S(1)}, u32[]{:S(2)}, u32[]{:S(2)}) collective-permute-start(bf16[128,1536]{1,0:T(8,128)(2,1)S(1)} %constant_dynamic-update-slice_fusion.2.refs_0_), channel_id=1, source_target_pairs={{0,96},{32,0},{64,32},{96,64},{1,97},{33,1},{65,33},{97,65},{2,98}... | collective-permute-start | bytes 1179656 | tf_op jit(solution)/shard_map/ppermute | solution.py:38
  84.8 21.7 %collective-permute-start.11 = (bf16[128,1536]{1,0:T(8,128)(2,1)S(1)}, bf16[128,1536]{1,0:T(8,128)(2,1)S(1)}, u32[]{:S(2)}, u32[]{:S(2)}) collective-permute-start(bf16[128,1536]{1,0:T(8,128)(2,1)S(1)} %constant_dynamic-update-slice_fusion.2.refs_0_), channel_id=1, source_target_pairs={{0,64},{32,96},{64,0},{96,32},{1,65},{33,97},{65,1},{97,33},{2,66}... | collective-permute-start | bytes 1179656 | tf_op jit(solution)/shard_map/ppermute | solution.py:38
  84.9 21.6 %collective-permute-start.12 = (bf16[128,1536]{1,0:T(8,128)(2,1)S(1)}, bf16[128,1536]{1,0:T(8,128)(2,1)S(1)}, u32[]{:S(2)}, u32[]{:S(2)}) collective-permute-start(bf16[128,1536]{1,0:T(8,128)(2,1)S(1)} %constant_dynamic-update-slice_fusion.2.refs_0_), channel_id=1, source_target_pairs={{0,32},{32,64},{64,96},{96,0},{1,33},{33,65},{65,97},{97,1},{2,34}... | collective-permute-start | bytes 1179656 | tf_op jit(solution)/shard_map/ppermute | solution.py:38
  86.2 2.5 %copy-start.5 = (bf16[64,3072]{1,0:T(8,128)(2,1)}, bf16[64,3072]{1,0:T(8,128)(2,1)S(1)}, u32[]{:S(2)}) copy-start(bf16[64,3072]{1,0:T(8,128)(2,1)S(1)} %constant_dynamic-update-slice_fusion) | copy-start | bytes 1179652
  91.7 14.8 %copy-start = (bf16[1536,512]{1,0:T(8,128)(2,1)}, bf16[1536,512]{1,0:T(8,128)(2,1)S(1)}, u32[]{:S(2)}) copy-start(bf16[1536,512]{1,0:T(8,128)(2,1)S(1)} %turn_tokens.1.refs_0_) | copy-start | bytes 4718596
  105.3 1.2 copy-start.4
  109.0 0.9 copy-start.2
  109.9 5.0 %collective-permute-start.17 = (bf16[8,32,1536]{2,1,0:T(8,128)(2,1)S(1)}, bf16[8,32,1536]{2,1,0:T(8,128)(2,1)S(1)}, u32[]{:S(2)}, u32[]{:S(2)}) collective-permute-start(bf16[8,32,1536]{2,1,0:T(8,128)(2,1)S(1)} %get-tuple-element.79), channel_id=1, source_target_pairs={{0,1},{1,0},{2,3},{3,2},{4,5},{5,4},{6,7},{7,6},{8,9},{9,8},{10,11... | collective-permute-start | bytes 2359304 | tf_op jit(solution)/shard_map/ppermute | solution.py:46
  115.9 15.7 %all-to-all-start.1 = ((bf16[8,32,1536]{2,1,0:T(8,128)(2,1)}), bf16[8,32,1536]{2,1,0:T(8,128)(2,1)S(1)}, u32[]{:S(2)}, u32[]{:S(2)}) async-start(bf16[8,32,1536]{2,1,0:T(8,128)(2,1)} %chip_sum.1), calls=%async_computation.1 | async-start | bytes 1572864 | tf_op jit(solution)/shard_map/all_to_all | solution.py:493
  (1 other events, 0.9 us)

commit v4 on v3

--- a/solution.py
+++ b/solution.py
@@ -208,12 +208,10 @@
 
 def backward_first_kernel(pieces, *refs):
     grads = refs[: len(pieces)]
-    weight, out, full, held, sem = refs[len(pieces) :]
+    weight, out, held = refs[len(pieces) :]
     half = held.shape[0] // 2
     for core in range(2):
         assemble(grads, pieces, held.at[core * half : (core + 1) * half], core)
-    copy = pltpu.make_async_copy(held, full, sem)
-    copy.start()
 
     def body(i, carry):
         columns = pl.ds(pl.multiple_of(i * STEP, STEP), STEP)
@@ -221,7 +219,6 @@
         return carry
 
     lax.fori_loop(0, weight.shape[0] // STEP, body, 0)
-    copy.wait()
 
 
 def backward_first(grads, weight, pieces):
@@ -230,21 +227,19 @@
     return call(
         functools.partial(backward_first_kernel, pieces),
         "backward_first",
-        [((count, width), F32, ON_CHIP), ((count, hidden), BF16, IN_HBM)],
+        [((count, width), F32, ON_CHIP)],
         [ON_CHIP] * (len(grads) + 1),
         [*grads, weight],
         flops=2 * count * width * hidden,
         size=2 * width * hidden,
-        scratch=[pltpu.VMEM((count, hidden), BF16), pltpu.SemaphoreType.DMA(())],
-    )
+        scratch=[pltpu.VMEM((count, hidden), BF16)],
+    )[0]
 
 
 def backward_last_kernel(pieces, core, place, *refs):
     grads = refs[: len(pieces)]
-    weight, begun, out, full, held, sem = refs[len(pieces) :]
+    weight, begun, out, held = refs[len(pieces) :]
     assemble(grads, pieces, held, core)
-    copy = pltpu.make_async_copy(held, full, sem)
-    copy.start()
     rows = out.shape[1]
     half = slice(core * 2 * N_Y * rows, (core + 1) * 2 * N_Y * rows)
 
@@ -258,7 +253,6 @@
         return carry
 
     lax.fori_loop(0, weight.shape[0] // STEP, body, 0)
-    copy.wait()
 
 
 def backward_last(place, grads, weight, begun, pieces, core, name):
@@ -267,13 +261,13 @@
     return call(
         functools.partial(backward_last_kernel, pieces, core),
         name,
-        [((2 * N_Y, count // (2 * N_Y), width), BF16, ON_CHIP), ((count, hidden), BF16, IN_HBM)],
+        [((2 * N_Y, count // (2 * N_Y), width), BF16, ON_CHIP)],
         [SCALARS] + [ON_CHIP] * (len(grads) + 2),
         [place, *grads, weight, begun],
         flops=2 * count * width * hidden,
         size=2 * width * hidden,
-        scratch=[pltpu.VMEM((count, hidden), BF16), pltpu.SemaphoreType.DMA(())],
-    )
+        scratch=[pltpu.VMEM((count, hidden), BF16)],
+    )[0]
 
 
 def add_kernel(mine, got, out):
@@ -302,15 +296,25 @@
     )[0]
 
 
-def weight_grad_kernel(corners, *refs):
-    turned, *grads = refs[: len(corners) + 1]
-    out, held_turned, held, tiles, sems = refs[len(corners) + 1 :]
+def weight_grad_kernel(pieces, offsets, *refs):
+    turned, *grads = refs[: len(pieces) + 1]
+    out, held_turned, held, tiles, sems, load_sems = refs[len(pieces) + 1 :]
     step = tiles.shape[2]
     steps = held.shape[1] // step
-    loads = [pltpu.make_async_copy(turned, held_turned, sems.at[2])]
-    for i, (grad, (row, column)) in enumerate(zip(grads, corners)):
-        rows, columns = slice(row, row + grad.shape[0]), slice(column, column + grad.shape[1])
-        loads.append(pltpu.make_async_copy(grad, held.at[rows, columns], sems.at[3 + i]))
+    rows = held.shape[0] // (4 * N_Y)
+    loads = [pltpu.make_async_copy(turned, held_turned, load_sems.at[0])]
+    for grad, piece, offset in zip(grads, pieces, offsets):
+        columns = slice(offset, offset + grad.shape[1])
+        for slot, (distance, side) in enumerate(piece):
+            for core in range(2):
+                start, at = row_of(rows, core, distance, side), (2 * slot + core) * rows
+                loads.append(
+                    pltpu.make_async_copy(
+                        grad.at[at : at + rows, :],
+                        held.at[start : start + rows, columns],
+                        load_sems.at[len(loads)],
+                    )
+                )
     for load in loads:
         load.start()
     for load in loads:
@@ -338,10 +342,10 @@
     copy(steps - 1).wait()
 
 
-def weight_grad_of(turned, grads, corners, hidden):
+def weight_grad_of(turned, grads, pieces, offsets, hidden):
     width, rows = turned.shape
     return call(
-        functools.partial(weight_grad_kernel, corners),
+        functools.partial(weight_grad_kernel, pieces, offsets),
         "weight_grad",
         [((width, hidden), BF16, IN_HBM)],
         [ANYWHERE] * (1 + len(grads)),
@@ -352,7 +356,8 @@
             pltpu.VMEM(turned.shape, BF16),
             pltpu.VMEM((rows, hidden), BF16),
             pltpu.VMEM((2, width, STEP), BF16),
-            pltpu.SemaphoreType.DMA((3 + len(grads),)),
+            pltpu.SemaphoreType.DMA((2,)),
+            pltpu.SemaphoreType.DMA((1 + 2 * sum(len(piece) for piece in pieces),)),
         ],
         limit=56,
     )[0]
@@ -461,26 +466,25 @@
     got_far = across(far)
 
     act_b, grad_b = gelu_step(place, [kept, *got_b], cotangent, cut, "gelu_b")
-    grad_b_far = across(grad_b)
+    by_y = [grad_b] + [ahead(grad_b, -d) for d in (1, 2, 3)]
+    by_y_far = [across(grad) for grad in by_y]
     got_far = after(got_far, grad_b)
     act_a, grad_a = gelu_step(place, [near, got_far], cotangent, 0, "gelu_a")
-    by_y = [ahead(grad_a, -d) for d in (1, 2, 3)]
-    both = jnp.concatenate([grad_b, grad_b_far], axis=0)
-    wide = [ahead(both, -d) for d in (1, 2, 3)]
-    by_y = jnp.concatenate([grad_a] + after(by_y, both), axis=0)
-    by_y_far = across(by_y)
-    late, toks = after((weight, toks), by_y)
+    both = jnp.concatenate([grad_a, across(grad_a)], axis=0)
+    wide = [both] + [ahead(both, -d) for d in (1, 2, 3)]
+    late, toks = after((weight, toks), both)
     held_a, held_b = load(late, part_a, "load_a"), load(late, part_b, "load_b")
     turned = turn(toks)
     activated = jnp.concatenate([act_a, act_b], axis=1)
 
-    by_y_far = after(by_y_far, held_a, held_b, turned, activated)
-    begun, full_a = backward_first([by_y, by_y_far], held_a, BY_SIDE)
-    wide = [both, *after(wide, begun)]
-    theirs, full_theirs = backward_last(place, wide, held_b, begun, BY_DISTANCE, 1, "backward_other")
+    grads_b = [*by_y, *by_y_far]
+    pieces_b = tuple(((d, s),) for s in range(2) for d in range(N_Y))
+    begun = backward_first(after(grads_b, held_a, held_b, turned, activated), held_b, pieces_b)
+    wide_last = after(wide, begun)
+    theirs = backward_last(place, wide_last, held_a, begun, BY_DISTANCE, 1, "backward_other")
     arrived = other_core(theirs)
-    wide = after(wide, theirs)
-    mine, full_mine = backward_last(place, wide, held_b, begun, BY_DISTANCE, 0, "backward_own")
+    wide_last = after(wide_last, theirs)
+    mine = backward_last(place, wide_last, held_a, begun, BY_DISTANCE, 0, "backward_own")
     (chip,) = call(
         add_kernel,
         "chip_sum",
@@ -491,9 +495,9 @@
         size=6 * mine.size,
     )
     last = lax.all_to_all(chip, PLANE, 0, 0, tiled=True)
-    full_mine = after(full_mine, chip)
-    corners = [(0, 0), (0, cut), (8 * rows, cut)]
-    weight_grad = weight_grad_of(turned, [full_a, full_mine, full_theirs], corners, hidden)
+    grads = after([*grads_b, *wide], chip)
+    offsets = [cut] * len(grads_b) + [0] * len(wide)
+    weight_grad = weight_grad_of(turned, grads, pieces_b + BY_DISTANCE, offsets, hidden)
     (input_grad,) = call(
         last_sum_kernel,
         "last_sum",

time: 133 us -> 125 us (0.940)
  waiting for transfers between devices: 43 us -> 30.7 us
  starting transfers between devices: 28.6 us -> 35.4 us
  local copies, waits for them, and re-layouts: 4.02 us -> 2.41 us
    ppermute x4 -> x7, waiting for transfers between devices: 21.2 us -> 8.82 us  [across(): return lax.ppermute(array, 'xh', SWAP)]
    ppermute x4 -> x7, starting transfers between devices: 6.23 us -> 11.3 us  [across(): return lax.ppermute(array, 'xh', SWAP)]
    unnamed x17 -> x30, local copies, waits for them, and re-layouts: 3.03 us -> 0.76 us
    ppermute x12, starting transfers between devices: 14.9 us -> 17.1 us  [ahead(): lax.ppermute(array, 'y', [(i, (i + distance) % N_Y) for i in range(N_Y)])]
  transfers between devices with their start and end apart: 19 -> 22, of which waited for: 10 -> 9; matrix products, arithmetic and copies ran while one was open for 0% -> 1% of each run, Pallas kernels for 23% -> 23%
where the time goes in v4:
time: 125 us
  Pallas kernels  37.5 us (30%)
  starting transfers between devices  35.4 us (28%)
  waiting for transfers between devices  30.7 us (25%)
  blocking collectives  18.1 us (14%)
  local copies, waits for them, and re-layouts  2.41 us (2%)
    pallas_call x16, Pallas kernels, call(): pl.pallas_call(kernel, out_shape=[jax.ShapeDtypeStruct(shape, dtype) for...  37.5 us
    ppermute x12, waiting for transfers between devices, ahead(): lax.ppermute(array, 'y', [(i, (i + distance) % N_Y) for i in range(N_Y)])  19.7 us
    all_to_all x1, blocking collectives, local(): own = lax.all_to_all(spread, PLANE, 0, 0, tiled=True)  18.1 us
    ppermute x12, starting transfers between devices, ahead(): lax.ppermute(array, 'y', [(i, (i + distance) % N_Y) for i in range(N_Y)])  17.1 us
    ppermute x7, starting transfers between devices, across(): return lax.ppermute(array, 'xh', SWAP)  11.3 us
    ppermute x7, waiting for transfers between devices, across(): return lax.ppermute(array, 'xh', SWAP)  8.82 us
    all_to_all x1, starting transfers between devices, local(): last = lax.all_to_all(chip, PLANE, 0, 0, tiled=True)  3.55 us
    ppermute x2, starting transfers between devices, other_core(): return lax.ppermute(array, 'c', SWAP)  3.42 us
  transfers between devices with their start and end apart: 22, of which 9 were waited for; matrix products, arithmetic and copies ran while one was open for 1% of the time, Pallas kernels for 23%

profile of v4, /device:TPU:1, one launch (start us, length us, event | category | flops | bytes accessed | tf_op | source)
XLA Modules:
  0.0 125.1 jit_solution(8414352821229657764)
XLA Ops:
  1.6 18.1 %all_to_all.10.own = bf16[8,32,1536]{2,1,0:T(8,128)(2,1)S(1)} all-to-all(bf16[8,32,1536]{2,1,0:T(8,128)(2,1)S(1)} %broadcast_in_dim.2), channel_id=1, replica_groups=mesh['y'=4,'xh'=2,'xl'=2,'z'=4,'c'=2] {'xl','z'}, dimensions={0} | all-to-all | bytes 1572864 | tf_op jit(solution)/shard_map/all_to_all | solution.py:437
  19.7 2.4 %collective-permute-start = (bf16[8,32,1536]{2,1,0:T(8,128)(2,1)S(1)}, bf16[8,32,1536]{2,1,0:T(8,128)(2,1)S(1)}, u32[]{:S(2)}, u32[]{:S(2)}) collective-permute-start(bf16[8,32,1536]{2,1,0:T(8,128)(2,1)S(1)} %all_to_all.10.own), channel_id=1, source_target_pairs={{0,1},{1,0},{2,3},{3,2},{4,5},{5,4},{6,7},{7,6},{8,9},{9,8},{10,11... | collective-permute-start | bytes 2359304 | tf_op jit(solution)/shard_map/ppermute | solution.py:46
  22.1 2.3 %load_forward.1.weight = bf16[1536,1536]{1,0:T(8,128)(2,1)S(1)} custom-call(bf16[1536,3072]{1,0:T(8,128)(2,1)} %source.2), custom_call_target="tpu_custom_call" | custom-call | bytes 9437184 | tf_op jit(solution)/shard_map/load_forward/pallas_call | solution.py:62
  24.5 3.6 %forward_side.1 = (bf16[512,1536]{1,0:T(8,128)(2,1)S(1)}, bf16[256,1536]{1,0:T(8,128)(2,1)S(1)}, bf16[256,1536]{1,0:T(8,128)(2,1)S(1)}) custom-call(s32[3]{0:T(128)S(1)} %pad_add_fusion.place, bf16[8,32,1536]{2,1,0:T(8,128)(2,1)S(1)} %all_to_all.10.own, bf16[8,32,1536]{2,1,0:T(8,128)(2,1)S(1)} %collective-permute-done.other, ...), custom_call_target="tpu_custom_call" | custom-call | flops 2415919104 | bytes 4718592 | tf_op jit(solution)/shard_map/forward_side/pallas_call | solution.py:62
  28.1 2.5 %collective-permute-start.4 = (bf16[256,1536]{1,0:T(8,128)(2,1)S(1)}, bf16[256,1536]{1,0:T(8,128)(2,1)S(1)}, u32[]{:S(2)}, u32[]{:S(2)}) collective-permute-start(bf16[256,1536]{1,0:T(8,128)(2,1)S(1)} %get-tuple-element.63), channel_id=1, source_target_pairs={{0,16},{16,0},{1,17},{17,1},{2,18},{18,2},{3,19},{19,3},{4,20},{20... | collective-permute-start | bytes 2359304 | tf_op jit(solution)/shard_map/ppermute | solution.py:42
  30.6 4.4 %forward_distance.1 = (bf16[128,1536]{1,0:T(8,128)(2,1)S(1)}, bf16[128,1536]{1,0:T(8,128)(2,1)S(1)}, bf16[128,1536]{1,0:T(8,128)(2,1)S(1)}, bf16[128,1536]{1,0:T(8,128)(2,1)S(1)}) custom-call(bf16[512,1536]{1,0:T(8,128)(2,1)S(1)} %get-tuple-element.80.toks.tok, bf16[1536,3072]{1,0:T(8,128)(2,1)} %source.2), custom_call_target="tpu_custom_call" | custom-call | flops 2415919104 | bytes 4718592 | tf_op jit(solution)/shard_map/forward_distance/pallas_call | solution.py:62
  36.4 2.6 %collective-permute-start.2 = (bf16[128,1536]{1,0:T(8,128)(2,1)S(1)}, bf16[128,1536]{1,0:T(8,128)(2,1)S(1)}, u32[]{:S(2)}, u32[]{:S(2)}) collective-permute-start(bf16[128,1536]{1,0:T(8,128)(2,1)S(1)} %get-tuple-element.60), channel_id=1, source_target_pairs={{0,64},{32,96},{64,0},{96,32},{1,65},{33,97},{65,1},{97,33},{2,66}... | collective-permute-start | bytes 1179656 | tf_op jit(solution)/shard_map/ppermute | solution.py:38
  40.1 8.7 %collective-permute-done.4.got = bf16[256,1536]{1,0:T(8,128)(2,1)S(1)} collective-permute-done((bf16[256,1536]{1,0:T(8,128)(2,1)S(1)}, bf16[256,1536]{1,0:T(8,128)(2,1)S(1)}, u32[]{:S(2)}, u32[]{:S(2)}) %collective-permute-start.4) | collective-permute-done | bytes 786464 | tf_op jit(solution)/shard_map/ppermute | solution.py:42
  50.4 2.6 %collective-permute-start.7 = (bf16[64,1536]{1,0:T(8,128)(2,1)S(1)}, bf16[64,1536]{1,0:T(8,128)(2,1)S(1)}, u32[]{:S(2)}, u32[]{:S(2)}) collective-permute-start(bf16[64,1536]{1,0:T(8,128)(2,1)S(1)} %get-tuple-element.72), channel_id=1, source_target_pairs={{0,64},{32,96},{64,0},{96,32},{1,65},{33,97},{65,1},{97,33},{2,66}... | collective-permute-start | bytes 589832 | tf_op jit(solution)/shard_map/ppermute | solution.py:38
  54.1 2.4 %collective-permute-done.2.got_2 = bf16[128,1536]{1,0:T(8,128)(2,1)S(1)} collective-permute-done((bf16[128,1536]{1,0:T(8,128)(2,1)S(1)}, bf16[128,1536]{1,0:T(8,128)(2,1)S(1)}, u32[]{:S(2)}, u32[]{:S(2)}) %collective-permute-start.2) | collective-permute-done | bytes 393248 | tf_op jit(solution)/shard_map/ppermute | solution.py:38
  57.2 4.6 %collective-permute-done.6.refs_1_ = bf16[64,1536]{1,0:T(8,128)(2,1)S(1)} collective-permute-done((bf16[64,1536]{1,0:T(8,128)(2,1)S(1)}, bf16[64,1536]{1,0:T(8,128)(2,1)S(1)}, u32[]{:S(2)}, u32[]{:S(2)}) %collective-permute-start.6) | collective-permute-done | bytes 196640 | tf_op jit(solution)/shard_map/ppermute | solution.py:38
  61.8 3.1 %collective-permute-done.7.refs_2_ = bf16[64,1536]{1,0:T(8,128)(2,1)S(1)} collective-permute-done((bf16[64,1536]{1,0:T(8,128)(2,1)S(1)}, bf16[64,1536]{1,0:T(8,128)(2,1)S(1)}, u32[]{:S(2)}, u32[]{:S(2)}) %collective-permute-start.7) | collective-permute-done | bytes 196640 | tf_op jit(solution)/shard_map/ppermute | solution.py:38
  67.3 2.5 %collective-permute-start.13 = (bf16[64,1536]{1,0:T(8,128)(2,1)S(1)}, bf16[64,1536]{1,0:T(8,128)(2,1)S(1)}, u32[]{:S(2)}, u32[]{:S(2)}) collective-permute-start(bf16[64,1536]{1,0:T(8,128)(2,1)S(1)} %get-tuple-element.97.refs_0_.refs_1_), channel_id=1, source_target_pairs={{0,96},{32,0},{64,32},{96,64},{1,97},{33,1},{65,33},{97,65},{2,98}... | collective-permute-start | bytes 589832 | tf_op jit(solution)/shard_map/ppermute | solution.py:38
  70.4 2.4 %collective-permute-start.16 = (bf16[64,1536]{1,0:T(8,128)(2,1)S(1)}, bf16[64,1536]{1,0:T(8,128)(2,1)S(1)}, u32[]{:S(2)}, u32[]{:S(2)}) collective-permute-start(bf16[64,1536]{1,0:T(8,128)(2,1)S(1)} %get-tuple-element.97.refs_0_.refs_1_), channel_id=1, source_target_pairs={{0,16},{16,0},{1,17},{17,1},{2,18},{18,2},{3,19},{19,3},{4,20},{20... | collective-permute-start | bytes 589832 | tf_op jit(solution)/shard_map/ppermute | solution.py:42
  77.3 3.9 %collective-permute-start.10 = (bf16[128,1536]{1,0:T(8,128)(2,1)S(1)}, bf16[128,1536]{1,0:T(8,128)(2,1)S(1)}, u32[]{:S(2)}, u32[]{:S(2)}) collective-permute-start(bf16[128,1536]{1,0:T(8,128)(2,1)S(1)} %constant_dynamic-update-slice_fusion.2.refs_0_.refs_9_), channel_id=1, source_target_pairs={{0,96},{32,0},{64,32},{96,64},{1,97},{33,1},{65,33},{97,65},{2,98}... | collective-permute-start | bytes 1179656 | tf_op jit(solution)/shard_map/ppermute | solution.py:38
  82.0 2.8 %collective-permute-start.18 = (bf16[64,1536]{1,0:T(8,128)(2,1)S(1)}, bf16[64,1536]{1,0:T(8,128)(2,1)S(1)}, u32[]{:S(2)}, u32[]{:S(2)}) collective-permute-start(bf16[64,1536]{1,0:T(8,128)(2,1)S(1)} %collective-permute-done.14.refs_2_.refs_3_), channel_id=1, source_target_pairs={{0,16},{16,0},{1,17},{17,1},{2,18},{18,2},{3,19},{19,3},{4,20},{20... | collective-permute-start | bytes 589832 | tf_op jit(solution)/shard_map/ppermute | solution.py:42
  85.7 2.3 %load_a.1.refs_4_ = bf16[1536,1536]{1,0:T(8,128)(2,1)S(1)} custom-call(bf16[1536,3072]{1,0:T(8,128)(2,1)} %source.2), custom_call_target="tpu_custom_call" | custom-call | bytes 9437184 | tf_op jit(solution)/shard_map/load_a/pallas_call | solution.py:62
  88.1 2.3 %load_b.1.refs_8_ = bf16[1536,1536]{1,0:T(8,128)(2,1)S(1)} custom-call(bf16[1536,3072]{1,0:T(8,128)(2,1)} %source.2), custom_call_target="tpu_custom_call" | custom-call | bytes 9437184 | tf_op jit(solution)/shard_map/load_b/pallas_call | solution.py:62
  91.2 3.1 %backward_first.1.refs_5_ = f32[512,1536]{1,0:T(8,128)S(1)} custom-call(bf16[64,1536]{1,0:T(8,128)(2,1)S(1)} %get-tuple-element.97.refs_0_.refs_1_, bf16[64,1536]{1,0:T(8,128)(2,1)S(1)} %collective-permute-done.13.refs_1_.refs_2_, bf16[64,1536]{1,0:T(8,128)(2,1)S(1)} %collective-permute-done.14.refs_2_.refs_3_, ...), custom_call_target="tpu_custom_call" | custom-call | flops 2415919104 | bytes 4718592 | tf_op jit(solution)/shard_map/backward_first/pallas_call | solution.py:62
  94.4 7.3 %collective-permute-done.12.refs_3_.refs_12_ = bf16[128,1536]{1,0:T(8,128)(2,1)S(1)} collective-permute-done((bf16[128,1536]{1,0:T(8,128)(2,1)S(1)}, bf16[128,1536]{1,0:T(8,128)(2,1)S(1)}, u32[]{:S(2)}, u32[]{:S(2)}) %collective-permute-start.12) | collective-permute-done | bytes 393248 | tf_op jit(solution)/shard_map/ppermute | solution.py:38
  101.7 2.4 %backward_other.1 = bf16[8,32,1536]{2,1,0:T(8,128)(2,1)S(1)} custom-call(s32[3]{0:T(128)S(1)} %pad_add_fusion.place, bf16[128,1536]{1,0:T(8,128)(2,1)S(1)} %constant_dynamic-update-slice_fusion.2.refs_0_.refs_9_, bf16[128,1536]{1,0:T(8,128)(2,1)S(1)} %collective-permute-done.10.refs_1_.refs_10_, ...), custom_call_target="tpu_custom_call" | custom-call | flops 1207959552 | bytes 4718592 | tf_op jit(solution)/shard_map/backward_other/pallas_call | solution.py:62
  105.2 2.4 %backward_own.1.mine = bf16[8,32,1536]{2,1,0:T(8,128)(2,1)S(1)} custom-call(s32[3]{0:T(128)S(1)} %pad_add_fusion.place, bf16[128,1536]{1,0:T(8,128)(2,1)S(1)} %constant_dynamic-update-slice_fusion.2.refs_0_.refs_9_, bf16[128,1536]{1,0:T(8,128)(2,1)S(1)} %collective-permute-done.10.refs_1_.refs_10_, ...), custom_call_target="tpu_custom_call" | custom-call | flops 1207959552 | bytes 4718592 | tf_op jit(solution)/shard_map/backward_own/pallas_call | solution.py:62
  108.7 3.5 %all-to-all-start.1 = ((bf16[8,32,1536]{2,1,0:T(8,128)(2,1)}), bf16[8,32,1536]{2,1,0:T(8,128)(2,1)S(1)}, u32[]{:S(2)}, u32[]{:S(2)}) async-start(bf16[8,32,1536]{2,1,0:T(8,128)(2,1)} %chip_sum.1), calls=%async_computation.1 | async-start | bytes 1572864 | tf_op jit(solution)/shard_map/all_to_all | solution.py:497
  112.2 10.0 %weight_grad.1 = bf16[1536,3072]{1,0:T(8,128)(2,1)} custom-call(bf16[1536,512]{1,0:T(8,128)(2,1)} %copy-done.4, bf16[64,1536]{1,0:T(8,128)(2,1)} %copy-done.6, bf16[64,1536]{1,0:T(8,128)(2,1)} %copy-done.7, bf16[64,1536]{1,0:T(8,128)(2,1)} %copy-done.8, bf16[64,1536]{1,0:T(8,128)(2,1)} %copy-done.9, bf16[64,1536]{1,0:T(8,128)(2,1)} %copy-done.10, ...), custom_call_target="tpu_custom_call" | custom-call | flops 4831838208 | bytes 9437184 | tf_op jit(solution)/shard_map/weight_grad/pallas_call | solution.py:62
  (71 shorter events, 21.6 us)
Async XLA Ops:
  19.7 4.8 %collective-permute-start = (bf16[8,32,1536]{2,1,0:T(8,128)(2,1)S(1)}, bf16[8,32,1536]{2,1,0:T(8,128)(2,1)S(1)}, u32[]{:S(2)}, u32[]{:S(2)}) collective-permute-start(bf16[8,32,1536]{2,1,0:T(8,128)(2,1)S(1)} %all_to_all.10.own), channel_id=1, source_target_pairs={{0,1},{1,0},{2,3},{3,2},{4,5},{5,4},{6,7},{7,6},{8,9},{9,8},{10,11... | collective-permute-start | bytes 2359304 | tf_op jit(solution)/shard_map/ppermute | solution.py:46
  28.1 20.8 %collective-permute-start.4 = (bf16[256,1536]{1,0:T(8,128)(2,1)S(1)}, bf16[256,1536]{1,0:T(8,128)(2,1)S(1)}, u32[]{:S(2)}, u32[]{:S(2)}) collective-permute-start(bf16[256,1536]{1,0:T(8,128)(2,1)S(1)} %get-tuple-element.63), channel_id=1, source_target_pairs={{0,16},{16,0},{1,17},{17,1},{2,18},{18,2},{3,19},{19,3},{4,20},{20... | collective-permute-start | bytes 2359304 | tf_op jit(solution)/shard_map/ppermute | solution.py:42
  30.6 34.3 %copy-start.5 = (bf16[64,3072]{1,0:T(8,128)(2,1)S(1)}, bf16[64,3072]{1,0:T(8,128)(2,1)}, u32[]{:S(2)}) copy-start(bf16[64,3072]{1,0:T(8,128)(2,1)} %refs_2_.1) | copy-start | bytes 1179652
  35.0 18.0 %collective-permute-start.1 = (bf16[128,1536]{1,0:T(8,128)(2,1)S(1)}, bf16[128,1536]{1,0:T(8,128)(2,1)S(1)}, u32[]{:S(2)}, u32[]{:S(2)}) collective-permute-start(bf16[128,1536]{1,0:T(8,128)(2,1)S(1)} %get-tuple-element.59), channel_id=1, source_target_pairs={{0,32},{32,64},{64,96},{96,0},{1,33},{33,65},{65,97},{97,1},{2,34}... | collective-permute-start | bytes 1179656 | tf_op jit(solution)/shard_map/ppermute | solution.py:38
  36.4 20.1 %collective-permute-start.2 = (bf16[128,1536]{1,0:T(8,128)(2,1)S(1)}, bf16[128,1536]{1,0:T(8,128)(2,1)S(1)}, u32[]{:S(2)}, u32[]{:S(2)}) collective-permute-start(bf16[128,1536]{1,0:T(8,128)(2,1)S(1)} %get-tuple-element.60), channel_id=1, source_target_pairs={{0,64},{32,96},{64,0},{96,32},{1,65},{33,97},{65,1},{97,33},{2,66}... | collective-permute-start | bytes 1179656 | tf_op jit(solution)/shard_map/ppermute | solution.py:38
  39.0 17.4 %collective-permute-start.3 = (bf16[128,1536]{1,0:T(8,128)(2,1)S(1)}, bf16[128,1536]{1,0:T(8,128)(2,1)S(1)}, u32[]{:S(2)}, u32[]{:S(2)}) collective-permute-start(bf16[128,1536]{1,0:T(8,128)(2,1)S(1)} %get-tuple-element.61), channel_id=1, source_target_pairs={{0,96},{32,0},{64,32},{96,64},{1,97},{33,1},{65,33},{97,65},{2,98}... | collective-permute-start | bytes 1179656 | tf_op jit(solution)/shard_map/ppermute | solution.py:38
  49.0 12.8 %collective-permute-start.6 = (bf16[64,1536]{1,0:T(8,128)(2,1)S(1)}, bf16[64,1536]{1,0:T(8,128)(2,1)S(1)}, u32[]{:S(2)}, u32[]{:S(2)}) collective-permute-start(bf16[64,1536]{1,0:T(8,128)(2,1)S(1)} %get-tuple-element.65), channel_id=1, source_target_pairs={{0,32},{32,64},{64,96},{96,0},{1,33},{33,65},{65,97},{97,1},{2,34}... | collective-permute-start | bytes 589832 | tf_op jit(solution)/shard_map/ppermute | solution.py:38
  50.4 14.5 %collective-permute-start.7 = (bf16[64,1536]{1,0:T(8,128)(2,1)S(1)}, bf16[64,1536]{1,0:T(8,128)(2,1)S(1)}, u32[]{:S(2)}, u32[]{:S(2)}) collective-permute-start(bf16[64,1536]{1,0:T(8,128)(2,1)S(1)} %get-tuple-element.72), channel_id=1, source_target_pairs={{0,64},{32,96},{64,0},{96,32},{1,65},{33,97},{65,1},{97,33},{2,66}... | collective-permute-start | bytes 589832 | tf_op jit(solution)/shard_map/ppermute | solution.py:38
  53.0 11.9 %collective-permute-start.8 = (bf16[64,1536]{1,0:T(8,128)(2,1)S(1)}, bf16[64,1536]{1,0:T(8,128)(2,1)S(1)}, u32[]{:S(2)}, u32[]{:S(2)}) collective-permute-start(bf16[64,1536]{1,0:T(8,128)(2,1)S(1)} %get-tuple-element.73), channel_id=1, source_target_pairs={{0,96},{32,0},{64,32},{96,64},{1,97},{33,1},{65,33},{97,65},{2,98}... | collective-permute-start | bytes 589832 | tf_op jit(solution)/shard_map/ppermute | solution.py:38
  56.7 9.2 %collective-permute-start.5 = (bf16[64,1536]{1,0:T(8,128)(2,1)S(1)}, bf16[64,1536]{1,0:T(8,128)(2,1)S(1)}, u32[]{:S(2)}, u32[]{:S(2)}) collective-permute-start(bf16[64,1536]{1,0:T(8,128)(2,1)S(1)} %get-tuple-element.70), channel_id=1, source_target_pairs={{0,16},{16,0},{1,17},{17,1},{2,18},{18,2},{3,19},{19,3},{4,20},{20... | collective-permute-start | bytes 589832 | tf_op jit(solution)/shard_map/ppermute | solution.py:42
  66.7 10.5 %collective-permute-start.9 = (bf16[64,1536]{1,0:T(8,128)(2,1)S(1)}, bf16[64,1536]{1,0:T(8,128)(2,1)S(1)}, u32[]{:S(2)}, u32[]{:S(2)}) collective-permute-start(bf16[64,1536]{1,0:T(8,128)(2,1)S(1)} %get-tuple-element.78), channel_id=1, source_target_pairs={{0,16},{16,0},{1,17},{17,1},{2,18},{18,2},{3,19},{19,3},{4,20},{20... | collective-permute-start | bytes 589832 | tf_op jit(solution)/shard_map/ppermute | solution.py:42
  67.3 7.7 %collective-permute-start.13 = (bf16[64,1536]{1,0:T(8,128)(2,1)S(1)}, bf16[64,1536]{1,0:T(8,128)(2,1)S(1)}, u32[]{:S(2)}, u32[]{:S(2)}) collective-permute-start(bf16[64,1536]{1,0:T(8,128)(2,1)S(1)} %get-tuple-element.97.refs_0_.refs_1_), channel_id=1, source_target_pairs={{0,96},{32,0},{64,32},{96,64},{1,97},{33,1},{65,33},{97,65},{2,98}... | collective-permute-start | bytes 589832 | tf_op jit(solution)/shard_map/ppermute | solution.py:38
  69.8 11.4 %collective-permute-start.14 = (bf16[64,1536]{1,0:T(8,128)(2,1)S(1)}, bf16[64,1536]{1,0:T(8,128)(2,1)S(1)}, u32[]{:S(2)}, u32[]{:S(2)}) collective-permute-start(bf16[64,1536]{1,0:T(8,128)(2,1)S(1)} %get-tuple-element.97.refs_0_.refs_1_), channel_id=1, source_target_pairs={{0,64},{32,96},{64,0},{96,32},{1,65},{33,97},{65,1},{97,33},{2,66}... | collective-permute-start | bytes 589832 | tf_op jit(solution)/shard_map/ppermute | solution.py:38
  69.9 12.0 %collective-permute-start.15 = (bf16[64,1536]{1,0:T(8,128)(2,1)S(1)}, bf16[64,1536]{1,0:T(8,128)(2,1)S(1)}, u32[]{:S(2)}, u32[]{:S(2)}) collective-permute-start(bf16[64,1536]{1,0:T(8,128)(2,1)S(1)} %get-tuple-element.97.refs_0_.refs_1_), channel_id=1, source_target_pairs={{0,32},{32,64},{64,96},{96,0},{1,33},{33,65},{65,97},{97,1},{2,34}... | collective-permute-start | bytes 589832 | tf_op jit(solution)/shard_map/ppermute | solution.py:38
  70.4 11.6 %collective-permute-start.16 = (bf16[64,1536]{1,0:T(8,128)(2,1)S(1)}, bf16[64,1536]{1,0:T(8,128)(2,1)S(1)}, u32[]{:S(2)}, u32[]{:S(2)}) collective-permute-start(bf16[64,1536]{1,0:T(8,128)(2,1)S(1)} %get-tuple-element.97.refs_0_.refs_1_), channel_id=1, source_target_pairs={{0,16},{16,0},{1,17},{17,1},{2,18},{18,2},{3,19},{19,3},{4,20},{20... | collective-permute-start | bytes 589832 | tf_op jit(solution)/shard_map/ppermute | solution.py:42
  75.0 9.8 %collective-permute-start.17 = (bf16[64,1536]{1,0:T(8,128)(2,1)S(1)}, bf16[64,1536]{1,0:T(8,128)(2,1)S(1)}, u32[]{:S(2)}, u32[]{:S(2)}) collective-permute-start(bf16[64,1536]{1,0:T(8,128)(2,1)S(1)} %collective-permute-done.13.refs_1_.refs_2_), channel_id=1, source_target_pairs={{0,16},{16,0},{1,17},{17,1},{2,18},{18,2},{3,19},{19,3},{4,20},{20... | collective-permute-start | bytes 589832 | tf_op jit(solution)/shard_map/ppermute | solution.py:42
  77.3 27.9 %copy-start = (bf16[128,1536]{1,0:T(8,128)(2,1)}, bf16[128,1536]{1,0:T(8,128)(2,1)S(1)}, u32[]{:S(2)}) copy-start(bf16[128,1536]{1,0:T(8,128)(2,1)S(1)} %constant_dynamic-update-slice_fusion.2.refs_0_.refs_9_) | copy-start | bytes 1179652
  77.3 17.1 %collective-permute-start.10 = (bf16[128,1536]{1,0:T(8,128)(2,1)S(1)}, bf16[128,1536]{1,0:T(8,128)(2,1)S(1)}, u32[]{:S(2)}, u32[]{:S(2)}) collective-permute-start(bf16[128,1536]{1,0:T(8,128)(2,1)S(1)} %constant_dynamic-update-slice_fusion.2.refs_0_.refs_9_), channel_id=1, source_target_pairs={{0,96},{32,0},{64,32},{96,64},{1,97},{33,1},{65,33},{97,65},{2,98}... | collective-permute-start | bytes 1179656 | tf_op jit(solution)/shard_map/ppermute | solution.py:38
  81.2 13.2 %collective-permute-start.11 = (bf16[128,1536]{1,0:T(8,128)(2,1)S(1)}, bf16[128,1536]{1,0:T(8,128)(2,1)S(1)}, u32[]{:S(2)}, u32[]{:S(2)}) collective-permute-start(bf16[128,1536]{1,0:T(8,128)(2,1)S(1)} %constant_dynamic-update-slice_fusion.2.refs_0_.refs_9_), channel_id=1, source_target_pairs={{0,64},{32,96},{64,0},{96,32},{1,65},{33,97},{65,1},{97,33},{2,66}... | collective-permute-start | bytes 1179656 | tf_op jit(solution)/shard_map/ppermute | solution.py:38
  82.0 19.8 %collective-permute-start.12 = (bf16[128,1536]{1,0:T(8,128)(2,1)S(1)}, bf16[128,1536]{1,0:T(8,128)(2,1)S(1)}, u32[]{:S(2)}, u32[]{:S(2)}) collective-permute-start(bf16[128,1536]{1,0:T(8,128)(2,1)S(1)} %constant_dynamic-update-slice_fusion.2.refs_0_.refs_9_), channel_id=1, source_target_pairs={{0,32},{32,64},{64,96},{96,0},{1,33},{33,65},{65,97},{97,1},{2,34}... | collective-permute-start | bytes 1179656 | tf_op jit(solution)/shard_map/ppermute | solution.py:38
  82.0 9.1 %collective-permute-start.18 = (bf16[64,1536]{1,0:T(8,128)(2,1)S(1)}, bf16[64,1536]{1,0:T(8,128)(2,1)S(1)}, u32[]{:S(2)}, u32[]{:S(2)}) collective-permute-start(bf16[64,1536]{1,0:T(8,128)(2,1)S(1)} %collective-permute-done.14.refs_2_.refs_3_), channel_id=1, source_target_pairs={{0,16},{16,0},{1,17},{17,1},{2,18},{18,2},{3,19},{19,3},{4,20},{20... | collective-permute-start | bytes 589832 | tf_op jit(solution)/shard_map/ppermute | solution.py:42
  84.8 6.3 %collective-permute-start.19 = (bf16[64,1536]{1,0:T(8,128)(2,1)S(1)}, bf16[64,1536]{1,0:T(8,128)(2,1)S(1)}, u32[]{:S(2)}, u32[]{:S(2)}) collective-permute-start(bf16[64,1536]{1,0:T(8,128)(2,1)S(1)} %collective-permute-done.15.refs_3_.refs_4_), channel_id=1, source_target_pairs={{0,16},{16,0},{1,17},{17,1},{2,18},{18,2},{3,19},{19,3},{4,20},{20... | collective-permute-start | bytes 589832 | tf_op jit(solution)/shard_map/ppermute | solution.py:42
  104.1 3.4 %collective-permute-start.20 = (bf16[8,32,1536]{2,1,0:T(8,128)(2,1)S(1)}, bf16[8,32,1536]{2,1,0:T(8,128)(2,1)S(1)}, u32[]{:S(2)}, u32[]{:S(2)}) collective-permute-start(bf16[8,32,1536]{2,1,0:T(8,128)(2,1)S(1)} %backward_other.1), channel_id=1, source_target_pairs={{0,1},{1,0},{2,3},{3,2},{4,5},{5,4},{6,7},{7,6},{8,9},{9,8},{10,11... | collective-permute-start | bytes 2359304 | tf_op jit(solution)/shard_map/ppermute | solution.py:46
  108.7 15.7 %all-to-all-start.1 = ((bf16[8,32,1536]{2,1,0:T(8,128)(2,1)}), bf16[8,32,1536]{2,1,0:T(8,128)(2,1)S(1)}, u32[]{:S(2)}, u32[]{:S(2)}) async-start(bf16[8,32,1536]{2,1,0:T(8,128)(2,1)} %chip_sum.1), calls=%async_computation.1 | async-start | bytes 1572864 | tf_op jit(solution)/shard_map/all_to_all | solution.py:497
  (12 other events, 110.8 us)

commit v5 on v4

--- a/solution.py
+++ b/solution.py
@@ -116,11 +116,6 @@
             out[to : to + rows, columns] = part[start : start + rows, :]
 
 
-def tile_copy(weight, offset, tiles, sems, i):
-    columns = pl.ds(pl.multiple_of(offset + i * STEP, STEP), STEP)
-    return pltpu.make_async_copy(weight.at[:, columns], tiles.at[i], sems.at[i])
-
-
 def forward_side_kernel(place, own, other, weight, toks, first, second):
     rows = own.shape[1]
     place_tokens(place, own, toks, 0)
@@ -152,43 +147,34 @@
     )
 
 
-def forward_distance_kernel(offset, toks, weight, *refs):
-    *outs, tiles, sems = refs
-    steps = tiles.shape[0]
+def forward_distance_kernel(part, toks, weight, *outs):
     rows = outs[0].shape[0] // 4
-    for i in range(steps):
-        tile_copy(weight, offset, tiles, sems, i).start()
 
     def body(i, carry):
-        tile_copy(weight, offset, tiles, sems, i).wait()
         columns = pl.ds(pl.multiple_of(i * STEP, STEP), STEP)
-        part = jnp.dot(toks[...], tiles[i], preferred_element_type=F32).astype(BF16)
+        taken = pl.ds(pl.multiple_of(part.start + i * STEP, STEP), STEP)
+        sums = jnp.dot(toks[...], weight[:, taken], preferred_element_type=F32).astype(BF16)
         for distance, out in enumerate(outs):
             for side in range(2):
                 for core in range(2):
                     start, to = row_of(rows, core, distance, side), (2 * side + core) * rows
-                    out[to : to + rows, columns] = part[start : start + rows, :]
+                    out[to : to + rows, columns] = sums[start : start + rows, :]
         return carry
 
-    lax.fori_loop(0, steps, body, 0)
+    lax.fori_loop(0, (part.stop - part.start) // STEP, body, 0)
 
 
 def forward_distance(toks, weight, part):
     tokens, width = toks.shape
     count = part.stop - part.start
     return call(
-        functools.partial(forward_distance_kernel, part.start),
+        functools.partial(forward_distance_kernel, part),
         "forward_distance",
         [((tokens // N_Y, count), BF16, ON_CHIP)] * N_Y,
-        [ON_CHIP, ANYWHERE],
+        [ON_CHIP, ON_CHIP],
         [toks, weight],
         flops=2 * tokens * width * count,
         size=2 * width * count,
-        scratch=[
-            pltpu.VMEM((count // STEP, width, STEP), BF16),
-            pltpu.SemaphoreType.DMA((count // STEP,)),
-        ],
-        limit=48,
     )
 
 
@@ -200,13 +186,13 @@
             held[start : start + rows, :] = grad[at : at + rows, :]
 
 
-def times_weight(grad, weight, columns):
+def times_weight(grad, weight, columns, part):
     return lax.dot_general(
-        grad, weight[columns, :], (((1,), (1,)), ((), ())), preferred_element_type=F32
-    )
-
-
-def backward_first_kernel(pieces, *refs):
+        grad, weight[columns, part], (((1,), (1,)), ((), ())), preferred_element_type=F32
+    )
+
+
+def backward_first_kernel(pieces, part, *refs):
     grads = refs[: len(pieces)]
     weight, out, held = refs[len(pieces) :]
     half = held.shape[0] // 2
@@ -215,17 +201,17 @@
 
     def body(i, carry):
         columns = pl.ds(pl.multiple_of(i * STEP, STEP), STEP)
-        out[:, columns] = times_weight(held[...], weight, columns)
+        out[:, columns] = times_weight(held[...], weight, columns, part)
         return carry
 
     lax.fori_loop(0, weight.shape[0] // STEP, body, 0)
 
 
-def backward_first(grads, weight, pieces):
-    width, hidden = weight.shape
+def backward_first(grads, weight, pieces, part):
+    width, hidden = weight.shape[0], part.stop - part.start
     count = sum(grad.shape[0] for grad in grads)
     return call(
-        functools.partial(backward_first_kernel, pieces),
+        functools.partial(backward_first_kernel, pieces, part),
         "backward_first",
         [((count, width), F32, ON_CHIP)],
         [ON_CHIP] * (len(grads) + 1),
@@ -236,7 +222,7 @@
     )[0]
 
 
-def backward_last_kernel(pieces, core, place, *refs):
+def backward_last_kernel(pieces, part, core, place, *refs):
     grads = refs[: len(pieces)]
     weight, begun, out, held = refs[len(pieces) :]
     assemble(grads, pieces, held, core)
@@ -245,21 +231,22 @@
 
     def body(i, carry):
         columns = pl.ds(pl.multiple_of(i * STEP, STEP), STEP)
-        part = (begun[half, columns] + times_weight(held[...], weight, columns)).astype(BF16)
+        total = begun[half, columns] + times_weight(held[...], weight, columns, part)
+        total = total.astype(BF16)
         for distance in range(N_Y):
             for side in range(2):
                 start = (2 * distance + side) * rows
-                out[block_of(place, distance, side), :, columns] = part[start : start + rows, :]
+                out[block_of(place, distance, side), :, columns] = total[start : start + rows, :]
         return carry
 
     lax.fori_loop(0, weight.shape[0] // STEP, body, 0)
 
 
-def backward_last(place, grads, weight, begun, pieces, core, name):
-    width, hidden = weight.shape
+def backward_last(place, grads, weight, begun, pieces, part, core, name):
+    width, hidden = weight.shape[0], part.stop - part.start
     count = begun.shape[0] // 2
     return call(
-        functools.partial(backward_last_kernel, pieces, core),
+        functools.partial(backward_last_kernel, pieces, part, core),
         name,
         [((2 * N_Y, count // (2 * N_Y), width), BF16, ON_CHIP)],
         [SCALARS] + [ON_CHIP] * (len(grads) + 2),
@@ -472,19 +459,17 @@
     act_a, grad_a = gelu_step(place, [near, got_far], cotangent, 0, "gelu_a")
     both = jnp.concatenate([grad_a, across(grad_a)], axis=0)
     wide = [both] + [ahead(both, -d) for d in (1, 2, 3)]
-    late, toks = after((weight, toks), both)
-    held_a, held_b = load(late, part_a, "load_a"), load(late, part_b, "load_b")
-    turned = turn(toks)
+    turned = turn(after(toks, both))
     activated = jnp.concatenate([act_a, act_b], axis=1)
 
     grads_b = [*by_y, *by_y_far]
     pieces_b = tuple(((d, s),) for s in range(2) for d in range(N_Y))
-    begun = backward_first(after(grads_b, held_a, held_b, turned, activated), held_b, pieces_b)
+    begun = backward_first(after(grads_b, turned, activated), weight, pieces_b, part_b)
     wide_last = after(wide, begun)
-    theirs = backward_last(place, wide_last, held_a, begun, BY_DISTANCE, 1, "backward_other")
+    theirs = backward_last(place, wide_last, weight, begun, BY_DISTANCE, part_a, 1, "backward_other")
     arrived = other_core(theirs)
     wide_last = after(wide_last, theirs)
-    mine = backward_last(place, wide_last, held_a, begun, BY_DISTANCE, 0, "backward_own")
+    mine = backward_last(place, wide_last, weight, begun, BY_DISTANCE, part_a, 0, "backward_own")
     (chip,) = call(
         add_kernel,
         "chip_sum",

time: 125 us -> 122 us (0.976)
  Pallas kernels: 37.5 us -> 31.6 us
  waiting for transfers between devices: 30.7 us -> 33.3 us
  starting transfers between devices: 35.4 us -> 36.8 us
  local copies, waits for them, and re-layouts: 2.41 us -> 1.08 us
    ppermute x7, waiting for transfers between devices: 8.82 us -> 17.3 us  [across(): return lax.ppermute(array, 'xh', SWAP)]
    pallas_call x16 -> x14, Pallas kernels: 37.5 us -> 31.6 us  [call(): pl.pallas_call(kernel, out_shape=[jax.ShapeDtypeStruct(shape, dtype) for...]
    ppermute x12, waiting for transfers between devices: 19.7 us -> 13.9 us  [ahead(): lax.ppermute(array, 'y', [(i, (i + distance) % N_Y) for i in range(N_Y)])]
    ppermute x2, starting transfers between devices: 3.42 us -> 5.44 us  [other_core(): return lax.ppermute(array, 'c', SWAP)]
  transfers between devices with their start and end apart: 22 -> 22, of which waited for: 9 -> 11; matrix products, arithmetic and copies ran while one was open for 1% -> 0% of each run, Pallas kernels for 23% -> 20%
where the time goes in v5:
time: 122 us
  starting transfers between devices  36.8 us (30%)
  waiting for transfers between devices  33.3 us (27%)
  Pallas kernels  31.6 us (26%)
  blocking collectives  18.1 us (15%)
    pallas_call x14, Pallas kernels, call(): pl.pallas_call(kernel, out_shape=[jax.ShapeDtypeStruct(shape, dtype) for...  31.6 us
    all_to_all x1, blocking collectives, local(): own = lax.all_to_all(spread, PLANE, 0, 0, tiled=True)  18.1 us
    ppermute x12, starting transfers between devices, ahead(): lax.ppermute(array, 'y', [(i, (i + distance) % N_Y) for i in range(N_Y)])  17.4 us
    ppermute x7, waiting for transfers between devices, across(): return lax.ppermute(array, 'xh', SWAP)  17.3 us
    ppermute x12, waiting for transfers between devices, ahead(): lax.ppermute(array, 'y', [(i, (i + distance) % N_Y) for i in range(N_Y)])  13.9 us
    ppermute x7, starting transfers between devices, across(): return lax.ppermute(array, 'xh', SWAP)  10.5 us
    ppermute x2, starting transfers between devices, other_core(): return lax.ppermute(array, 'c', SWAP)  5.44 us
    all_to_all x1, starting transfers between devices, local(): last = lax.all_to_all(chip, PLANE, 0, 0, tiled=True)  3.55 us
  transfers between devices with their start and end apart: 22, of which 11 were waited for; matrix products, arithmetic and copies ran while one was open for 0% of the time, Pallas kernels for 20%

profile of v5, /device:TPU:1, one launch (start us, length us, event | category | flops | bytes accessed | tf_op | source)
XLA Modules:
  0.0 122.0 jit_solution(15583740640728162046)
XLA Ops:
  1.6 18.1 %all_to_all.10.own = bf16[8,32,1536]{2,1,0:T(8,128)(2,1)S(1)} all-to-all(bf16[8,32,1536]{2,1,0:T(8,128)(2,1)S(1)} %broadcast_in_dim.2), channel_id=1, replica_groups=mesh['y'=4,'xh'=2,'xl'=2,'z'=4,'c'=2] {'xl','z'}, dimensions={0} | all-to-all | bytes 1572864 | tf_op jit(solution)/shard_map/all_to_all | solution.py:424
  19.7 2.4 %collective-permute-start = (bf16[8,32,1536]{2,1,0:T(8,128)(2,1)S(1)}, bf16[8,32,1536]{2,1,0:T(8,128)(2,1)S(1)}, u32[]{:S(2)}, u32[]{:S(2)}) collective-permute-start(bf16[8,32,1536]{2,1,0:T(8,128)(2,1)S(1)} %all_to_all.10.own), channel_id=1, source_target_pairs={{0,1},{1,0},{2,3},{3,2},{4,5},{5,4},{6,7},{7,6},{8,9},{9,8},{10,11... | collective-permute-start | bytes 2359304 | tf_op jit(solution)/shard_map/ppermute | solution.py:46
  22.1 2.5 %load_forward.1.weight = bf16[1536,1536]{1,0:T(8,128)(2,1)S(1)} custom-call(bf16[1536,3072]{1,0:T(8,128)(2,1)} %refs_4_.5), custom_call_target="tpu_custom_call" | custom-call | bytes 9437184 | tf_op jit(solution)/shard_map/load_forward/pallas_call | solution.py:62
  24.7 3.6 %forward_side.1 = (bf16[512,1536]{1,0:T(8,128)(2,1)S(1)}, bf16[256,1536]{1,0:T(8,128)(2,1)S(1)}, bf16[256,1536]{1,0:T(8,128)(2,1)S(1)}) custom-call(s32[3]{0:T(128)S(1)} %pad_add_fusion.place, bf16[8,32,1536]{2,1,0:T(8,128)(2,1)S(1)} %all_to_all.10.own, bf16[8,32,1536]{2,1,0:T(8,128)(2,1)S(1)} %collective-permute-done.other, ...), custom_call_target="tpu_custom_call" | custom-call | flops 2415919104 | bytes 4718592 | tf_op jit(solution)/shard_map/forward_side/pallas_call | solution.py:62
  28.3 2.5 %collective-permute-start.4 = (bf16[256,1536]{1,0:T(8,128)(2,1)S(1)}, bf16[256,1536]{1,0:T(8,128)(2,1)S(1)}, u32[]{:S(2)}, u32[]{:S(2)}) collective-permute-start(bf16[256,1536]{1,0:T(8,128)(2,1)S(1)} %get-tuple-element.62), channel_id=1, source_target_pairs={{0,16},{16,0},{1,17},{17,1},{2,18},{18,2},{3,19},{19,3},{4,20},{20... | collective-permute-start | bytes 2359304 | tf_op jit(solution)/shard_map/ppermute | solution.py:42
  30.8 3.0 %forward_distance.1 = (bf16[128,1536]{1,0:T(8,128)(2,1)S(1)}, bf16[128,1536]{1,0:T(8,128)(2,1)S(1)}, bf16[128,1536]{1,0:T(8,128)(2,1)S(1)}, bf16[128,1536]{1,0:T(8,128)(2,1)S(1)}) custom-call(bf16[512,1536]{1,0:T(8,128)(2,1)S(1)} %get-tuple-element.78.toks.tok, bf16[1536,3072]{1,0:T(8,128)(2,1)S(1)} %bitcast.4), custom_call_target="tpu_custom_call" | custom-call | flops 2415919104 | bytes 4718592 | tf_op jit(solution)/shard_map/forward_distance/pallas_call | solution.py:62
  35.2 2.6 %collective-permute-start.2 = (bf16[128,1536]{1,0:T(8,128)(2,1)S(1)}, bf16[128,1536]{1,0:T(8,128)(2,1)S(1)}, u32[]{:S(2)}, u32[]{:S(2)}) collective-permute-start(bf16[128,1536]{1,0:T(8,128)(2,1)S(1)} %get-tuple-element.59), channel_id=1, source_target_pairs={{0,64},{32,96},{64,0},{96,32},{1,65},{33,97},{65,1},{97,33},{2,66}... | collective-permute-start | bytes 1179656 | tf_op jit(solution)/shard_map/ppermute | solution.py:38
  38.9 10.1 %collective-permute-done.4.got = bf16[256,1536]{1,0:T(8,128)(2,1)S(1)} collective-permute-done((bf16[256,1536]{1,0:T(8,128)(2,1)S(1)}, bf16[256,1536]{1,0:T(8,128)(2,1)S(1)}, u32[]{:S(2)}, u32[]{:S(2)}) %collective-permute-start.4) | collective-permute-done | bytes 786464 | tf_op jit(solution)/shard_map/ppermute | solution.py:42
  49.2 3.0 %collective-permute-start.7 = (bf16[64,1536]{1,0:T(8,128)(2,1)S(1)}, bf16[64,1536]{1,0:T(8,128)(2,1)S(1)}, u32[]{:S(2)}, u32[]{:S(2)}) collective-permute-start(bf16[64,1536]{1,0:T(8,128)(2,1)S(1)} %get-tuple-element.71), channel_id=1, source_target_pairs={{0,64},{32,96},{64,0},{96,32},{1,65},{33,97},{65,1},{97,33},{2,66}... | collective-permute-start | bytes 589832 | tf_op jit(solution)/shard_map/ppermute | solution.py:38
  56.4 3.0 %collective-permute-done.7.refs_2_ = bf16[64,1536]{1,0:T(8,128)(2,1)S(1)} collective-permute-done((bf16[64,1536]{1,0:T(8,128)(2,1)S(1)}, bf16[64,1536]{1,0:T(8,128)(2,1)S(1)}, u32[]{:S(2)}, u32[]{:S(2)}) %collective-permute-start.7) | collective-permute-done | bytes 196640 | tf_op jit(solution)/shard_map/ppermute | solution.py:38
  59.5 3.6 %collective-permute-done.8.refs_3_ = bf16[64,1536]{1,0:T(8,128)(2,1)S(1)} collective-permute-done((bf16[64,1536]{1,0:T(8,128)(2,1)S(1)}, bf16[64,1536]{1,0:T(8,128)(2,1)S(1)}, u32[]{:S(2)}, u32[]{:S(2)}) %collective-permute-start.8) | collective-permute-done | bytes 196640 | tf_op jit(solution)/shard_map/ppermute | solution.py:38
  66.3 2.9 %collective-permute-start.14 = (bf16[64,1536]{1,0:T(8,128)(2,1)S(1)}, bf16[64,1536]{1,0:T(8,128)(2,1)S(1)}, u32[]{:S(2)}, u32[]{:S(2)}) collective-permute-start(bf16[64,1536]{1,0:T(8,128)(2,1)S(1)} %get-tuple-element.95.refs_0_.refs_1_), channel_id=1, source_target_pairs={{0,64},{32,96},{64,0},{96,32},{1,65},{33,97},{65,1},{97,33},{2,66}... | collective-permute-start | bytes 589832 | tf_op jit(solution)/shard_map/ppermute | solution.py:38
  72.8 2.3 %collective-permute-start.19 = (bf16[64,1536]{1,0:T(8,128)(2,1)S(1)}, bf16[64,1536]{1,0:T(8,128)(2,1)S(1)}, u32[]{:S(2)}, u32[]{:S(2)}) collective-permute-start(bf16[64,1536]{1,0:T(8,128)(2,1)S(1)} %collective-permute-done.15.refs_3_.refs_4_), channel_id=1, source_target_pairs={{0,16},{16,0},{1,17},{17,1},{2,18},{18,2},{3,19},{19,3},{4,20},{20... | collective-permute-start | bytes 589832 | tf_op jit(solution)/shard_map/ppermute | solution.py:42
  75.1 2.5 %collective-permute-done.9 = bf16[64,1536]{1,0:T(8,128)(2,1)S(1)} collective-permute-done((bf16[64,1536]{1,0:T(8,128)(2,1)S(1)}, bf16[64,1536]{1,0:T(8,128)(2,1)S(1)}, u32[]{:S(2)}, u32[]{:S(2)}) %collective-permute-start.9) | collective-permute-done | bytes 196640 | tf_op jit(solution)/shard_map/ppermute | solution.py:42
  80.4 2.3 %collective-permute-start.18 = (bf16[64,1536]{1,0:T(8,128)(2,1)S(1)}, bf16[64,1536]{1,0:T(8,128)(2,1)S(1)}, u32[]{:S(2)}, u32[]{:S(2)}) collective-permute-start(bf16[64,1536]{1,0:T(8,128)(2,1)S(1)} %collective-permute-done.14.refs_2_.refs_3_), channel_id=1, source_target_pairs={{0,16},{16,0},{1,17},{17,1},{2,18},{18,2},{3,19},{19,3},{4,20},{20... | collective-permute-start | bytes 589832 | tf_op jit(solution)/shard_map/ppermute | solution.py:42
  84.1 2.4 %collective-permute-done.18.refs_6_.refs_7_ = bf16[64,1536]{1,0:T(8,128)(2,1)S(1)} collective-permute-done((bf16[64,1536]{1,0:T(8,128)(2,1)S(1)}, bf16[64,1536]{1,0:T(8,128)(2,1)S(1)}, u32[]{:S(2)}, u32[]{:S(2)}) %collective-permute-start.18) | collective-permute-done | bytes 196640 | tf_op jit(solution)/shard_map/ppermute | solution.py:42
  86.5 2.3 %collective-permute-done.17.refs_5_.refs_6_ = bf16[64,1536]{1,0:T(8,128)(2,1)S(1)} collective-permute-done((bf16[64,1536]{1,0:T(8,128)(2,1)S(1)}, bf16[64,1536]{1,0:T(8,128)(2,1)S(1)}, u32[]{:S(2)}, u32[]{:S(2)}) %collective-permute-start.17) | collective-permute-done | bytes 196640 | tf_op jit(solution)/shard_map/ppermute | solution.py:42
  88.7 3.1 %backward_first.1.refs_5_ = f32[512,1536]{1,0:T(8,128)S(1)} custom-call(bf16[64,1536]{1,0:T(8,128)(2,1)S(1)} %get-tuple-element.95.refs_0_.refs_1_, bf16[64,1536]{1,0:T(8,128)(2,1)S(1)} %collective-permute-done.13.refs_1_.refs_2_, bf16[64,1536]{1,0:T(8,128)(2,1)S(1)} %collective-permute-done.14.refs_2_.refs_3_, ...), custom_call_target="tpu_custom_call" | custom-call | flops 2415919104 | bytes 4718592 | tf_op jit(solution)/shard_map/backward_first/pallas_call | solution.py:62
  92.5 4.1 %collective-permute-done.10.refs_1_.refs_10_ = bf16[128,1536]{1,0:T(8,128)(2,1)S(1)} collective-permute-done((bf16[128,1536]{1,0:T(8,128)(2,1)S(1)}, bf16[128,1536]{1,0:T(8,128)(2,1)S(1)}, u32[]{:S(2)}, u32[]{:S(2)}) %collective-permute-start.10) | collective-permute-done | bytes 393248 | tf_op jit(solution)/shard_map/ppermute | solution.py:38
  96.5 2.4 %backward_other.1 = bf16[8,32,1536]{2,1,0:T(8,128)(2,1)S(1)} custom-call(s32[3]{0:T(128)S(1)} %pad_add_fusion.place, bf16[128,1536]{1,0:T(8,128)(2,1)S(1)} %constant_dynamic-update-slice_fusion.2.refs_0_.refs_9_, bf16[128,1536]{1,0:T(8,128)(2,1)S(1)} %collective-permute-done.10.refs_1_.refs_10_, ...), custom_call_target="tpu_custom_call" | custom-call | flops 1207959552 | bytes 4718592 | tf_op jit(solution)/shard_map/backward_other/pallas_call | solution.py:62
  99.0 3.0 %collective-permute-start.20 = (bf16[8,32,1536]{2,1,0:T(8,128)(2,1)S(1)}, bf16[8,32,1536]{2,1,0:T(8,128)(2,1)S(1)}, u32[]{:S(2)}, u32[]{:S(2)}) collective-permute-start(bf16[8,32,1536]{2,1,0:T(8,128)(2,1)S(1)} %backward_other.1), channel_id=1, source_target_pairs={{0,1},{1,0},{2,3},{3,2},{4,5},{5,4},{6,7},{7,6},{8,9},{9,8},{10,11... | collective-permute-start | bytes 2359304 | tf_op jit(solution)/shard_map/ppermute | solution.py:46
  102.0 2.4 %backward_own.1.mine = bf16[8,32,1536]{2,1,0:T(8,128)(2,1)S(1)} custom-call(s32[3]{0:T(128)S(1)} %pad_add_fusion.place, bf16[128,1536]{1,0:T(8,128)(2,1)S(1)} %constant_dynamic-update-slice_fusion.2.refs_0_.refs_9_, bf16[128,1536]{1,0:T(8,128)(2,1)S(1)} %collective-permute-done.10.refs_1_.refs_10_, ...), custom_call_target="tpu_custom_call" | custom-call | flops 1207959552 | bytes 4718592 | tf_op jit(solution)/shard_map/backward_own/pallas_call | solution.py:62
  105.5 3.5 %all-to-all-start.1 = ((bf16[8,32,1536]{2,1,0:T(8,128)(2,1)}), bf16[8,32,1536]{2,1,0:T(8,128)(2,1)S(1)}, u32[]{:S(2)}, u32[]{:S(2)}) async-start(bf16[8,32,1536]{2,1,0:T(8,128)(2,1)} %chip_sum.1), calls=%async_computation.1 | async-start | bytes 1572864 | tf_op jit(solution)/shard_map/all_to_all | solution.py:482
  109.1 10.0 %weight_grad.1 = bf16[1536,3072]{1,0:T(8,128)(2,1)} custom-call(bf16[1536,512]{1,0:T(8,128)(2,1)} %copy-done.1, bf16[64,1536]{1,0:T(8,128)(2,1)} %copy-done.6, bf16[64,1536]{1,0:T(8,128)(2,1)} %copy-done.10, bf16[64,1536]{1,0:T(8,128)(2,1)} %copy-done.9, bf16[64,1536]{1,0:T(8,128)(2,1)} %copy-done.8, bf16[64,1536]{1,0:T(8,128)(2,1)} %copy-done.7, ...), custom_call_target="tpu_custom_call" | custom-call | flops 4831838208 | bytes 9437184 | tf_op jit(solution)/shard_map/weight_grad/pallas_call | solution.py:62
  (78 shorter events, 23.2 us)
Async XLA Ops:
  19.7 5.0 %collective-permute-start = (bf16[8,32,1536]{2,1,0:T(8,128)(2,1)S(1)}, bf16[8,32,1536]{2,1,0:T(8,128)(2,1)S(1)}, u32[]{:S(2)}, u32[]{:S(2)}) collective-permute-start(bf16[8,32,1536]{2,1,0:T(8,128)(2,1)S(1)} %all_to_all.10.own), channel_id=1, source_target_pairs={{0,1},{1,0},{2,3},{3,2},{4,5},{5,4},{6,7},{7,6},{8,9},{9,8},{10,11... | collective-permute-start | bytes 2359304 | tf_op jit(solution)/shard_map/ppermute | solution.py:46
  28.3 20.8 %collective-permute-start.4 = (bf16[256,1536]{1,0:T(8,128)(2,1)S(1)}, bf16[256,1536]{1,0:T(8,128)(2,1)S(1)}, u32[]{:S(2)}, u32[]{:S(2)}) collective-permute-start(bf16[256,1536]{1,0:T(8,128)(2,1)S(1)} %get-tuple-element.62), channel_id=1, source_target_pairs={{0,16},{16,0},{1,17},{17,1},{2,18},{18,2},{3,19},{19,3},{4,20},{20... | collective-permute-start | bytes 2359304 | tf_op jit(solution)/shard_map/ppermute | solution.py:42
  30.8 33.4 %copy-start.2 = (bf16[64,3072]{1,0:T(8,128)(2,1)S(1)}, bf16[64,3072]{1,0:T(8,128)(2,1)}, u32[]{:S(2)}) copy-start(bf16[64,3072]{1,0:T(8,128)(2,1)} %refs_2_.1) | copy-start | bytes 1179652
  33.8 19.2 %collective-permute-start.1 = (bf16[128,1536]{1,0:T(8,128)(2,1)S(1)}, bf16[128,1536]{1,0:T(8,128)(2,1)S(1)}, u32[]{:S(2)}, u32[]{:S(2)}) collective-permute-start(bf16[128,1536]{1,0:T(8,128)(2,1)S(1)} %get-tuple-element.58), channel_id=1, source_target_pairs={{0,32},{32,64},{64,96},{96,0},{1,33},{33,65},{65,97},{97,1},{2,34}... | collective-permute-start | bytes 1179656 | tf_op jit(solution)/shard_map/ppermute | solution.py:38
  35.2 20.0 %collective-permute-start.2 = (bf16[128,1536]{1,0:T(8,128)(2,1)S(1)}, bf16[128,1536]{1,0:T(8,128)(2,1)S(1)}, u32[]{:S(2)}, u32[]{:S(2)}) collective-permute-start(bf16[128,1536]{1,0:T(8,128)(2,1)S(1)} %get-tuple-element.59), channel_id=1, source_target_pairs={{0,64},{32,96},{64,0},{96,32},{1,65},{33,97},{65,1},{97,33},{2,66}... | collective-permute-start | bytes 1179656 | tf_op jit(solution)/shard_map/ppermute | solution.py:38
  37.8 17.4 %collective-permute-start.3 = (bf16[128,1536]{1,0:T(8,128)(2,1)S(1)}, bf16[128,1536]{1,0:T(8,128)(2,1)S(1)}, u32[]{:S(2)}, u32[]{:S(2)}) collective-permute-start(bf16[128,1536]{1,0:T(8,128)(2,1)S(1)} %get-tuple-element.60), channel_id=1, source_target_pairs={{0,96},{32,0},{64,32},{96,64},{1,97},{33,1},{65,33},{97,65},{2,98}... | collective-permute-start | bytes 1179656 | tf_op jit(solution)/shard_map/ppermute | solution.py:38
  49.2 10.2 %collective-permute-start.7 = (bf16[64,1536]{1,0:T(8,128)(2,1)S(1)}, bf16[64,1536]{1,0:T(8,128)(2,1)S(1)}, u32[]{:S(2)}, u32[]{:S(2)}) collective-permute-start(bf16[64,1536]{1,0:T(8,128)(2,1)S(1)} %get-tuple-element.71), channel_id=1, source_target_pairs={{0,64},{32,96},{64,0},{96,32},{1,65},{33,97},{65,1},{97,33},{2,66}... | collective-permute-start | bytes 589832 | tf_op jit(solution)/shard_map/ppermute | solution.py:38
  52.2 10.8 %collective-permute-start.8 = (bf16[64,1536]{1,0:T(8,128)(2,1)S(1)}, bf16[64,1536]{1,0:T(8,128)(2,1)S(1)}, u32[]{:S(2)}, u32[]{:S(2)}) collective-permute-start(bf16[64,1536]{1,0:T(8,128)(2,1)S(1)} %get-tuple-element.72), channel_id=1, source_target_pairs={{0,96},{32,0},{64,32},{96,64},{1,97},{33,1},{65,33},{97,65},{2,98}... | collective-permute-start | bytes 589832 | tf_op jit(solution)/shard_map/ppermute | solution.py:38
  53.0 11.2 %collective-permute-start.6 = (bf16[64,1536]{1,0:T(8,128)(2,1)S(1)}, bf16[64,1536]{1,0:T(8,128)(2,1)S(1)}, u32[]{:S(2)}, u32[]{:S(2)}) collective-permute-start(bf16[64,1536]{1,0:T(8,128)(2,1)S(1)} %get-tuple-element.64), channel_id=1, source_target_pairs={{0,32},{32,64},{64,96},{96,0},{1,33},{33,65},{65,97},{97,1},{2,34}... | collective-permute-start | bytes 589832 | tf_op jit(solution)/shard_map/ppermute | solution.py:38
  55.4 14.9 %collective-permute-start.5 = (bf16[64,1536]{1,0:T(8,128)(2,1)S(1)}, bf16[64,1536]{1,0:T(8,128)(2,1)S(1)}, u32[]{:S(2)}, u32[]{:S(2)}) collective-permute-start(bf16[64,1536]{1,0:T(8,128)(2,1)S(1)} %get-tuple-element.69), channel_id=1, source_target_pairs={{0,16},{16,0},{1,17},{17,1},{2,18},{18,2},{3,19},{19,3},{4,20},{20... | collective-permute-start | bytes 589832 | tf_op jit(solution)/shard_map/ppermute | solution.py:42
  65.1 26.7 %copy-start.6 = (bf16[64,1536]{1,0:T(8,128)(2,1)}, bf16[64,1536]{1,0:T(8,128)(2,1)S(1)}, u32[]{:S(2)}) copy-start(bf16[64,1536]{1,0:T(8,128)(2,1)S(1)} %get-tuple-element.95.refs_0_.refs_1_) | copy-start | bytes 589828
  65.2 12.6 %collective-permute-start.16 = (bf16[64,1536]{1,0:T(8,128)(2,1)S(1)}, bf16[64,1536]{1,0:T(8,128)(2,1)S(1)}, u32[]{:S(2)}, u32[]{:S(2)}) collective-permute-start(bf16[64,1536]{1,0:T(8,128)(2,1)S(1)} %get-tuple-element.95.refs_0_.refs_1_), channel_id=1, source_target_pairs={{0,16},{16,0},{1,17},{17,1},{2,18},{18,2},{3,19},{19,3},{4,20},{20... | collective-permute-start | bytes 589832 | tf_op jit(solution)/shard_map/ppermute | solution.py:42
  65.2 7.5 %collective-permute-start.15 = (bf16[64,1536]{1,0:T(8,128)(2,1)S(1)}, bf16[64,1536]{1,0:T(8,128)(2,1)S(1)}, u32[]{:S(2)}, u32[]{:S(2)}) collective-permute-start(bf16[64,1536]{1,0:T(8,128)(2,1)S(1)} %get-tuple-element.95.refs_0_.refs_1_), channel_id=1, source_target_pairs={{0,32},{32,64},{64,96},{96,0},{1,33},{33,65},{65,97},{97,1},{2,34}... | collective-permute-start | bytes 589832 | tf_op jit(solution)/shard_map/ppermute | solution.py:38
  66.3 12.9 %collective-permute-start.14 = (bf16[64,1536]{1,0:T(8,128)(2,1)S(1)}, bf16[64,1536]{1,0:T(8,128)(2,1)S(1)}, u32[]{:S(2)}, u32[]{:S(2)}) collective-permute-start(bf16[64,1536]{1,0:T(8,128)(2,1)S(1)} %get-tuple-element.95.refs_0_.refs_1_), channel_id=1, source_target_pairs={{0,64},{32,96},{64,0},{96,32},{1,65},{33,97},{65,1},{97,33},{2,66}... | collective-permute-start | bytes 589832 | tf_op jit(solution)/shard_map/ppermute | solution.py:38
  69.2 11.2 %collective-permute-start.13 = (bf16[64,1536]{1,0:T(8,128)(2,1)S(1)}, bf16[64,1536]{1,0:T(8,128)(2,1)S(1)}, u32[]{:S(2)}, u32[]{:S(2)}) collective-permute-start(bf16[64,1536]{1,0:T(8,128)(2,1)S(1)} %get-tuple-element.95.refs_0_.refs_1_), channel_id=1, source_target_pairs={{0,96},{32,0},{64,32},{96,64},{1,97},{33,1},{65,33},{97,65},{2,98}... | collective-permute-start | bytes 589832 | tf_op jit(solution)/shard_map/ppermute | solution.py:38
  71.2 6.4 %collective-permute-start.9 = (bf16[64,1536]{1,0:T(8,128)(2,1)S(1)}, bf16[64,1536]{1,0:T(8,128)(2,1)S(1)}, u32[]{:S(2)}, u32[]{:S(2)}) collective-permute-start(bf16[64,1536]{1,0:T(8,128)(2,1)S(1)} %get-tuple-element.77), channel_id=1, source_target_pairs={{0,16},{16,0},{1,17},{17,1},{2,18},{18,2},{3,19},{19,3},{4,20},{20... | collective-permute-start | bytes 589832 | tf_op jit(solution)/shard_map/ppermute | solution.py:42
  72.8 9.9 %collective-permute-start.19 = (bf16[64,1536]{1,0:T(8,128)(2,1)S(1)}, bf16[64,1536]{1,0:T(8,128)(2,1)S(1)}, u32[]{:S(2)}, u32[]{:S(2)}) collective-permute-start(bf16[64,1536]{1,0:T(8,128)(2,1)S(1)} %collective-permute-done.15.refs_3_.refs_4_), channel_id=1, source_target_pairs={{0,16},{16,0},{1,17},{17,1},{2,18},{18,2},{3,19},{19,3},{4,20},{20... | collective-permute-start | bytes 589832 | tf_op jit(solution)/shard_map/ppermute | solution.py:42
  77.6 14.4 %collective-permute-start.12 = (bf16[128,1536]{1,0:T(8,128)(2,1)S(1)}, bf16[128,1536]{1,0:T(8,128)(2,1)S(1)}, u32[]{:S(2)}, u32[]{:S(2)}) collective-permute-start(bf16[128,1536]{1,0:T(8,128)(2,1)S(1)} %constant_dynamic-update-slice_fusion.2.refs_0_.refs_9_), channel_id=1, source_target_pairs={{0,32},{32,64},{64,96},{96,0},{1,33},{33,65},{65,97},{97,1},{2,34}... | collective-permute-start | bytes 1179656 | tf_op jit(solution)/shard_map/ppermute | solution.py:38
  77.8 14.7 %collective-permute-start.11 = (bf16[128,1536]{1,0:T(8,128)(2,1)S(1)}, bf16[128,1536]{1,0:T(8,128)(2,1)S(1)}, u32[]{:S(2)}, u32[]{:S(2)}) collective-permute-start(bf16[128,1536]{1,0:T(8,128)(2,1)S(1)} %constant_dynamic-update-slice_fusion.2.refs_0_.refs_9_), channel_id=1, source_target_pairs={{0,64},{32,96},{64,0},{96,32},{1,65},{33,97},{65,1},{97,33},{2,66}... | collective-permute-start | bytes 1179656 | tf_op jit(solution)/shard_map/ppermute | solution.py:38
  79.1 17.4 %collective-permute-start.10 = (bf16[128,1536]{1,0:T(8,128)(2,1)S(1)}, bf16[128,1536]{1,0:T(8,128)(2,1)S(1)}, u32[]{:S(2)}, u32[]{:S(2)}) collective-permute-start(bf16[128,1536]{1,0:T(8,128)(2,1)S(1)} %constant_dynamic-update-slice_fusion.2.refs_0_.refs_9_), channel_id=1, source_target_pairs={{0,96},{32,0},{64,32},{96,64},{1,97},{33,1},{65,33},{97,65},{2,98}... | collective-permute-start | bytes 1179656 | tf_op jit(solution)/shard_map/ppermute | solution.py:38
  80.4 6.0 %collective-permute-start.18 = (bf16[64,1536]{1,0:T(8,128)(2,1)S(1)}, bf16[64,1536]{1,0:T(8,128)(2,1)S(1)}, u32[]{:S(2)}, u32[]{:S(2)}) collective-permute-start(bf16[64,1536]{1,0:T(8,128)(2,1)S(1)} %collective-permute-done.14.refs_2_.refs_3_), channel_id=1, source_target_pairs={{0,16},{16,0},{1,17},{17,1},{2,18},{18,2},{3,19},{19,3},{4,20},{20... | collective-permute-start | bytes 589832 | tf_op jit(solution)/shard_map/ppermute | solution.py:42
  82.7 6.0 %collective-permute-start.17 = (bf16[64,1536]{1,0:T(8,128)(2,1)S(1)}, bf16[64,1536]{1,0:T(8,128)(2,1)S(1)}, u32[]{:S(2)}, u32[]{:S(2)}) collective-permute-start(bf16[64,1536]{1,0:T(8,128)(2,1)S(1)} %collective-permute-done.13.refs_1_.refs_2_), channel_id=1, source_target_pairs={{0,16},{16,0},{1,17},{17,1},{2,18},{18,2},{3,19},{19,3},{4,20},{20... | collective-permute-start | bytes 589832 | tf_op jit(solution)/shard_map/ppermute | solution.py:42
  99.0 5.5 %collective-permute-start.20 = (bf16[8,32,1536]{2,1,0:T(8,128)(2,1)S(1)}, bf16[8,32,1536]{2,1,0:T(8,128)(2,1)S(1)}, u32[]{:S(2)}, u32[]{:S(2)}) collective-permute-start(bf16[8,32,1536]{2,1,0:T(8,128)(2,1)S(1)} %backward_other.1), channel_id=1, source_target_pairs={{0,1},{1,0},{2,3},{3,2},{4,5},{5,4},{6,7},{7,6},{8,9},{9,8},{10,11... | collective-permute-start | bytes 2359304 | tf_op jit(solution)/shard_map/ppermute | solution.py:46
  105.5 15.7 %all-to-all-start.1 = ((bf16[8,32,1536]{2,1,0:T(8,128)(2,1)}), bf16[8,32,1536]{2,1,0:T(8,128)(2,1)S(1)}, u32[]{:S(2)}, u32[]{:S(2)}) async-start(bf16[8,32,1536]{2,1,0:T(8,128)(2,1)} %chip_sum.1), calls=%async_computation.1 | async-start | bytes 1572864 | tf_op jit(solution)/shard_map/all_to_all | solution.py:482
  (16 other events, 164.8 us)

commit v6 on v5

--- a/solution.py
+++ b/solution.py
@@ -258,8 +258,7 @@
 
 
 def add_kernel(mine, got, out):
-    for block in range(out.shape[0]):
-        out[block] = (mine[block].astype(F32) + got[block].astype(F32)).astype(BF16)
+    out[...] = mine[...] + got[...]
 
 
 def turn_kernel(tok, out, held, sem):
@@ -453,10 +452,12 @@
     got_far = across(far)
 
     act_b, grad_b = gelu_step(place, [kept, *got_b], cotangent, cut, "gelu_b")
-    by_y = [grad_b] + [ahead(grad_b, -d) for d in (1, 2, 3)]
-    by_y_far = [across(grad) for grad in by_y]
     got_far = after(got_far, grad_b)
     act_a, grad_a = gelu_step(place, [near, got_far], cotangent, 0, "gelu_a")
+    late_b = after(grad_b, grad_a)
+    by_y = [grad_b]
+    by_y += [ahead(late_b if d == 1 else grad_b, -d) for d in (1, 2, 3)]
+    by_y_far = [across(grad) for grad in by_y]
     both = jnp.concatenate([grad_a, across(grad_a)], axis=0)
     wide = [both] + [ahead(both, -d) for d in (1, 2, 3)]
     turned = turn(after(toks, both))

time: 122 us -> 121 us (level)
    ppermute x7, waiting for transfers between devices: 17.3 us -> 15.9 us  [across(): return lax.ppermute(array, 'xh', SWAP)]
    ppermute x2, starting transfers between devices: 5.44 us -> 4.11 us  [other_core(): return lax.ppermute(array, 'c', SWAP)]
    ppermute x12, waiting for transfers between devices: 13.9 us -> 15.1 us  [ahead(): lax.ppermute(array, 'y', [(i, (i + distance) % N_Y) for i in range(N_Y)])]
where the time goes in v6:
time: 121 us
  starting transfers between devices  36.1 us (30%)
  waiting for transfers between devices  33.2 us (27%)
  Pallas kernels  31.5 us (26%)
  blocking collectives  18.1 us (15%)
    pallas_call x14, Pallas kernels, call(): pl.pallas_call(kernel, out_shape=[jax.ShapeDtypeStruct(shape, dtype) for...  31.5 us
    all_to_all x1, blocking collectives, local(): own = lax.all_to_all(spread, PLANE, 0, 0, tiled=True)  18.1 us
    ppermute x12, starting transfers between devices, ahead(): lax.ppermute(array, 'y', [(i, (i + distance) % N_Y) for i in range(N_Y)])  17 us
    ppermute x7, waiting for transfers between devices, across(): return lax.ppermute(array, 'xh', SWAP)  15.9 us
    ppermute x12, waiting for transfers between devices, ahead(): lax.ppermute(array, 'y', [(i, (i + distance) % N_Y) for i in range(N_Y)])  15.1 us
    ppermute x7, starting transfers between devices, across(): return lax.ppermute(array, 'xh', SWAP)  11.4 us
    ppermute x2, starting transfers between devices, other_core(): return lax.ppermute(array, 'c', SWAP)  4.11 us
    all_to_all x1, starting transfers between devices, local(): last = lax.all_to_all(chip, PLANE, 0, 0, tiled=True)  3.55 us
  transfers between devices with their start and end apart: 22, of which 11 were waited for; matrix products, arithmetic and copies ran while one was open for 0% of the time, Pallas kernels for 20%

profile of v6, /device:TPU:1, one launch (start us, length us, event | category | flops | bytes accessed | tf_op | source)
XLA Modules:
  0.0 121.0 jit_solution(7156102995558772864)
XLA Ops:
  1.6 18.1 %all_to_all.10.own = bf16[8,32,1536]{2,1,0:T(8,128)(2,1)S(1)} all-to-all(bf16[8,32,1536]{2,1,0:T(8,128)(2,1)S(1)} %broadcast_in_dim.2), channel_id=1, replica_groups=mesh['y'=4,'xh'=2,'xl'=2,'z'=4,'c'=2] {'xl','z'}, dimensions={0} | all-to-all | bytes 1572864 | tf_op jit(solution)/shard_map/all_to_all | solution.py:423
  19.7 2.4 %collective-permute-start = (bf16[8,32,1536]{2,1,0:T(8,128)(2,1)S(1)}, bf16[8,32,1536]{2,1,0:T(8,128)(2,1)S(1)}, u32[]{:S(2)}, u32[]{:S(2)}) collective-permute-start(bf16[8,32,1536]{2,1,0:T(8,128)(2,1)S(1)} %all_to_all.10.own), channel_id=1, source_target_pairs={{0,1},{1,0},{2,3},{3,2},{4,5},{5,4},{6,7},{7,6},{8,9},{9,8},{10,11... | collective-permute-start | bytes 2359304 | tf_op jit(solution)/shard_map/ppermute | solution.py:46
  22.1 2.5 %load_forward.1.weight = bf16[1536,1536]{1,0:T(8,128)(2,1)S(1)} custom-call(bf16[1536,3072]{1,0:T(8,128)(2,1)} %refs_4_.5), custom_call_target="tpu_custom_call" | custom-call | bytes 9437184 | tf_op jit(solution)/shard_map/load_forward/pallas_call | solution.py:62
  24.7 3.6 %forward_side.1 = (bf16[512,1536]{1,0:T(8,128)(2,1)S(1)}, bf16[256,1536]{1,0:T(8,128)(2,1)S(1)}, bf16[256,1536]{1,0:T(8,128)(2,1)S(1)}) custom-call(s32[3]{0:T(128)S(1)} %pad_add_fusion.place, bf16[8,32,1536]{2,1,0:T(8,128)(2,1)S(1)} %all_to_all.10.own, bf16[8,32,1536]{2,1,0:T(8,128)(2,1)S(1)} %collective-permute-done.other, ...), custom_call_target="tpu_custom_call" | custom-call | flops 2415919104 | bytes 4718592 | tf_op jit(solution)/shard_map/forward_side/pallas_call | solution.py:62
  28.3 2.5 %collective-permute-start.4 = (bf16[256,1536]{1,0:T(8,128)(2,1)S(1)}, bf16[256,1536]{1,0:T(8,128)(2,1)S(1)}, u32[]{:S(2)}, u32[]{:S(2)}) collective-permute-start(bf16[256,1536]{1,0:T(8,128)(2,1)S(1)} %get-tuple-element.63), channel_id=1, source_target_pairs={{0,16},{16,0},{1,17},{17,1},{2,18},{18,2},{3,19},{19,3},{4,20},{20... | collective-permute-start | bytes 2359304 | tf_op jit(solution)/shard_map/ppermute | solution.py:42
  30.8 3.0 %forward_distance.1 = (bf16[128,1536]{1,0:T(8,128)(2,1)S(1)}, bf16[128,1536]{1,0:T(8,128)(2,1)S(1)}, bf16[128,1536]{1,0:T(8,128)(2,1)S(1)}, bf16[128,1536]{1,0:T(8,128)(2,1)S(1)}) custom-call(bf16[512,1536]{1,0:T(8,128)(2,1)S(1)} %get-tuple-element.80.toks.tok, bf16[1536,3072]{1,0:T(8,128)(2,1)S(1)} %bitcast.4), custom_call_target="tpu_custom_call" | custom-call | flops 2415919104 | bytes 4718592 | tf_op jit(solution)/shard_map/forward_distance/pallas_call | solution.py:62
  35.2 2.6 %collective-permute-start.2 = (bf16[128,1536]{1,0:T(8,128)(2,1)S(1)}, bf16[128,1536]{1,0:T(8,128)(2,1)S(1)}, u32[]{:S(2)}, u32[]{:S(2)}) collective-permute-start(bf16[128,1536]{1,0:T(8,128)(2,1)S(1)} %get-tuple-element.60), channel_id=1, source_target_pairs={{0,64},{32,96},{64,0},{96,32},{1,65},{33,97},{65,1},{97,33},{2,66}... | collective-permute-start | bytes 1179656 | tf_op jit(solution)/shard_map/ppermute | solution.py:38
  38.9 10.1 %collective-permute-done.4.got = bf16[256,1536]{1,0:T(8,128)(2,1)S(1)} collective-permute-done((bf16[256,1536]{1,0:T(8,128)(2,1)S(1)}, bf16[256,1536]{1,0:T(8,128)(2,1)S(1)}, u32[]{:S(2)}, u32[]{:S(2)}) %collective-permute-start.4) | collective-permute-done | bytes 786464 | tf_op jit(solution)/shard_map/ppermute | solution.py:42
  49.2 3.0 %collective-permute-start.7 = (bf16[64,1536]{1,0:T(8,128)(2,1)S(1)}, bf16[64,1536]{1,0:T(8,128)(2,1)S(1)}, u32[]{:S(2)}, u32[]{:S(2)}) collective-permute-start(bf16[64,1536]{1,0:T(8,128)(2,1)S(1)} %get-tuple-element.72), channel_id=1, source_target_pairs={{0,64},{32,96},{64,0},{96,32},{1,65},{33,97},{65,1},{97,33},{2,66}... | collective-permute-start | bytes 589832 | tf_op jit(solution)/shard_map/ppermute | solution.py:38
  56.4 3.0 %collective-permute-done.7.refs_2_ = bf16[64,1536]{1,0:T(8,128)(2,1)S(1)} collective-permute-done((bf16[64,1536]{1,0:T(8,128)(2,1)S(1)}, bf16[64,1536]{1,0:T(8,128)(2,1)S(1)}, u32[]{:S(2)}, u32[]{:S(2)}) %collective-permute-start.7) | collective-permute-done | bytes 196640 | tf_op jit(solution)/shard_map/ppermute | solution.py:38
  59.5 3.6 %collective-permute-done.8.refs_3_ = bf16[64,1536]{1,0:T(8,128)(2,1)S(1)} collective-permute-done((bf16[64,1536]{1,0:T(8,128)(2,1)S(1)}, bf16[64,1536]{1,0:T(8,128)(2,1)S(1)}, u32[]{:S(2)}, u32[]{:S(2)}) %collective-permute-start.8) | collective-permute-done | bytes 196640 | tf_op jit(solution)/shard_map/ppermute | solution.py:38
  66.3 2.9 %collective-permute-start.14 = (bf16[64,1536]{1,0:T(8,128)(2,1)S(1)}, bf16[64,1536]{1,0:T(8,128)(2,1)S(1)}, u32[]{:S(2)}, u32[]{:S(2)}) collective-permute-start(bf16[64,1536]{1,0:T(8,128)(2,1)S(1)} %get-tuple-element.97.refs_0_.refs_1_), channel_id=1, source_target_pairs={{0,64},{32,96},{64,0},{96,32},{1,65},{33,97},{65,1},{97,33},{2,66}... | collective-permute-start | bytes 589832 | tf_op jit(solution)/shard_map/ppermute | solution.py:38
  70.1 2.1 %collective-permute-start.9 = (bf16[64,1536]{1,0:T(8,128)(2,1)S(1)}, bf16[64,1536]{1,0:T(8,128)(2,1)S(1)}, u32[]{:S(2)}, u32[]{:S(2)}) collective-permute-start(bf16[64,1536]{1,0:T(8,128)(2,1)S(1)} %get-tuple-element.78), channel_id=1, source_target_pairs={{0,16},{16,0},{1,17},{17,1},{2,18},{18,2},{3,19},{19,3},{4,20},{20... | collective-permute-start | bytes 589832 | tf_op jit(solution)/shard_map/ppermute | solution.py:42
  72.8 2.2 %collective-permute-start.19 = (bf16[64,1536]{1,0:T(8,128)(2,1)S(1)}, bf16[64,1536]{1,0:T(8,128)(2,1)S(1)}, u32[]{:S(2)}, u32[]{:S(2)}) collective-permute-start(bf16[64,1536]{1,0:T(8,128)(2,1)S(1)} %collective-permute-done.15.refs_3_.refs_4_), channel_id=1, source_target_pairs={{0,16},{16,0},{1,17},{17,1},{2,18},{18,2},{3,19},{19,3},{4,20},{20... | collective-permute-start | bytes 589832 | tf_op jit(solution)/shard_map/ppermute | solution.py:42
  76.9 2.4 %collective-permute-start.11 = (bf16[128,1536]{1,0:T(8,128)(2,1)S(1)}, bf16[128,1536]{1,0:T(8,128)(2,1)S(1)}, u32[]{:S(2)}, u32[]{:S(2)}) collective-permute-start(bf16[128,1536]{1,0:T(8,128)(2,1)S(1)} %constant_dynamic-update-slice_fusion.2.refs_0_.refs_9_), channel_id=1, source_target_pairs={{0,64},{32,96},{64,0},{96,32},{1,65},{33,97},{65,1},{97,33},{2,66}... | collective-permute-start | bytes 1179656 | tf_op jit(solution)/shard_map/ppermute | solution.py:38
  83.8 2.0 %collective-permute-done.18.refs_6_.refs_7_ = bf16[64,1536]{1,0:T(8,128)(2,1)S(1)} collective-permute-done((bf16[64,1536]{1,0:T(8,128)(2,1)S(1)}, bf16[64,1536]{1,0:T(8,128)(2,1)S(1)}, u32[]{:S(2)}, u32[]{:S(2)}) %collective-permute-start.18) | collective-permute-done | bytes 196640 | tf_op jit(solution)/shard_map/ppermute | solution.py:42
  85.8 2.1 %collective-permute-done.17.refs_5_.refs_6_ = bf16[64,1536]{1,0:T(8,128)(2,1)S(1)} collective-permute-done((bf16[64,1536]{1,0:T(8,128)(2,1)S(1)}, bf16[64,1536]{1,0:T(8,128)(2,1)S(1)}, u32[]{:S(2)}, u32[]{:S(2)}) %collective-permute-start.17) | collective-permute-done | bytes 196640 | tf_op jit(solution)/shard_map/ppermute | solution.py:42
  87.9 3.1 %backward_first.1.refs_5_ = f32[512,1536]{1,0:T(8,128)S(1)} custom-call(bf16[64,1536]{1,0:T(8,128)(2,1)S(1)} %get-tuple-element.97.refs_0_.refs_1_, bf16[64,1536]{1,0:T(8,128)(2,1)S(1)} %collective-permute-done.13.refs_1_.refs_2_, bf16[64,1536]{1,0:T(8,128)(2,1)S(1)} %collective-permute-done.14.refs_2_.refs_3_, ...), custom_call_target="tpu_custom_call" | custom-call | flops 2415919104 | bytes 4718592 | tf_op jit(solution)/shard_map/backward_first/pallas_call | solution.py:62
  92.9 4.1 %collective-permute-done.10.refs_1_.refs_10_ = bf16[128,1536]{1,0:T(8,128)(2,1)S(1)} collective-permute-done((bf16[128,1536]{1,0:T(8,128)(2,1)S(1)}, bf16[128,1536]{1,0:T(8,128)(2,1)S(1)}, u32[]{:S(2)}, u32[]{:S(2)}) %collective-permute-start.10) | collective-permute-done | bytes 393248 | tf_op jit(solution)/shard_map/ppermute | solution.py:38
  97.0 2.4 %backward_other.1 = bf16[8,32,1536]{2,1,0:T(8,128)(2,1)S(1)} custom-call(s32[3]{0:T(128)S(1)} %pad_add_fusion.place, bf16[128,1536]{1,0:T(8,128)(2,1)S(1)} %constant_dynamic-update-slice_fusion.2.refs_0_.refs_9_, bf16[128,1536]{1,0:T(8,128)(2,1)S(1)} %collective-permute-done.10.refs_1_.refs_10_, ...), custom_call_target="tpu_custom_call" | custom-call | flops 1207959552 | bytes 4718592 | tf_op jit(solution)/shard_map/backward_other/pallas_call | solution.py:62
  101.2 2.4 %backward_own.1.mine = bf16[8,32,1536]{2,1,0:T(8,128)(2,1)S(1)} custom-call(s32[3]{0:T(128)S(1)} %pad_add_fusion.place, bf16[128,1536]{1,0:T(8,128)(2,1)S(1)} %constant_dynamic-update-slice_fusion.2.refs_0_.refs_9_, bf16[128,1536]{1,0:T(8,128)(2,1)S(1)} %collective-permute-done.10.refs_1_.refs_10_, ...), custom_call_target="tpu_custom_call" | custom-call | flops 1207959552 | bytes 4718592 | tf_op jit(solution)/shard_map/backward_own/pallas_call | solution.py:62
  104.6 3.5 %all-to-all-start.1 = ((bf16[8,32,1536]{2,1,0:T(8,128)(2,1)}), bf16[8,32,1536]{2,1,0:T(8,128)(2,1)S(1)}, u32[]{:S(2)}, u32[]{:S(2)}) async-start(bf16[8,32,1536]{2,1,0:T(8,128)(2,1)} %chip_sum.1), calls=%async_computation.1 | async-start | bytes 1572864 | tf_op jit(solution)/shard_map/all_to_all | solution.py:483
  108.1 10.0 %weight_grad.1 = bf16[1536,3072]{1,0:T(8,128)(2,1)} custom-call(bf16[1536,512]{1,0:T(8,128)(2,1)} %copy-done.1, bf16[64,1536]{1,0:T(8,128)(2,1)} %copy-done.6, bf16[64,1536]{1,0:T(8,128)(2,1)} %copy-done.10, bf16[64,1536]{1,0:T(8,128)(2,1)} %copy-done.9, bf16[64,1536]{1,0:T(8,128)(2,1)} %copy-done.8, bf16[64,1536]{1,0:T(8,128)(2,1)} %copy-done.7, ...), custom_call_target="tpu_custom_call" | custom-call | flops 4831838208 | bytes 9437184 | tf_op jit(solution)/shard_map/weight_grad/pallas_call | solution.py:62
  118.1 2.2 %all-to-all-done.1.got = bf16[8,32,1536]{2,1,0:T(8,128)(2,1)S(1)} async-done(((bf16[8,32,1536]{2,1,0:T(8,128)(2,1)}), bf16[8,32,1536]{2,1,0:T(8,128)(2,1)S(1)}, u32[]{:S(2)}, u32[]{:S(2)}) %all-to-all-start.1) | async-done | bytes 786464 | tf_op jit(solution)/shard_map/all_to_all | solution.py:483
  (78 shorter events, 24.0 us)
Async XLA Ops:
  19.7 5.0 %collective-permute-start = (bf16[8,32,1536]{2,1,0:T(8,128)(2,1)S(1)}, bf16[8,32,1536]{2,1,0:T(8,128)(2,1)S(1)}, u32[]{:S(2)}, u32[]{:S(2)}) collective-permute-start(bf16[8,32,1536]{2,1,0:T(8,128)(2,1)S(1)} %all_to_all.10.own), channel_id=1, source_target_pairs={{0,1},{1,0},{2,3},{3,2},{4,5},{5,4},{6,7},{7,6},{8,9},{9,8},{10,11... | collective-permute-start | bytes 2359304 | tf_op jit(solution)/shard_map/ppermute | solution.py:46
  28.3 20.8 %collective-permute-start.4 = (bf16[256,1536]{1,0:T(8,128)(2,1)S(1)}, bf16[256,1536]{1,0:T(8,128)(2,1)S(1)}, u32[]{:S(2)}, u32[]{:S(2)}) collective-permute-start(bf16[256,1536]{1,0:T(8,128)(2,1)S(1)} %get-tuple-element.63), channel_id=1, source_target_pairs={{0,16},{16,0},{1,17},{17,1},{2,18},{18,2},{3,19},{19,3},{4,20},{20... | collective-permute-start | bytes 2359304 | tf_op jit(solution)/shard_map/ppermute | solution.py:42
  30.8 33.4 %copy-start.2 = (bf16[64,3072]{1,0:T(8,128)(2,1)S(1)}, bf16[64,3072]{1,0:T(8,128)(2,1)}, u32[]{:S(2)}) copy-start(bf16[64,3072]{1,0:T(8,128)(2,1)} %refs_2_.1) | copy-start | bytes 1179652
  33.8 19.2 %collective-permute-start.1 = (bf16[128,1536]{1,0:T(8,128)(2,1)S(1)}, bf16[128,1536]{1,0:T(8,128)(2,1)S(1)}, u32[]{:S(2)}, u32[]{:S(2)}) collective-permute-start(bf16[128,1536]{1,0:T(8,128)(2,1)S(1)} %get-tuple-element.59), channel_id=1, source_target_pairs={{0,32},{32,64},{64,96},{96,0},{1,33},{33,65},{65,97},{97,1},{2,34}... | collective-permute-start | bytes 1179656 | tf_op jit(solution)/shard_map/ppermute | solution.py:38
  35.2 20.0 %collective-permute-start.2 = (bf16[128,1536]{1,0:T(8,128)(2,1)S(1)}, bf16[128,1536]{1,0:T(8,128)(2,1)S(1)}, u32[]{:S(2)}, u32[]{:S(2)}) collective-permute-start(bf16[128,1536]{1,0:T(8,128)(2,1)S(1)} %get-tuple-element.60), channel_id=1, source_target_pairs={{0,64},{32,96},{64,0},{96,32},{1,65},{33,97},{65,1},{97,33},{2,66}... | collective-permute-start | bytes 1179656 | tf_op jit(solution)/shard_map/ppermute | solution.py:38
  37.8 17.4 %collective-permute-start.3 = (bf16[128,1536]{1,0:T(8,128)(2,1)S(1)}, bf16[128,1536]{1,0:T(8,128)(2,1)S(1)}, u32[]{:S(2)}, u32[]{:S(2)}) collective-permute-start(bf16[128,1536]{1,0:T(8,128)(2,1)S(1)} %get-tuple-element.61), channel_id=1, source_target_pairs={{0,96},{32,0},{64,32},{96,64},{1,97},{33,1},{65,33},{97,65},{2,98}... | collective-permute-start | bytes 1179656 | tf_op jit(solution)/shard_map/ppermute | solution.py:38
  49.2 10.2 %collective-permute-start.7 = (bf16[64,1536]{1,0:T(8,128)(2,1)S(1)}, bf16[64,1536]{1,0:T(8,128)(2,1)S(1)}, u32[]{:S(2)}, u32[]{:S(2)}) collective-permute-start(bf16[64,1536]{1,0:T(8,128)(2,1)S(1)} %get-tuple-element.72), channel_id=1, source_target_pairs={{0,64},{32,96},{64,0},{96,32},{1,65},{33,97},{65,1},{97,33},{2,66}... | collective-permute-start | bytes 589832 | tf_op jit(solution)/shard_map/ppermute | solution.py:38
  52.2 10.8 %collective-permute-start.8 = (bf16[64,1536]{1,0:T(8,128)(2,1)S(1)}, bf16[64,1536]{1,0:T(8,128)(2,1)S(1)}, u32[]{:S(2)}, u32[]{:S(2)}) collective-permute-start(bf16[64,1536]{1,0:T(8,128)(2,1)S(1)} %get-tuple-element.73), channel_id=1, source_target_pairs={{0,96},{32,0},{64,32},{96,64},{1,97},{33,1},{65,33},{97,65},{2,98}... | collective-permute-start | bytes 589832 | tf_op jit(solution)/shard_map/ppermute | solution.py:38
  53.0 11.2 %collective-permute-start.6 = (bf16[64,1536]{1,0:T(8,128)(2,1)S(1)}, bf16[64,1536]{1,0:T(8,128)(2,1)S(1)}, u32[]{:S(2)}, u32[]{:S(2)}) collective-permute-start(bf16[64,1536]{1,0:T(8,128)(2,1)S(1)} %get-tuple-element.65), channel_id=1, source_target_pairs={{0,32},{32,64},{64,96},{96,0},{1,33},{33,65},{65,97},{97,1},{2,34}... | collective-permute-start | bytes 589832 | tf_op jit(solution)/shard_map/ppermute | solution.py:38
  55.4 13.8 %collective-permute-start.5 = (bf16[64,1536]{1,0:T(8,128)(2,1)S(1)}, bf16[64,1536]{1,0:T(8,128)(2,1)S(1)}, u32[]{:S(2)}, u32[]{:S(2)}) collective-permute-start(bf16[64,1536]{1,0:T(8,128)(2,1)S(1)} %get-tuple-element.70), channel_id=1, source_target_pairs={{0,16},{16,0},{1,17},{17,1},{2,18},{18,2},{3,19},{19,3},{4,20},{20... | collective-permute-start | bytes 589832 | tf_op jit(solution)/shard_map/ppermute | solution.py:42
  65.1 25.9 %copy-start.6 = (bf16[64,1536]{1,0:T(8,128)(2,1)}, bf16[64,1536]{1,0:T(8,128)(2,1)S(1)}, u32[]{:S(2)}) copy-start(bf16[64,1536]{1,0:T(8,128)(2,1)S(1)} %get-tuple-element.97.refs_0_.refs_1_) | copy-start | bytes 589828
  65.2 11.7 %collective-permute-start.16 = (bf16[64,1536]{1,0:T(8,128)(2,1)S(1)}, bf16[64,1536]{1,0:T(8,128)(2,1)S(1)}, u32[]{:S(2)}, u32[]{:S(2)}) collective-permute-start(bf16[64,1536]{1,0:T(8,128)(2,1)S(1)} %get-tuple-element.97.refs_0_.refs_1_), channel_id=1, source_target_pairs={{0,16},{16,0},{1,17},{17,1},{2,18},{18,2},{3,19},{19,3},{4,20},{20... | collective-permute-start | bytes 589832 | tf_op jit(solution)/shard_map/ppermute | solution.py:42
  65.2 7.6 %collective-permute-start.15 = (bf16[64,1536]{1,0:T(8,128)(2,1)S(1)}, bf16[64,1536]{1,0:T(8,128)(2,1)S(1)}, u32[]{:S(2)}, u32[]{:S(2)}) collective-permute-start(bf16[64,1536]{1,0:T(8,128)(2,1)S(1)} %get-tuple-element.97.refs_0_.refs_1_), channel_id=1, source_target_pairs={{0,32},{32,64},{64,96},{96,0},{1,33},{33,65},{65,97},{97,1},{2,34}... | collective-permute-start | bytes 589832 | tf_op jit(solution)/shard_map/ppermute | solution.py:38
  66.3 13.0 %collective-permute-start.14 = (bf16[64,1536]{1,0:T(8,128)(2,1)S(1)}, bf16[64,1536]{1,0:T(8,128)(2,1)S(1)}, u32[]{:S(2)}, u32[]{:S(2)}) collective-permute-start(bf16[64,1536]{1,0:T(8,128)(2,1)S(1)} %get-tuple-element.97.refs_0_.refs_1_), channel_id=1, source_target_pairs={{0,64},{32,96},{64,0},{96,32},{1,65},{33,97},{65,1},{97,33},{2,66}... | collective-permute-start | bytes 589832 | tf_op jit(solution)/shard_map/ppermute | solution.py:38
  70.1 6.6 %collective-permute-start.9 = (bf16[64,1536]{1,0:T(8,128)(2,1)S(1)}, bf16[64,1536]{1,0:T(8,128)(2,1)S(1)}, u32[]{:S(2)}, u32[]{:S(2)}) collective-permute-start(bf16[64,1536]{1,0:T(8,128)(2,1)S(1)} %get-tuple-element.78), channel_id=1, source_target_pairs={{0,16},{16,0},{1,17},{17,1},{2,18},{18,2},{3,19},{19,3},{4,20},{20... | collective-permute-start | bytes 589832 | tf_op jit(solution)/shard_map/ppermute | solution.py:42
  72.2 7.5 %collective-permute-start.13 = (bf16[64,1536]{1,0:T(8,128)(2,1)S(1)}, bf16[64,1536]{1,0:T(8,128)(2,1)S(1)}, u32[]{:S(2)}, u32[]{:S(2)}) collective-permute-start(bf16[64,1536]{1,0:T(8,128)(2,1)S(1)} %get-tuple-element.97.refs_0_.refs_1_), channel_id=1, source_target_pairs={{0,96},{32,0},{64,32},{96,64},{1,97},{33,1},{65,33},{97,65},{2,98}... | collective-permute-start | bytes 589832 | tf_op jit(solution)/shard_map/ppermute | solution.py:38
  72.8 8.8 %collective-permute-start.19 = (bf16[64,1536]{1,0:T(8,128)(2,1)S(1)}, bf16[64,1536]{1,0:T(8,128)(2,1)S(1)}, u32[]{:S(2)}, u32[]{:S(2)}) collective-permute-start(bf16[64,1536]{1,0:T(8,128)(2,1)S(1)} %collective-permute-done.15.refs_3_.refs_4_), channel_id=1, source_target_pairs={{0,16},{16,0},{1,17},{17,1},{2,18},{18,2},{3,19},{19,3},{4,20},{20... | collective-permute-start | bytes 589832 | tf_op jit(solution)/shard_map/ppermute | solution.py:42
  76.8 14.4 %collective-permute-start.12 = (bf16[128,1536]{1,0:T(8,128)(2,1)S(1)}, bf16[128,1536]{1,0:T(8,128)(2,1)S(1)}, u32[]{:S(2)}, u32[]{:S(2)}) collective-permute-start(bf16[128,1536]{1,0:T(8,128)(2,1)S(1)} %constant_dynamic-update-slice_fusion.2.refs_0_.refs_9_), channel_id=1, source_target_pairs={{0,32},{32,64},{64,96},{96,0},{1,33},{33,65},{65,97},{97,1},{2,34}... | collective-permute-start | bytes 1179656 | tf_op jit(solution)/shard_map/ppermute | solution.py:38
  76.9 16.0 %collective-permute-start.11 = (bf16[128,1536]{1,0:T(8,128)(2,1)S(1)}, bf16[128,1536]{1,0:T(8,128)(2,1)S(1)}, u32[]{:S(2)}, u32[]{:S(2)}) collective-permute-start(bf16[128,1536]{1,0:T(8,128)(2,1)S(1)} %constant_dynamic-update-slice_fusion.2.refs_0_.refs_9_), channel_id=1, source_target_pairs={{0,64},{32,96},{64,0},{96,32},{1,65},{33,97},{65,1},{97,33},{2,66}... | collective-permute-start | bytes 1179656 | tf_op jit(solution)/shard_map/ppermute | solution.py:38
  79.3 17.7 %collective-permute-start.10 = (bf16[128,1536]{1,0:T(8,128)(2,1)S(1)}, bf16[128,1536]{1,0:T(8,128)(2,1)S(1)}, u32[]{:S(2)}, u32[]{:S(2)}) collective-permute-start(bf16[128,1536]{1,0:T(8,128)(2,1)S(1)} %constant_dynamic-update-slice_fusion.2.refs_0_.refs_9_), channel_id=1, source_target_pairs={{0,96},{32,0},{64,32},{96,64},{1,97},{33,1},{65,33},{97,65},{2,98}... | collective-permute-start | bytes 1179656 | tf_op jit(solution)/shard_map/ppermute | solution.py:38
  79.8 6.0 %collective-permute-start.18 = (bf16[64,1536]{1,0:T(8,128)(2,1)S(1)}, bf16[64,1536]{1,0:T(8,128)(2,1)S(1)}, u32[]{:S(2)}, u32[]{:S(2)}) collective-permute-start(bf16[64,1536]{1,0:T(8,128)(2,1)S(1)} %collective-permute-done.14.refs_2_.refs_3_), channel_id=1, source_target_pairs={{0,16},{16,0},{1,17},{17,1},{2,18},{18,2},{3,19},{19,3},{4,20},{20... | collective-permute-start | bytes 589832 | tf_op jit(solution)/shard_map/ppermute | solution.py:42
  81.7 6.2 %collective-permute-start.17 = (bf16[64,1536]{1,0:T(8,128)(2,1)S(1)}, bf16[64,1536]{1,0:T(8,128)(2,1)S(1)}, u32[]{:S(2)}, u32[]{:S(2)}) collective-permute-start(bf16[64,1536]{1,0:T(8,128)(2,1)S(1)} %collective-permute-done.13.refs_1_.refs_2_), channel_id=1, source_target_pairs={{0,16},{16,0},{1,17},{17,1},{2,18},{18,2},{3,19},{19,3},{4,20},{20... | collective-permute-start | bytes 589832 | tf_op jit(solution)/shard_map/ppermute | solution.py:42
  99.4 4.2 %collective-permute-start.20 = (bf16[8,32,1536]{2,1,0:T(8,128)(2,1)S(1)}, bf16[8,32,1536]{2,1,0:T(8,128)(2,1)S(1)}, u32[]{:S(2)}, u32[]{:S(2)}) collective-permute-start(bf16[8,32,1536]{2,1,0:T(8,128)(2,1)S(1)} %backward_other.1), channel_id=1, source_target_pairs={{0,1},{1,0},{2,3},{3,2},{4,5},{5,4},{6,7},{7,6},{8,9},{9,8},{10,11... | collective-permute-start | bytes 2359304 | tf_op jit(solution)/shard_map/ppermute | solution.py:46
  104.6 15.7 %all-to-all-start.1 = ((bf16[8,32,1536]{2,1,0:T(8,128)(2,1)}), bf16[8,32,1536]{2,1,0:T(8,128)(2,1)S(1)}, u32[]{:S(2)}, u32[]{:S(2)}) async-start(bf16[8,32,1536]{2,1,0:T(8,128)(2,1)} %chip_sum.1), calls=%async_computation.1 | async-start | bytes 1572864 | tf_op jit(solution)/shard_map/all_to_all | solution.py:483
  (16 other events, 159.1 us)

commit v7 on v6

--- a/solution.py
+++ b/solution.py
@@ -459,7 +459,7 @@
     by_y += [ahead(late_b if d == 1 else grad_b, -d) for d in (1, 2, 3)]
     by_y_far = [across(grad) for grad in by_y]
     both = jnp.concatenate([grad_a, across(grad_a)], axis=0)
-    wide = [both] + [ahead(both, -d) for d in (1, 2, 3)]
+    wide = [both] + [ahead(after(both, by_y[2]) if d == 2 else both, -d) for d in (1, 2, 3)]
     turned = turn(after(toks, both))
     activated = jnp.concatenate([act_a, act_b], axis=1)
 

time: 121 us -> 121 us (level)
  waiting for transfers between devices: 33.2 us -> 29.9 us
  starting transfers between devices: 36.1 us -> 38.8 us
    ppermute x2, starting transfers between devices: 4.11 us -> 7.59 us  [other_core(): return lax.ppermute(array, 'c', SWAP)]
    ppermute x12, waiting for transfers between devices: 15.1 us -> 12 us  [ahead(): lax.ppermute(array, 'y', [(i, (i + distance) % N_Y) for i in range(N_Y)])]
where the time goes in v7:
time: 121 us; the launch traced here: 120 us
  starting transfers between devices  38.8 us (32%)
  Pallas kernels  31.5 us (26%)
  waiting for transfers between devices  29.9 us (25%)
  blocking collectives  18.1 us (15%)
    pallas_call x14, Pallas kernels, call(): pl.pallas_call(kernel, out_shape=[jax.ShapeDtypeStruct(shape, dtype) for...  31.5 us
    all_to_all x1, blocking collectives, local(): own = lax.all_to_all(spread, PLANE, 0, 0, tiled=True)  18.1 us
    ppermute x12, starting transfers between devices, ahead(): lax.ppermute(array, 'y', [(i, (i + distance) % N_Y) for i in range(N_Y)])  16 us
    ppermute x7, waiting for transfers between devices, across(): return lax.ppermute(array, 'xh', SWAP)  15.8 us
    ppermute x12, waiting for transfers between devices, ahead(): lax.ppermute(array, 'y', [(i, (i + distance) % N_Y) for i in range(N_Y)])  12 us
    ppermute x7, starting transfers between devices, across(): return lax.ppermute(array, 'xh', SWAP)  11.6 us
    ppermute x2, starting transfers between devices, other_core(): return lax.ppermute(array, 'c', SWAP)  7.59 us
    all_to_all x1, starting transfers between devices, local(): last = lax.all_to_all(chip, PLANE, 0, 0, tiled=True)  3.55 us
  transfers between devices with their start and end apart: 22, of which 11 were waited for; matrix products, arithmetic and copies ran while one was open for 0% of the time, Pallas kernels for 20%

profile of v7, /device:TPU:1, one launch (start us, length us, event | category | flops | bytes accessed | tf_op | source)
XLA Modules:
  0.0 120.4 jit_solution(2354606619220801914)
XLA Ops:
  1.6 18.1 %all_to_all.10.own = bf16[8,32,1536]{2,1,0:T(8,128)(2,1)S(1)} all-to-all(bf16[8,32,1536]{2,1,0:T(8,128)(2,1)S(1)} %broadcast_in_dim.2), channel_id=1, replica_groups=mesh['y'=4,'xh'=2,'xl'=2,'z'=4,'c'=2] {'xl','z'}, dimensions={0} | all-to-all | bytes 1572864 | tf_op jit(solution)/shard_map/all_to_all | solution.py:423
  19.7 2.4 %collective-permute-start = (bf16[8,32,1536]{2,1,0:T(8,128)(2,1)S(1)}, bf16[8,32,1536]{2,1,0:T(8,128)(2,1)S(1)}, u32[]{:S(2)}, u32[]{:S(2)}) collective-permute-start(bf16[8,32,1536]{2,1,0:T(8,128)(2,1)S(1)} %all_to_all.10.own), channel_id=1, source_target_pairs={{0,1},{1,0},{2,3},{3,2},{4,5},{5,4},{6,7},{7,6},{8,9},{9,8},{10,11... | collective-permute-start | bytes 2359304 | tf_op jit(solution)/shard_map/ppermute | solution.py:46
  22.1 2.5 %load_forward.1.weight = bf16[1536,1536]{1,0:T(8,128)(2,1)S(1)} custom-call(bf16[1536,3072]{1,0:T(8,128)(2,1)} %refs_4_.5), custom_call_target="tpu_custom_call" | custom-call | bytes 9437184 | tf_op jit(solution)/shard_map/load_forward/pallas_call | solution.py:62
  24.7 3.6 %forward_side.1 = (bf16[512,1536]{1,0:T(8,128)(2,1)S(1)}, bf16[256,1536]{1,0:T(8,128)(2,1)S(1)}, bf16[256,1536]{1,0:T(8,128)(2,1)S(1)}) custom-call(s32[3]{0:T(128)S(1)} %pad_add_fusion.place, bf16[8,32,1536]{2,1,0:T(8,128)(2,1)S(1)} %all_to_all.10.own, bf16[8,32,1536]{2,1,0:T(8,128)(2,1)S(1)} %collective-permute-done.other, ...), custom_call_target="tpu_custom_call" | custom-call | flops 2415919104 | bytes 4718592 | tf_op jit(solution)/shard_map/forward_side/pallas_call | solution.py:62
  28.3 2.5 %collective-permute-start.4 = (bf16[256,1536]{1,0:T(8,128)(2,1)S(1)}, bf16[256,1536]{1,0:T(8,128)(2,1)S(1)}, u32[]{:S(2)}, u32[]{:S(2)}) collective-permute-start(bf16[256,1536]{1,0:T(8,128)(2,1)S(1)} %get-tuple-element.64), channel_id=1, source_target_pairs={{0,16},{16,0},{1,17},{17,1},{2,18},{18,2},{3,19},{19,3},{4,20},{20... | collective-permute-start | bytes 2359304 | tf_op jit(solution)/shard_map/ppermute | solution.py:42
  30.8 3.0 %forward_distance.1 = (bf16[128,1536]{1,0:T(8,128)(2,1)S(1)}, bf16[128,1536]{1,0:T(8,128)(2,1)S(1)}, bf16[128,1536]{1,0:T(8,128)(2,1)S(1)}, bf16[128,1536]{1,0:T(8,128)(2,1)S(1)}) custom-call(bf16[512,1536]{1,0:T(8,128)(2,1)S(1)} %get-tuple-element.82.toks.tok, bf16[1536,3072]{1,0:T(8,128)(2,1)S(1)} %bitcast.4), custom_call_target="tpu_custom_call" | custom-call | flops 2415919104 | bytes 4718592 | tf_op jit(solution)/shard_map/forward_distance/pallas_call | solution.py:62
  35.2 2.6 %collective-permute-start.2 = (bf16[128,1536]{1,0:T(8,128)(2,1)S(1)}, bf16[128,1536]{1,0:T(8,128)(2,1)S(1)}, u32[]{:S(2)}, u32[]{:S(2)}) collective-permute-start(bf16[128,1536]{1,0:T(8,128)(2,1)S(1)} %get-tuple-element.61), channel_id=1, source_target_pairs={{0,64},{32,96},{64,0},{96,32},{1,65},{33,97},{65,1},{97,33},{2,66}... | collective-permute-start | bytes 1179656 | tf_op jit(solution)/shard_map/ppermute | solution.py:38
  38.9 10.1 %collective-permute-done.4.got = bf16[256,1536]{1,0:T(8,128)(2,1)S(1)} collective-permute-done((bf16[256,1536]{1,0:T(8,128)(2,1)S(1)}, bf16[256,1536]{1,0:T(8,128)(2,1)S(1)}, u32[]{:S(2)}, u32[]{:S(2)}) %collective-permute-start.4) | collective-permute-done | bytes 786464 | tf_op jit(solution)/shard_map/ppermute | solution.py:42
  49.2 3.0 %collective-permute-start.7 = (bf16[64,1536]{1,0:T(8,128)(2,1)S(1)}, bf16[64,1536]{1,0:T(8,128)(2,1)S(1)}, u32[]{:S(2)}, u32[]{:S(2)}) collective-permute-start(bf16[64,1536]{1,0:T(8,128)(2,1)S(1)} %get-tuple-element.73), channel_id=1, source_target_pairs={{0,64},{32,96},{64,0},{96,32},{1,65},{33,97},{65,1},{97,33},{2,66}... | collective-permute-start | bytes 589832 | tf_op jit(solution)/shard_map/ppermute | solution.py:38
  56.4 3.0 %collective-permute-done.7.refs_2_ = bf16[64,1536]{1,0:T(8,128)(2,1)S(1)} collective-permute-done((bf16[64,1536]{1,0:T(8,128)(2,1)S(1)}, bf16[64,1536]{1,0:T(8,128)(2,1)S(1)}, u32[]{:S(2)}, u32[]{:S(2)}) %collective-permute-start.7) | collective-permute-done | bytes 196640 | tf_op jit(solution)/shard_map/ppermute | solution.py:38
  59.5 3.6 %collective-permute-done.8.refs_3_ = bf16[64,1536]{1,0:T(8,128)(2,1)S(1)} collective-permute-done((bf16[64,1536]{1,0:T(8,128)(2,1)S(1)}, bf16[64,1536]{1,0:T(8,128)(2,1)S(1)}, u32[]{:S(2)}, u32[]{:S(2)}) %collective-permute-start.8) | collective-permute-done | bytes 196640 | tf_op jit(solution)/shard_map/ppermute | solution.py:38
  66.3 2.9 %collective-permute-start.11 = (bf16[64,1536]{1,0:T(8,128)(2,1)S(1)}, bf16[64,1536]{1,0:T(8,128)(2,1)S(1)}, u32[]{:S(2)}, u32[]{:S(2)}) collective-permute-start(bf16[64,1536]{1,0:T(8,128)(2,1)S(1)} %get-tuple-element.99.refs_0_.refs_1_), channel_id=1, source_target_pairs={{0,64},{32,96},{64,0},{96,32},{1,65},{33,97},{65,1},{97,33},{2,66}... | collective-permute-start | bytes 589832 | tf_op jit(solution)/shard_map/ppermute | solution.py:38
  70.1 2.1 %collective-permute-start.9 = (bf16[64,1536]{1,0:T(8,128)(2,1)S(1)}, bf16[64,1536]{1,0:T(8,128)(2,1)S(1)}, u32[]{:S(2)}, u32[]{:S(2)}) collective-permute-start(bf16[64,1536]{1,0:T(8,128)(2,1)S(1)} %get-tuple-element.79), channel_id=1, source_target_pairs={{0,16},{16,0},{1,17},{17,1},{2,18},{18,2},{3,19},{19,3},{4,20},{20... | collective-permute-start | bytes 589832 | tf_op jit(solution)/shard_map/ppermute | solution.py:42
  72.8 2.2 %collective-permute-start.19 = (bf16[64,1536]{1,0:T(8,128)(2,1)S(1)}, bf16[64,1536]{1,0:T(8,128)(2,1)S(1)}, u32[]{:S(2)}, u32[]{:S(2)}) collective-permute-start(bf16[64,1536]{1,0:T(8,128)(2,1)S(1)} %collective-permute-done.15.refs_3_.refs_4_), channel_id=1, source_target_pairs={{0,16},{16,0},{1,17},{17,1},{2,18},{18,2},{3,19},{19,3},{4,20},{20... | collective-permute-start | bytes 589832 | tf_op jit(solution)/shard_map/ppermute | solution.py:42
  77.6 1.9 %collective-permute-start.10 = (bf16[128,1536]{1,0:T(8,128)(2,1)S(1)}, bf16[128,1536]{1,0:T(8,128)(2,1)S(1)}, u32[]{:S(2)}, u32[]{:S(2)}) collective-permute-start(bf16[128,1536]{1,0:T(8,128)(2,1)S(1)} %constant_dynamic-update-slice_fusion.2.refs_0_.refs_9_), channel_id=1, source_target_pairs={{0,96},{32,0},{64,32},{96,64},{1,97},{33,1},{65,33},{97,65},{2,98}... | collective-permute-start | bytes 1179656 | tf_op jit(solution)/shard_map/ppermute | solution.py:38
  79.6 2.1 %collective-permute-start.18 = (bf16[64,1536]{1,0:T(8,128)(2,1)S(1)}, bf16[64,1536]{1,0:T(8,128)(2,1)S(1)}, u32[]{:S(2)}, u32[]{:S(2)}) collective-permute-start(bf16[64,1536]{1,0:T(8,128)(2,1)S(1)} %collective-permute-done.11.refs_2_.refs_3_), channel_id=1, source_target_pairs={{0,16},{16,0},{1,17},{17,1},{2,18},{18,2},{3,19},{19,3},{4,20},{20... | collective-permute-start | bytes 589832 | tf_op jit(solution)/shard_map/ppermute | solution.py:42
  85.7 2.1 %collective-permute-done.17.refs_5_.refs_6_ = bf16[64,1536]{1,0:T(8,128)(2,1)S(1)} collective-permute-done((bf16[64,1536]{1,0:T(8,128)(2,1)S(1)}, bf16[64,1536]{1,0:T(8,128)(2,1)S(1)}, u32[]{:S(2)}, u32[]{:S(2)}) %collective-permute-start.17) | collective-permute-done | bytes 196640 | tf_op jit(solution)/shard_map/ppermute | solution.py:42
  87.8 3.1 %backward_first.1.refs_5_ = f32[512,1536]{1,0:T(8,128)S(1)} custom-call(bf16[64,1536]{1,0:T(8,128)(2,1)S(1)} %get-tuple-element.99.refs_0_.refs_1_, bf16[64,1536]{1,0:T(8,128)(2,1)S(1)} %collective-permute-done.14.refs_1_.refs_2_, bf16[64,1536]{1,0:T(8,128)(2,1)S(1)} %collective-permute-done.11.refs_2_.refs_3_, ...), custom_call_target="tpu_custom_call" | custom-call | flops 2415919104 | bytes 4718592 | tf_op jit(solution)/shard_map/backward_first/pallas_call | solution.py:62
  92.9 2.4 %backward_other.1 = bf16[8,32,1536]{2,1,0:T(8,128)(2,1)S(1)} custom-call(s32[3]{0:T(128)S(1)} %pad_add_fusion.place, bf16[128,1536]{1,0:T(8,128)(2,1)S(1)} %constant_dynamic-update-slice_fusion.2.refs_0_.refs_9_, bf16[128,1536]{1,0:T(8,128)(2,1)S(1)} %collective-permute-done.10.refs_1_.refs_10_, ...), custom_call_target="tpu_custom_call" | custom-call | flops 1207959552 | bytes 4718592 | tf_op jit(solution)/shard_map/backward_other/pallas_call | solution.py:62
  95.3 5.2 %collective-permute-start.20 = (bf16[8,32,1536]{2,1,0:T(8,128)(2,1)S(1)}, bf16[8,32,1536]{2,1,0:T(8,128)(2,1)S(1)}, u32[]{:S(2)}, u32[]{:S(2)}) collective-permute-start(bf16[8,32,1536]{2,1,0:T(8,128)(2,1)S(1)} %backward_other.1), channel_id=1, source_target_pairs={{0,1},{1,0},{2,3},{3,2},{4,5},{5,4},{6,7},{7,6},{8,9},{9,8},{10,11... | collective-permute-start | bytes 2359304 | tf_op jit(solution)/shard_map/ppermute | solution.py:46
  100.5 2.4 %backward_own.1.mine = bf16[8,32,1536]{2,1,0:T(8,128)(2,1)S(1)} custom-call(s32[3]{0:T(128)S(1)} %pad_add_fusion.place, bf16[128,1536]{1,0:T(8,128)(2,1)S(1)} %constant_dynamic-update-slice_fusion.2.refs_0_.refs_9_, bf16[128,1536]{1,0:T(8,128)(2,1)S(1)} %collective-permute-done.10.refs_1_.refs_10_, ...), custom_call_target="tpu_custom_call" | custom-call | flops 1207959552 | bytes 4718592 | tf_op jit(solution)/shard_map/backward_own/pallas_call | solution.py:62
  103.9 3.5 %all-to-all-start.1 = ((bf16[8,32,1536]{2,1,0:T(8,128)(2,1)}), bf16[8,32,1536]{2,1,0:T(8,128)(2,1)S(1)}, u32[]{:S(2)}, u32[]{:S(2)}) async-start(bf16[8,32,1536]{2,1,0:T(8,128)(2,1)} %chip_sum.1), calls=%async_computation.1 | async-start | bytes 1572864 | tf_op jit(solution)/shard_map/all_to_all | solution.py:483
  107.5 10.0 %weight_grad.1 = bf16[1536,3072]{1,0:T(8,128)(2,1)} custom-call(bf16[1536,512]{1,0:T(8,128)(2,1)} %copy-done.1, bf16[64,1536]{1,0:T(8,128)(2,1)} %copy-done.6, bf16[64,1536]{1,0:T(8,128)(2,1)} %copy-done.10, bf16[64,1536]{1,0:T(8,128)(2,1)} %copy-done.9, bf16[64,1536]{1,0:T(8,128)(2,1)} %copy-done.8, bf16[64,1536]{1,0:T(8,128)(2,1)} %copy-done.7, ...), custom_call_target="tpu_custom_call" | custom-call | flops 4831838208 | bytes 9437184 | tf_op jit(solution)/shard_map/weight_grad/pallas_call | solution.py:62
  117.5 2.2 %all-to-all-done.1.got = bf16[8,32,1536]{2,1,0:T(8,128)(2,1)S(1)} async-done(((bf16[8,32,1536]{2,1,0:T(8,128)(2,1)}), bf16[8,32,1536]{2,1,0:T(8,128)(2,1)S(1)}, u32[]{:S(2)}, u32[]{:S(2)}) %all-to-all-start.1) | async-done | bytes 786464 | tf_op jit(solution)/shard_map/all_to_all | solution.py:483
  (78 shorter events, 22.7 us)
Async XLA Ops:
  19.7 5.0 %collective-permute-start = (bf16[8,32,1536]{2,1,0:T(8,128)(2,1)S(1)}, bf16[8,32,1536]{2,1,0:T(8,128)(2,1)S(1)}, u32[]{:S(2)}, u32[]{:S(2)}) collective-permute-start(bf16[8,32,1536]{2,1,0:T(8,128)(2,1)S(1)} %all_to_all.10.own), channel_id=1, source_target_pairs={{0,1},{1,0},{2,3},{3,2},{4,5},{5,4},{6,7},{7,6},{8,9},{9,8},{10,11... | collective-permute-start | bytes 2359304 | tf_op jit(solution)/shard_map/ppermute | solution.py:46
  28.3 20.8 %collective-permute-start.4 = (bf16[256,1536]{1,0:T(8,128)(2,1)S(1)}, bf16[256,1536]{1,0:T(8,128)(2,1)S(1)}, u32[]{:S(2)}, u32[]{:S(2)}) collective-permute-start(bf16[256,1536]{1,0:T(8,128)(2,1)S(1)} %get-tuple-element.64), channel_id=1, source_target_pairs={{0,16},{16,0},{1,17},{17,1},{2,18},{18,2},{3,19},{19,3},{4,20},{20... | collective-permute-start | bytes 2359304 | tf_op jit(solution)/shard_map/ppermute | solution.py:42
  30.8 33.4 %copy-start.2 = (bf16[64,3072]{1,0:T(8,128)(2,1)S(1)}, bf16[64,3072]{1,0:T(8,128)(2,1)}, u32[]{:S(2)}) copy-start(bf16[64,3072]{1,0:T(8,128)(2,1)} %refs_2_.1) | copy-start | bytes 1179652
  33.8 19.2 %collective-permute-start.1 = (bf16[128,1536]{1,0:T(8,128)(2,1)S(1)}, bf16[128,1536]{1,0:T(8,128)(2,1)S(1)}, u32[]{:S(2)}, u32[]{:S(2)}) collective-permute-start(bf16[128,1536]{1,0:T(8,128)(2,1)S(1)} %get-tuple-element.60), channel_id=1, source_target_pairs={{0,32},{32,64},{64,96},{96,0},{1,33},{33,65},{65,97},{97,1},{2,34}... | collective-permute-start | bytes 1179656 | tf_op jit(solution)/shard_map/ppermute | solution.py:38
  35.2 20.0 %collective-permute-start.2 = (bf16[128,1536]{1,0:T(8,128)(2,1)S(1)}, bf16[128,1536]{1,0:T(8,128)(2,1)S(1)}, u32[]{:S(2)}, u32[]{:S(2)}) collective-permute-start(bf16[128,1536]{1,0:T(8,128)(2,1)S(1)} %get-tuple-element.61), channel_id=1, source_target_pairs={{0,64},{32,96},{64,0},{96,32},{1,65},{33,97},{65,1},{97,33},{2,66}... | collective-permute-start | bytes 1179656 | tf_op jit(solution)/shard_map/ppermute | solution.py:38
  37.8 17.4 %collective-permute-start.3 = (bf16[128,1536]{1,0:T(8,128)(2,1)S(1)}, bf16[128,1536]{1,0:T(8,128)(2,1)S(1)}, u32[]{:S(2)}, u32[]{:S(2)}) collective-permute-start(bf16[128,1536]{1,0:T(8,128)(2,1)S(1)} %get-tuple-element.62), channel_id=1, source_target_pairs={{0,96},{32,0},{64,32},{96,64},{1,97},{33,1},{65,33},{97,65},{2,98}... | collective-permute-start | bytes 1179656 | tf_op jit(solution)/shard_map/ppermute | solution.py:38
  49.2 10.2 %collective-permute-start.7 = (bf16[64,1536]{1,0:T(8,128)(2,1)S(1)}, bf16[64,1536]{1,0:T(8,128)(2,1)S(1)}, u32[]{:S(2)}, u32[]{:S(2)}) collective-permute-start(bf16[64,1536]{1,0:T(8,128)(2,1)S(1)} %get-tuple-element.73), channel_id=1, source_target_pairs={{0,64},{32,96},{64,0},{96,32},{1,65},{33,97},{65,1},{97,33},{2,66}... | collective-permute-start | bytes 589832 | tf_op jit(solution)/shard_map/ppermute | solution.py:38
  52.2 10.8 %collective-permute-start.8 = (bf16[64,1536]{1,0:T(8,128)(2,1)S(1)}, bf16[64,1536]{1,0:T(8,128)(2,1)S(1)}, u32[]{:S(2)}, u32[]{:S(2)}) collective-permute-start(bf16[64,1536]{1,0:T(8,128)(2,1)S(1)} %get-tuple-element.74), channel_id=1, source_target_pairs={{0,96},{32,0},{64,32},{96,64},{1,97},{33,1},{65,33},{97,65},{2,98}... | collective-permute-start | bytes 589832 | tf_op jit(solution)/shard_map/ppermute | solution.py:38
  53.0 11.2 %collective-permute-start.6 = (bf16[64,1536]{1,0:T(8,128)(2,1)S(1)}, bf16[64,1536]{1,0:T(8,128)(2,1)S(1)}, u32[]{:S(2)}, u32[]{:S(2)}) collective-permute-start(bf16[64,1536]{1,0:T(8,128)(2,1)S(1)} %get-tuple-element.66), channel_id=1, source_target_pairs={{0,32},{32,64},{64,96},{96,0},{1,33},{33,65},{65,97},{97,1},{2,34}... | collective-permute-start | bytes 589832 | tf_op jit(solution)/shard_map/ppermute | solution.py:38
  55.4 13.8 %collective-permute-start.5 = (bf16[64,1536]{1,0:T(8,128)(2,1)S(1)}, bf16[64,1536]{1,0:T(8,128)(2,1)S(1)}, u32[]{:S(2)}, u32[]{:S(2)}) collective-permute-start(bf16[64,1536]{1,0:T(8,128)(2,1)S(1)} %get-tuple-element.71), channel_id=1, source_target_pairs={{0,16},{16,0},{1,17},{17,1},{2,18},{18,2},{3,19},{19,3},{4,20},{20... | collective-permute-start | bytes 589832 | tf_op jit(solution)/shard_map/ppermute | solution.py:42
  65.1 25.8 %copy-start.6 = (bf16[64,1536]{1,0:T(8,128)(2,1)}, bf16[64,1536]{1,0:T(8,128)(2,1)S(1)}, u32[]{:S(2)}) copy-start(bf16[64,1536]{1,0:T(8,128)(2,1)S(1)} %get-tuple-element.99.refs_0_.refs_1_) | copy-start | bytes 589828
  65.2 14.4 %collective-permute-start.16 = (bf16[64,1536]{1,0:T(8,128)(2,1)S(1)}, bf16[64,1536]{1,0:T(8,128)(2,1)S(1)}, u32[]{:S(2)}, u32[]{:S(2)}) collective-permute-start(bf16[64,1536]{1,0:T(8,128)(2,1)S(1)} %get-tuple-element.99.refs_0_.refs_1_), channel_id=1, source_target_pairs={{0,16},{16,0},{1,17},{17,1},{2,18},{18,2},{3,19},{19,3},{4,20},{20... | collective-permute-start | bytes 589832 | tf_op jit(solution)/shard_map/ppermute | solution.py:42
  65.2 7.6 %collective-permute-start.15 = (bf16[64,1536]{1,0:T(8,128)(2,1)S(1)}, bf16[64,1536]{1,0:T(8,128)(2,1)S(1)}, u32[]{:S(2)}, u32[]{:S(2)}) collective-permute-start(bf16[64,1536]{1,0:T(8,128)(2,1)S(1)} %get-tuple-element.99.refs_0_.refs_1_), channel_id=1, source_target_pairs={{0,32},{32,64},{64,96},{96,0},{1,33},{33,65},{65,97},{97,1},{2,34}... | collective-permute-start | bytes 589832 | tf_op jit(solution)/shard_map/ppermute | solution.py:38
  66.3 11.3 %collective-permute-start.11 = (bf16[64,1536]{1,0:T(8,128)(2,1)S(1)}, bf16[64,1536]{1,0:T(8,128)(2,1)S(1)}, u32[]{:S(2)}, u32[]{:S(2)}) collective-permute-start(bf16[64,1536]{1,0:T(8,128)(2,1)S(1)} %get-tuple-element.99.refs_0_.refs_1_), channel_id=1, source_target_pairs={{0,64},{32,96},{64,0},{96,32},{1,65},{33,97},{65,1},{97,33},{2,66}... | collective-permute-start | bytes 589832 | tf_op jit(solution)/shard_map/ppermute | solution.py:38
  70.1 6.6 %collective-permute-start.9 = (bf16[64,1536]{1,0:T(8,128)(2,1)S(1)}, bf16[64,1536]{1,0:T(8,128)(2,1)S(1)}, u32[]{:S(2)}, u32[]{:S(2)}) collective-permute-start(bf16[64,1536]{1,0:T(8,128)(2,1)S(1)} %get-tuple-element.79), channel_id=1, source_target_pairs={{0,16},{16,0},{1,17},{17,1},{2,18},{18,2},{3,19},{19,3},{4,20},{20... | collective-permute-start | bytes 589832 | tf_op jit(solution)/shard_map/ppermute | solution.py:42
  72.2 7.3 %collective-permute-start.14 = (bf16[64,1536]{1,0:T(8,128)(2,1)S(1)}, bf16[64,1536]{1,0:T(8,128)(2,1)S(1)}, u32[]{:S(2)}, u32[]{:S(2)}) collective-permute-start(bf16[64,1536]{1,0:T(8,128)(2,1)S(1)} %get-tuple-element.99.refs_0_.refs_1_), channel_id=1, source_target_pairs={{0,96},{32,0},{64,32},{96,64},{1,97},{33,1},{65,33},{97,65},{2,98}... | collective-permute-start | bytes 589832 | tf_op jit(solution)/shard_map/ppermute | solution.py:38
  72.8 8.9 %collective-permute-start.19 = (bf16[64,1536]{1,0:T(8,128)(2,1)S(1)}, bf16[64,1536]{1,0:T(8,128)(2,1)S(1)}, u32[]{:S(2)}, u32[]{:S(2)}) collective-permute-start(bf16[64,1536]{1,0:T(8,128)(2,1)S(1)} %collective-permute-done.15.refs_3_.refs_4_), channel_id=1, source_target_pairs={{0,16},{16,0},{1,17},{17,1},{2,18},{18,2},{3,19},{19,3},{4,20},{20... | collective-permute-start | bytes 589832 | tf_op jit(solution)/shard_map/ppermute | solution.py:42
  76.8 16.1 %collective-permute-start.13 = (bf16[128,1536]{1,0:T(8,128)(2,1)S(1)}, bf16[128,1536]{1,0:T(8,128)(2,1)S(1)}, u32[]{:S(2)}, u32[]{:S(2)}) collective-permute-start(bf16[128,1536]{1,0:T(8,128)(2,1)S(1)} %constant_dynamic-update-slice_fusion.2.refs_0_.refs_9_), channel_id=1, source_target_pairs={{0,32},{32,64},{64,96},{96,0},{1,33},{33,65},{65,97},{97,1},{2,34}... | collective-permute-start | bytes 1179656 | tf_op jit(solution)/shard_map/ppermute | solution.py:38
  77.6 15.3 %collective-permute-start.10 = (bf16[128,1536]{1,0:T(8,128)(2,1)S(1)}, bf16[128,1536]{1,0:T(8,128)(2,1)S(1)}, u32[]{:S(2)}, u32[]{:S(2)}) collective-permute-start(bf16[128,1536]{1,0:T(8,128)(2,1)S(1)} %constant_dynamic-update-slice_fusion.2.refs_0_.refs_9_), channel_id=1, source_target_pairs={{0,96},{32,0},{64,32},{96,64},{1,97},{33,1},{65,33},{97,65},{2,98}... | collective-permute-start | bytes 1179656 | tf_op jit(solution)/shard_map/ppermute | solution.py:38
  79.5 13.4 %collective-permute-start.12 = (bf16[128,1536]{1,0:T(8,128)(2,1)S(1)}, bf16[128,1536]{1,0:T(8,128)(2,1)S(1)}, u32[]{:S(2)}, u32[]{:S(2)}) collective-permute-start(bf16[128,1536]{1,0:T(8,128)(2,1)S(1)} %constant_dynamic-update-slice_fusion.2.refs_0_.refs_9_), channel_id=1, source_target_pairs={{0,64},{32,96},{64,0},{96,32},{1,65},{33,97},{65,1},{97,33},{2,66}... | collective-permute-start | bytes 1179656 | tf_op jit(solution)/shard_map/ppermute | solution.py:38
  79.6 6.1 %collective-permute-start.18 = (bf16[64,1536]{1,0:T(8,128)(2,1)S(1)}, bf16[64,1536]{1,0:T(8,128)(2,1)S(1)}, u32[]{:S(2)}, u32[]{:S(2)}) collective-permute-start(bf16[64,1536]{1,0:T(8,128)(2,1)S(1)} %collective-permute-done.11.refs_2_.refs_3_), channel_id=1, source_target_pairs={{0,16},{16,0},{1,17},{17,1},{2,18},{18,2},{3,19},{19,3},{4,20},{20... | collective-permute-start | bytes 589832 | tf_op jit(solution)/shard_map/ppermute | solution.py:42
  81.7 6.1 %collective-permute-start.17 = (bf16[64,1536]{1,0:T(8,128)(2,1)S(1)}, bf16[64,1536]{1,0:T(8,128)(2,1)S(1)}, u32[]{:S(2)}, u32[]{:S(2)}) collective-permute-start(bf16[64,1536]{1,0:T(8,128)(2,1)S(1)} %collective-permute-done.14.refs_1_.refs_2_), channel_id=1, source_target_pairs={{0,16},{16,0},{1,17},{17,1},{2,18},{18,2},{3,19},{19,3},{4,20},{20... | collective-permute-start | bytes 589832 | tf_op jit(solution)/shard_map/ppermute | solution.py:42
  95.3 7.6 %collective-permute-start.20 = (bf16[8,32,1536]{2,1,0:T(8,128)(2,1)S(1)}, bf16[8,32,1536]{2,1,0:T(8,128)(2,1)S(1)}, u32[]{:S(2)}, u32[]{:S(2)}) collective-permute-start(bf16[8,32,1536]{2,1,0:T(8,128)(2,1)S(1)} %backward_other.1), channel_id=1, source_target_pairs={{0,1},{1,0},{2,3},{3,2},{4,5},{5,4},{6,7},{7,6},{8,9},{9,8},{10,11... | collective-permute-start | bytes 2359304 | tf_op jit(solution)/shard_map/ppermute | solution.py:46
  103.9 15.7 %all-to-all-start.1 = ((bf16[8,32,1536]{2,1,0:T(8,128)(2,1)}), bf16[8,32,1536]{2,1,0:T(8,128)(2,1)S(1)}, u32[]{:S(2)}, u32[]{:S(2)}) async-start(bf16[8,32,1536]{2,1,0:T(8,128)(2,1)} %chip_sum.1), calls=%async_computation.1 | async-start | bytes 1572864 | tf_op jit(solution)/shard_map/all_to_all | solution.py:483
  (16 other events, 157.1 us)

commit v8 on v7

--- a/solution.py
+++ b/solution.py
@@ -457,8 +457,8 @@
     late_b = after(grad_b, grad_a)
     by_y = [grad_b]
     by_y += [ahead(late_b if d == 1 else grad_b, -d) for d in (1, 2, 3)]
-    by_y_far = [across(grad) for grad in by_y]
     both = jnp.concatenate([grad_a, across(grad_a)], axis=0)
+    by_y_far = [across(after(grad, both) if d == 1 else grad) for d, grad in enumerate(by_y)]
     wide = [both] + [ahead(after(both, by_y[2]) if d == 2 else both, -d) for d in (1, 2, 3)]
     turned = turn(after(toks, both))
     activated = jnp.concatenate([act_a, act_b], axis=1)

time: 121 us -> 121 us (level)
    ppermute x2, starting transfers between devices: 7.59 us -> 5.3 us  [other_core(): return lax.ppermute(array, 'c', SWAP)]
  transfers between devices with their start and end apart: 22 -> 22, of which waited for: 11 -> 10; matrix products, arithmetic and copies ran while one was open for 0% -> 0% of each run, Pallas kernels for 20% -> 20%
where the time goes in v8:
time: 121 us; the launch traced here: 120 us
  starting transfers between devices  38.3 us (32%)
  Pallas kernels  31.5 us (26%)
  waiting for transfers between devices  30.5 us (25%)
  blocking collectives  18.1 us (15%)
    pallas_call x14, Pallas kernels, call(): pl.pallas_call(kernel, out_shape=[jax.ShapeDtypeStruct(shape, dtype) for...  31.5 us
    all_to_all x1, blocking collectives, local(): own = lax.all_to_all(spread, PLANE, 0, 0, tiled=True)  18.1 us
    ppermute x12, starting transfers between devices, ahead(): lax.ppermute(array, 'y', [(i, (i + distance) % N_Y) for i in range(N_Y)])  16.7 us
    ppermute x7, waiting for transfers between devices, across(): return lax.ppermute(array, 'xh', SWAP)  16.1 us
    ppermute x7, starting transfers between devices, across(): return lax.ppermute(array, 'xh', SWAP)  12.7 us
    ppermute x12, waiting for transfers between devices, ahead(): lax.ppermute(array, 'y', [(i, (i + distance) % N_Y) for i in range(N_Y)])  12.2 us
    ppermute x2, starting transfers between devices, other_core(): return lax.ppermute(array, 'c', SWAP)  5.3 us
    all_to_all x1, starting transfers between devices, local(): last = lax.all_to_all(chip, PLANE, 0, 0, tiled=True)  3.55 us
  transfers between devices with their start and end apart: 22, of which 10 were waited for; matrix products, arithmetic and copies ran while one was open for 0% of the time, Pallas kernels for 20%

profile of v8, /device:TPU:1, one launch (start us, length us, event | category | flops | bytes accessed | tf_op | source)
XLA Modules:
  0.0 120.4 jit_solution(5765105273537273869)
XLA Ops:
  1.6 18.1 %all_to_all.10.own = bf16[8,32,1536]{2,1,0:T(8,128)(2,1)S(1)} all-to-all(bf16[8,32,1536]{2,1,0:T(8,128)(2,1)S(1)} %broadcast_in_dim.2), channel_id=1, replica_groups=mesh['y'=4,'xh'=2,'xl'=2,'z'=4,'c'=2] {'xl','z'}, dimensions={0} | all-to-all | bytes 1572864 | tf_op jit(solution)/shard_map/all_to_all | solution.py:423
  19.7 2.4 %collective-permute-start = (bf16[8,32,1536]{2,1,0:T(8,128)(2,1)S(1)}, bf16[8,32,1536]{2,1,0:T(8,128)(2,1)S(1)}, u32[]{:S(2)}, u32[]{:S(2)}) collective-permute-start(bf16[8,32,1536]{2,1,0:T(8,128)(2,1)S(1)} %all_to_all.10.own), channel_id=1, source_target_pairs={{0,1},{1,0},{2,3},{3,2},{4,5},{5,4},{6,7},{7,6},{8,9},{9,8},{10,11... | collective-permute-start | bytes 2359304 | tf_op jit(solution)/shard_map/ppermute | solution.py:46
  22.1 2.5 %load_forward.1.weight = bf16[1536,1536]{1,0:T(8,128)(2,1)S(1)} custom-call(bf16[1536,3072]{1,0:T(8,128)(2,1)} %refs_4_.5), custom_call_target="tpu_custom_call" | custom-call | bytes 9437184 | tf_op jit(solution)/shard_map/load_forward/pallas_call | solution.py:62
  24.7 3.6 %forward_side.1 = (bf16[512,1536]{1,0:T(8,128)(2,1)S(1)}, bf16[256,1536]{1,0:T(8,128)(2,1)S(1)}, bf16[256,1536]{1,0:T(8,128)(2,1)S(1)}) custom-call(s32[3]{0:T(128)S(1)} %pad_add_fusion.place, bf16[8,32,1536]{2,1,0:T(8,128)(2,1)S(1)} %all_to_all.10.own, bf16[8,32,1536]{2,1,0:T(8,128)(2,1)S(1)} %collective-permute-done.other, ...), custom_call_target="tpu_custom_call" | custom-call | flops 2415919104 | bytes 4718592 | tf_op jit(solution)/shard_map/forward_side/pallas_call | solution.py:62
  28.3 2.5 %collective-permute-start.4 = (bf16[256,1536]{1,0:T(8,128)(2,1)S(1)}, bf16[256,1536]{1,0:T(8,128)(2,1)S(1)}, u32[]{:S(2)}, u32[]{:S(2)}) collective-permute-start(bf16[256,1536]{1,0:T(8,128)(2,1)S(1)} %get-tuple-element.65), channel_id=1, source_target_pairs={{0,16},{16,0},{1,17},{17,1},{2,18},{18,2},{3,19},{19,3},{4,20},{20... | collective-permute-start | bytes 2359304 | tf_op jit(solution)/shard_map/ppermute | solution.py:42
  30.8 3.0 %forward_distance.1 = (bf16[128,1536]{1,0:T(8,128)(2,1)S(1)}, bf16[128,1536]{1,0:T(8,128)(2,1)S(1)}, bf16[128,1536]{1,0:T(8,128)(2,1)S(1)}, bf16[128,1536]{1,0:T(8,128)(2,1)S(1)}) custom-call(bf16[512,1536]{1,0:T(8,128)(2,1)S(1)} %get-tuple-element.84.toks.tok, bf16[1536,3072]{1,0:T(8,128)(2,1)S(1)} %bitcast.4), custom_call_target="tpu_custom_call" | custom-call | flops 2415919104 | bytes 4718592 | tf_op jit(solution)/shard_map/forward_distance/pallas_call | solution.py:62
  35.2 2.6 %collective-permute-start.2 = (bf16[128,1536]{1,0:T(8,128)(2,1)S(1)}, bf16[128,1536]{1,0:T(8,128)(2,1)S(1)}, u32[]{:S(2)}, u32[]{:S(2)}) collective-permute-start(bf16[128,1536]{1,0:T(8,128)(2,1)S(1)} %get-tuple-element.62), channel_id=1, source_target_pairs={{0,64},{32,96},{64,0},{96,32},{1,65},{33,97},{65,1},{97,33},{2,66}... | collective-permute-start | bytes 1179656 | tf_op jit(solution)/shard_map/ppermute | solution.py:38
  38.9 10.1 %collective-permute-done.4.got = bf16[256,1536]{1,0:T(8,128)(2,1)S(1)} collective-permute-done((bf16[256,1536]{1,0:T(8,128)(2,1)S(1)}, bf16[256,1536]{1,0:T(8,128)(2,1)S(1)}, u32[]{:S(2)}, u32[]{:S(2)}) %collective-permute-start.4) | collective-permute-done | bytes 786464 | tf_op jit(solution)/shard_map/ppermute | solution.py:42
  49.2 3.0 %collective-permute-start.7 = (bf16[64,1536]{1,0:T(8,128)(2,1)S(1)}, bf16[64,1536]{1,0:T(8,128)(2,1)S(1)}, u32[]{:S(2)}, u32[]{:S(2)}) collective-permute-start(bf16[64,1536]{1,0:T(8,128)(2,1)S(1)} %get-tuple-element.74), channel_id=1, source_target_pairs={{0,64},{32,96},{64,0},{96,32},{1,65},{33,97},{65,1},{97,33},{2,66}... | collective-permute-start | bytes 589832 | tf_op jit(solution)/shard_map/ppermute | solution.py:38
  56.4 3.0 %collective-permute-done.7.refs_2_ = bf16[64,1536]{1,0:T(8,128)(2,1)S(1)} collective-permute-done((bf16[64,1536]{1,0:T(8,128)(2,1)S(1)}, bf16[64,1536]{1,0:T(8,128)(2,1)S(1)}, u32[]{:S(2)}, u32[]{:S(2)}) %collective-permute-start.7) | collective-permute-done | bytes 196640 | tf_op jit(solution)/shard_map/ppermute | solution.py:38
  59.5 3.6 %collective-permute-done.8.refs_3_ = bf16[64,1536]{1,0:T(8,128)(2,1)S(1)} collective-permute-done((bf16[64,1536]{1,0:T(8,128)(2,1)S(1)}, bf16[64,1536]{1,0:T(8,128)(2,1)S(1)}, u32[]{:S(2)}, u32[]{:S(2)}) %collective-permute-start.8) | collective-permute-done | bytes 196640 | tf_op jit(solution)/shard_map/ppermute | solution.py:38
  66.3 2.9 %collective-permute-start.11 = (bf16[64,1536]{1,0:T(8,128)(2,1)S(1)}, bf16[64,1536]{1,0:T(8,128)(2,1)S(1)}, u32[]{:S(2)}, u32[]{:S(2)}) collective-permute-start(bf16[64,1536]{1,0:T(8,128)(2,1)S(1)} %get-tuple-element.101.refs_0_.refs_1_), channel_id=1, source_target_pairs={{0,64},{32,96},{64,0},{96,32},{1,65},{33,97},{65,1},{97,33},{2,66}... | collective-permute-start | bytes 589832 | tf_op jit(solution)/shard_map/ppermute | solution.py:38
  72.8 2.2 %collective-permute-start.19 = (bf16[64,1536]{1,0:T(8,128)(2,1)S(1)}, bf16[64,1536]{1,0:T(8,128)(2,1)S(1)}, u32[]{:S(2)}, u32[]{:S(2)}) collective-permute-start(bf16[64,1536]{1,0:T(8,128)(2,1)S(1)} %collective-permute-done.15.refs_3_.refs_4_), channel_id=1, source_target_pairs={{0,16},{16,0},{1,17},{17,1},{2,18},{18,2},{3,19},{19,3},{4,20},{20... | collective-permute-start | bytes 589832 | tf_op jit(solution)/shard_map/ppermute | solution.py:42
  77.1 2.4 %collective-permute-start.10 = (bf16[128,1536]{1,0:T(8,128)(2,1)S(1)}, bf16[128,1536]{1,0:T(8,128)(2,1)S(1)}, u32[]{:S(2)}, u32[]{:S(2)}) collective-permute-start(bf16[128,1536]{1,0:T(8,128)(2,1)S(1)} %constant_dynamic-update-slice_fusion.2.refs_0_.refs_9_), channel_id=1, source_target_pairs={{0,96},{32,0},{64,32},{96,64},{1,97},{33,1},{65,33},{97,65},{2,98}... | collective-permute-start | bytes 1179656 | tf_op jit(solution)/shard_map/ppermute | solution.py:38
  79.5 2.9 %collective-permute-start.17 = (bf16[64,1536]{1,0:T(8,128)(2,1)S(1)}, bf16[64,1536]{1,0:T(8,128)(2,1)S(1)}, u32[]{:S(2)}, u32[]{:S(2)}) collective-permute-start(bf16[64,1536]{1,0:T(8,128)(2,1)S(1)} %collective-permute-done.14.refs_1_.refs_2_), channel_id=1, source_target_pairs={{0,16},{16,0},{1,17},{17,1},{2,18},{18,2},{3,19},{19,3},{4,20},{20... | collective-permute-start | bytes 589832 | tf_op jit(solution)/shard_map/ppermute | solution.py:42
  85.1 4.2 %collective-permute-done.18.refs_6_.refs_7_ = bf16[64,1536]{1,0:T(8,128)(2,1)S(1)} collective-permute-done((bf16[64,1536]{1,0:T(8,128)(2,1)S(1)}, bf16[64,1536]{1,0:T(8,128)(2,1)S(1)}, u32[]{:S(2)}, u32[]{:S(2)}) %collective-permute-start.18) | collective-permute-done | bytes 196640 | tf_op jit(solution)/shard_map/ppermute | solution.py:42
  89.3 3.1 %backward_first.1.refs_5_ = f32[512,1536]{1,0:T(8,128)S(1)} custom-call(bf16[64,1536]{1,0:T(8,128)(2,1)S(1)} %get-tuple-element.101.refs_0_.refs_1_, bf16[64,1536]{1,0:T(8,128)(2,1)S(1)} %collective-permute-done.14.refs_1_.refs_2_, bf16[64,1536]{1,0:T(8,128)(2,1)S(1)} %collective-permute-done.11.refs_2_.refs_3_, ...), custom_call_target="tpu_custom_call" | custom-call | flops 2415919104 | bytes 4718592 | tf_op jit(solution)/shard_map/backward_first/pallas_call | solution.py:62
  92.6 2.6 %collective-permute-done.12.refs_2_.refs_11_ = bf16[128,1536]{1,0:T(8,128)(2,1)S(1)} collective-permute-done((bf16[128,1536]{1,0:T(8,128)(2,1)S(1)}, bf16[128,1536]{1,0:T(8,128)(2,1)S(1)}, u32[]{:S(2)}, u32[]{:S(2)}) %collective-permute-start.12) | collective-permute-done | bytes 393248 | tf_op jit(solution)/shard_map/ppermute | solution.py:38
  95.2 2.4 %backward_other.1 = bf16[8,32,1536]{2,1,0:T(8,128)(2,1)S(1)} custom-call(s32[3]{0:T(128)S(1)} %pad_add_fusion.place, bf16[128,1536]{1,0:T(8,128)(2,1)S(1)} %constant_dynamic-update-slice_fusion.2.refs_0_.refs_9_, bf16[128,1536]{1,0:T(8,128)(2,1)S(1)} %collective-permute-done.10.refs_1_.refs_10_, ...), custom_call_target="tpu_custom_call" | custom-call | flops 1207959552 | bytes 4718592 | tf_op jit(solution)/shard_map/backward_other/pallas_call | solution.py:62
  97.6 2.9 %collective-permute-start.20 = (bf16[8,32,1536]{2,1,0:T(8,128)(2,1)S(1)}, bf16[8,32,1536]{2,1,0:T(8,128)(2,1)S(1)}, u32[]{:S(2)}, u32[]{:S(2)}) collective-permute-start(bf16[8,32,1536]{2,1,0:T(8,128)(2,1)S(1)} %backward_other.1), channel_id=1, source_target_pairs={{0,1},{1,0},{2,3},{3,2},{4,5},{5,4},{6,7},{7,6},{8,9},{9,8},{10,11... | collective-permute-start | bytes 2359304 | tf_op jit(solution)/shard_map/ppermute | solution.py:46
  100.6 2.4 %backward_own.1.mine = bf16[8,32,1536]{2,1,0:T(8,128)(2,1)S(1)} custom-call(s32[3]{0:T(128)S(1)} %pad_add_fusion.place, bf16[128,1536]{1,0:T(8,128)(2,1)S(1)} %constant_dynamic-update-slice_fusion.2.refs_0_.refs_9_, bf16[128,1536]{1,0:T(8,128)(2,1)S(1)} %collective-permute-done.10.refs_1_.refs_10_, ...), custom_call_target="tpu_custom_call" | custom-call | flops 1207959552 | bytes 4718592 | tf_op jit(solution)/shard_map/backward_own/pallas_call | solution.py:62
  104.0 3.5 %all-to-all-start.1 = ((bf16[8,32,1536]{2,1,0:T(8,128)(2,1)}), bf16[8,32,1536]{2,1,0:T(8,128)(2,1)S(1)}, u32[]{:S(2)}, u32[]{:S(2)}) async-start(bf16[8,32,1536]{2,1,0:T(8,128)(2,1)} %chip_sum.1), calls=%async_computation.1 | async-start | bytes 1572864 | tf_op jit(solution)/shard_map/all_to_all | solution.py:483
  107.5 10.0 %weight_grad.1 = bf16[1536,3072]{1,0:T(8,128)(2,1)} custom-call(bf16[1536,512]{1,0:T(8,128)(2,1)} %copy-done.1, bf16[64,1536]{1,0:T(8,128)(2,1)} %copy-done.6, bf16[64,1536]{1,0:T(8,128)(2,1)} %copy-done.10, bf16[64,1536]{1,0:T(8,128)(2,1)} %copy-done.9, bf16[64,1536]{1,0:T(8,128)(2,1)} %copy-done.8, bf16[64,1536]{1,0:T(8,128)(2,1)} %copy-done.7, ...), custom_call_target="tpu_custom_call" | custom-call | flops 4831838208 | bytes 9437184 | tf_op jit(solution)/shard_map/weight_grad/pallas_call | solution.py:62
  117.5 2.2 %all-to-all-done.1.got = bf16[8,32,1536]{2,1,0:T(8,128)(2,1)S(1)} async-done(((bf16[8,32,1536]{2,1,0:T(8,128)(2,1)}), bf16[8,32,1536]{2,1,0:T(8,128)(2,1)S(1)}, u32[]{:S(2)}, u32[]{:S(2)}) %all-to-all-start.1) | async-done | bytes 786464 | tf_op jit(solution)/shard_map/all_to_all | solution.py:483
  (78 shorter events, 21.0 us)
Async XLA Ops:
  19.7 5.0 %collective-permute-start = (bf16[8,32,1536]{2,1,0:T(8,128)(2,1)S(1)}, bf16[8,32,1536]{2,1,0:T(8,128)(2,1)S(1)}, u32[]{:S(2)}, u32[]{:S(2)}) collective-permute-start(bf16[8,32,1536]{2,1,0:T(8,128)(2,1)S(1)} %all_to_all.10.own), channel_id=1, source_target_pairs={{0,1},{1,0},{2,3},{3,2},{4,5},{5,4},{6,7},{7,6},{8,9},{9,8},{10,11... | collective-permute-start | bytes 2359304 | tf_op jit(solution)/shard_map/ppermute | solution.py:46
  28.3 20.8 %collective-permute-start.4 = (bf16[256,1536]{1,0:T(8,128)(2,1)S(1)}, bf16[256,1536]{1,0:T(8,128)(2,1)S(1)}, u32[]{:S(2)}, u32[]{:S(2)}) collective-permute-start(bf16[256,1536]{1,0:T(8,128)(2,1)S(1)} %get-tuple-element.65), channel_id=1, source_target_pairs={{0,16},{16,0},{1,17},{17,1},{2,18},{18,2},{3,19},{19,3},{4,20},{20... | collective-permute-start | bytes 2359304 | tf_op jit(solution)/shard_map/ppermute | solution.py:42
  30.8 33.4 %copy-start.2 = (bf16[64,3072]{1,0:T(8,128)(2,1)S(1)}, bf16[64,3072]{1,0:T(8,128)(2,1)}, u32[]{:S(2)}) copy-start(bf16[64,3072]{1,0:T(8,128)(2,1)} %refs_2_.1) | copy-start | bytes 1179652
  33.8 19.2 %collective-permute-start.1 = (bf16[128,1536]{1,0:T(8,128)(2,1)S(1)}, bf16[128,1536]{1,0:T(8,128)(2,1)S(1)}, u32[]{:S(2)}, u32[]{:S(2)}) collective-permute-start(bf16[128,1536]{1,0:T(8,128)(2,1)S(1)} %get-tuple-element.61), channel_id=1, source_target_pairs={{0,32},{32,64},{64,96},{96,0},{1,33},{33,65},{65,97},{97,1},{2,34}... | collective-permute-start | bytes 1179656 | tf_op jit(solution)/shard_map/ppermute | solution.py:38
  35.2 20.0 %collective-permute-start.2 = (bf16[128,1536]{1,0:T(8,128)(2,1)S(1)}, bf16[128,1536]{1,0:T(8,128)(2,1)S(1)}, u32[]{:S(2)}, u32[]{:S(2)}) collective-permute-start(bf16[128,1536]{1,0:T(8,128)(2,1)S(1)} %get-tuple-element.62), channel_id=1, source_target_pairs={{0,64},{32,96},{64,0},{96,32},{1,65},{33,97},{65,1},{97,33},{2,66}... | collective-permute-start | bytes 1179656 | tf_op jit(solution)/shard_map/ppermute | solution.py:38
  37.8 17.4 %collective-permute-start.3 = (bf16[128,1536]{1,0:T(8,128)(2,1)S(1)}, bf16[128,1536]{1,0:T(8,128)(2,1)S(1)}, u32[]{:S(2)}, u32[]{:S(2)}) collective-permute-start(bf16[128,1536]{1,0:T(8,128)(2,1)S(1)} %get-tuple-element.63), channel_id=1, source_target_pairs={{0,96},{32,0},{64,32},{96,64},{1,97},{33,1},{65,33},{97,65},{2,98}... | collective-permute-start | bytes 1179656 | tf_op jit(solution)/shard_map/ppermute | solution.py:38
  49.2 10.2 %collective-permute-start.7 = (bf16[64,1536]{1,0:T(8,128)(2,1)S(1)}, bf16[64,1536]{1,0:T(8,128)(2,1)S(1)}, u32[]{:S(2)}, u32[]{:S(2)}) collective-permute-start(bf16[64,1536]{1,0:T(8,128)(2,1)S(1)} %get-tuple-element.74), channel_id=1, source_target_pairs={{0,64},{32,96},{64,0},{96,32},{1,65},{33,97},{65,1},{97,33},{2,66}... | collective-permute-start | bytes 589832 | tf_op jit(solution)/shard_map/ppermute | solution.py:38
  52.2 10.8 %collective-permute-start.8 = (bf16[64,1536]{1,0:T(8,128)(2,1)S(1)}, bf16[64,1536]{1,0:T(8,128)(2,1)S(1)}, u32[]{:S(2)}, u32[]{:S(2)}) collective-permute-start(bf16[64,1536]{1,0:T(8,128)(2,1)S(1)} %get-tuple-element.75), channel_id=1, source_target_pairs={{0,96},{32,0},{64,32},{96,64},{1,97},{33,1},{65,33},{97,65},{2,98}... | collective-permute-start | bytes 589832 | tf_op jit(solution)/shard_map/ppermute | solution.py:38
  53.0 11.2 %collective-permute-start.6 = (bf16[64,1536]{1,0:T(8,128)(2,1)S(1)}, bf16[64,1536]{1,0:T(8,128)(2,1)S(1)}, u32[]{:S(2)}, u32[]{:S(2)}) collective-permute-start(bf16[64,1536]{1,0:T(8,128)(2,1)S(1)} %get-tuple-element.67), channel_id=1, source_target_pairs={{0,32},{32,64},{64,96},{96,0},{1,33},{33,65},{65,97},{97,1},{2,34}... | collective-permute-start | bytes 589832 | tf_op jit(solution)/shard_map/ppermute | solution.py:38
  55.4 13.8 %collective-permute-start.5 = (bf16[64,1536]{1,0:T(8,128)(2,1)S(1)}, bf16[64,1536]{1,0:T(8,128)(2,1)S(1)}, u32[]{:S(2)}, u32[]{:S(2)}) collective-permute-start(bf16[64,1536]{1,0:T(8,128)(2,1)S(1)} %get-tuple-element.72), channel_id=1, source_target_pairs={{0,16},{16,0},{1,17},{17,1},{2,18},{18,2},{3,19},{19,3},{4,20},{20... | collective-permute-start | bytes 589832 | tf_op jit(solution)/shard_map/ppermute | solution.py:42
  65.1 27.3 %copy-start.6 = (bf16[64,1536]{1,0:T(8,128)(2,1)}, bf16[64,1536]{1,0:T(8,128)(2,1)S(1)}, u32[]{:S(2)}) copy-start(bf16[64,1536]{1,0:T(8,128)(2,1)S(1)} %get-tuple-element.101.refs_0_.refs_1_) | copy-start | bytes 589828
  65.2 17.3 %collective-permute-start.16 = (bf16[64,1536]{1,0:T(8,128)(2,1)S(1)}, bf16[64,1536]{1,0:T(8,128)(2,1)S(1)}, u32[]{:S(2)}, u32[]{:S(2)}) collective-permute-start(bf16[64,1536]{1,0:T(8,128)(2,1)S(1)} %get-tuple-element.101.refs_0_.refs_1_), channel_id=1, source_target_pairs={{0,16},{16,0},{1,17},{17,1},{2,18},{18,2},{3,19},{19,3},{4,20},{20... | collective-permute-start | bytes 589832 | tf_op jit(solution)/shard_map/ppermute | solution.py:42
  65.2 7.6 %collective-permute-start.15 = (bf16[64,1536]{1,0:T(8,128)(2,1)S(1)}, bf16[64,1536]{1,0:T(8,128)(2,1)S(1)}, u32[]{:S(2)}, u32[]{:S(2)}) collective-permute-start(bf16[64,1536]{1,0:T(8,128)(2,1)S(1)} %get-tuple-element.101.refs_0_.refs_1_), channel_id=1, source_target_pairs={{0,32},{32,64},{64,96},{96,0},{1,33},{33,65},{65,97},{97,1},{2,34}... | collective-permute-start | bytes 589832 | tf_op jit(solution)/shard_map/ppermute | solution.py:38
  66.3 13.2 %collective-permute-start.11 = (bf16[64,1536]{1,0:T(8,128)(2,1)S(1)}, bf16[64,1536]{1,0:T(8,128)(2,1)S(1)}, u32[]{:S(2)}, u32[]{:S(2)}) collective-permute-start(bf16[64,1536]{1,0:T(8,128)(2,1)S(1)} %get-tuple-element.101.refs_0_.refs_1_), channel_id=1, source_target_pairs={{0,64},{32,96},{64,0},{96,32},{1,65},{33,97},{65,1},{97,33},{2,66}... | collective-permute-start | bytes 589832 | tf_op jit(solution)/shard_map/ppermute | solution.py:38
  70.1 6.6 %collective-permute-start.9 = (bf16[64,1536]{1,0:T(8,128)(2,1)S(1)}, bf16[64,1536]{1,0:T(8,128)(2,1)S(1)}, u32[]{:S(2)}, u32[]{:S(2)}) collective-permute-start(bf16[64,1536]{1,0:T(8,128)(2,1)S(1)} %get-tuple-element.80), channel_id=1, source_target_pairs={{0,16},{16,0},{1,17},{17,1},{2,18},{18,2},{3,19},{19,3},{4,20},{20... | collective-permute-start | bytes 589832 | tf_op jit(solution)/shard_map/ppermute | solution.py:42
  72.2 4.9 %collective-permute-start.14 = (bf16[64,1536]{1,0:T(8,128)(2,1)S(1)}, bf16[64,1536]{1,0:T(8,128)(2,1)S(1)}, u32[]{:S(2)}, u32[]{:S(2)}) collective-permute-start(bf16[64,1536]{1,0:T(8,128)(2,1)S(1)} %get-tuple-element.101.refs_0_.refs_1_), channel_id=1, source_target_pairs={{0,96},{32,0},{64,32},{96,64},{1,97},{33,1},{65,33},{97,65},{2,98}... | collective-permute-start | bytes 589832 | tf_op jit(solution)/shard_map/ppermute | solution.py:38
  72.8 9.8 %collective-permute-start.19 = (bf16[64,1536]{1,0:T(8,128)(2,1)S(1)}, bf16[64,1536]{1,0:T(8,128)(2,1)S(1)}, u32[]{:S(2)}, u32[]{:S(2)}) collective-permute-start(bf16[64,1536]{1,0:T(8,128)(2,1)S(1)} %collective-permute-done.15.refs_3_.refs_4_), channel_id=1, source_target_pairs={{0,16},{16,0},{1,17},{17,1},{2,18},{18,2},{3,19},{19,3},{4,20},{20... | collective-permute-start | bytes 589832 | tf_op jit(solution)/shard_map/ppermute | solution.py:42
  76.8 18.4 %collective-permute-start.13 = (bf16[128,1536]{1,0:T(8,128)(2,1)S(1)}, bf16[128,1536]{1,0:T(8,128)(2,1)S(1)}, u32[]{:S(2)}, u32[]{:S(2)}) collective-permute-start(bf16[128,1536]{1,0:T(8,128)(2,1)S(1)} %constant_dynamic-update-slice_fusion.2.refs_0_.refs_9_), channel_id=1, source_target_pairs={{0,32},{32,64},{64,96},{96,0},{1,33},{33,65},{65,97},{97,1},{2,34}... | collective-permute-start | bytes 1179656 | tf_op jit(solution)/shard_map/ppermute | solution.py:38
  77.1 18.1 %collective-permute-start.10 = (bf16[128,1536]{1,0:T(8,128)(2,1)S(1)}, bf16[128,1536]{1,0:T(8,128)(2,1)S(1)}, u32[]{:S(2)}, u32[]{:S(2)}) collective-permute-start(bf16[128,1536]{1,0:T(8,128)(2,1)S(1)} %constant_dynamic-update-slice_fusion.2.refs_0_.refs_9_), channel_id=1, source_target_pairs={{0,96},{32,0},{64,32},{96,64},{1,97},{33,1},{65,33},{97,65},{2,98}... | collective-permute-start | bytes 1179656 | tf_op jit(solution)/shard_map/ppermute | solution.py:38
  79.5 9.8 %collective-permute-start.17 = (bf16[64,1536]{1,0:T(8,128)(2,1)S(1)}, bf16[64,1536]{1,0:T(8,128)(2,1)S(1)}, u32[]{:S(2)}, u32[]{:S(2)}) collective-permute-start(bf16[64,1536]{1,0:T(8,128)(2,1)S(1)} %collective-permute-done.14.refs_1_.refs_2_), channel_id=1, source_target_pairs={{0,16},{16,0},{1,17},{17,1},{2,18},{18,2},{3,19},{19,3},{4,20},{20... | collective-permute-start | bytes 589832 | tf_op jit(solution)/shard_map/ppermute | solution.py:42
  82.5 12.7 %collective-permute-start.12 = (bf16[128,1536]{1,0:T(8,128)(2,1)S(1)}, bf16[128,1536]{1,0:T(8,128)(2,1)S(1)}, u32[]{:S(2)}, u32[]{:S(2)}) collective-permute-start(bf16[128,1536]{1,0:T(8,128)(2,1)S(1)} %constant_dynamic-update-slice_fusion.2.refs_0_.refs_9_), channel_id=1, source_target_pairs={{0,64},{32,96},{64,0},{96,32},{1,65},{33,97},{65,1},{97,33},{2,66}... | collective-permute-start | bytes 1179656 | tf_op jit(solution)/shard_map/ppermute | solution.py:38
  82.6 6.7 %collective-permute-start.18 = (bf16[64,1536]{1,0:T(8,128)(2,1)S(1)}, bf16[64,1536]{1,0:T(8,128)(2,1)S(1)}, u32[]{:S(2)}, u32[]{:S(2)}) collective-permute-start(bf16[64,1536]{1,0:T(8,128)(2,1)S(1)} %collective-permute-done.11.refs_2_.refs_3_), channel_id=1, source_target_pairs={{0,16},{16,0},{1,17},{17,1},{2,18},{18,2},{3,19},{19,3},{4,20},{20... | collective-permute-start | bytes 589832 | tf_op jit(solution)/shard_map/ppermute | solution.py:42
  97.6 5.3 %collective-permute-start.20 = (bf16[8,32,1536]{2,1,0:T(8,128)(2,1)S(1)}, bf16[8,32,1536]{2,1,0:T(8,128)(2,1)S(1)}, u32[]{:S(2)}, u32[]{:S(2)}) collective-permute-start(bf16[8,32,1536]{2,1,0:T(8,128)(2,1)S(1)} %backward_other.1), channel_id=1, source_target_pairs={{0,1},{1,0},{2,3},{3,2},{4,5},{5,4},{6,7},{7,6},{8,9},{9,8},{10,11... | collective-permute-start | bytes 2359304 | tf_op jit(solution)/shard_map/ppermute | solution.py:46
  104.0 15.7 %all-to-all-start.1 = ((bf16[8,32,1536]{2,1,0:T(8,128)(2,1)}), bf16[8,32,1536]{2,1,0:T(8,128)(2,1)S(1)}, u32[]{:S(2)}, u32[]{:S(2)}) async-start(bf16[8,32,1536]{2,1,0:T(8,128)(2,1)} %chip_sum.1), calls=%async_computation.1 | async-start | bytes 1572864 | tf_op jit(solution)/shard_map/all_to_all | solution.py:483
  (16 other events, 153.3 us)
